TPU v7x, 32 devices: a whole 2x2x4 slice. The times are simulated.
32 devices in a mesh: rep: 2 (over x), tp: 4 (over y, core), dp: 4 (over z).
Axes of the slice: x: 2, y: 2, z: 4, core: 2. Of those that a mesh axis runs over, the one named last changes fastest.
Arguments:
- patches: bfloat16 [2048, 3072], P(('rep', 'dp'), 'tp'), parts along dimension 0, may hold values from -6 to 6
- ordering: int32 [2048], P(('rep', 'dp')), parts along dimension 0, may hold values from 0 to 255, as said below
- w_in: bfloat16 [3072, 12288], P(None, 'tp'), may hold values from -0.109375 to 0.109375
- w_out: bfloat16 [12288, 3072], P('tp'), may hold values from -0.0546875 to 0.0546875
- cotangent: bfloat16 [2048, 3072], P(('rep', 'dp'), 'tp'), parts along dimension 0, may hold values from -1.5 to 1.5
Outputs:
- mixed: bfloat16 [2048, 3072], P(('rep', 'dp'), 'tp'), parts along dimension 0
- grad_patches: bfloat16 [2048, 3072], P(('rep', 'dp'), 'tp'), parts along dimension 0
- grad_in: float32 [6144, 12288], P(('rep', 'dp'), 'tp'), parts along dimension 0
- grad_out: float32 [24576, 3072], P(('rep', 'tp'), 'dp'), parts along dimension 0
There are 2 independent parts, one for each index of `rep`. A program takes and returns all parts, laid end to end along the dimension named above; an argument that names none is the same for every part. Nothing has to cross between parts.
Inputs may be any that keep to these rules, and one draw needn't show every extreme that they name: `ordering`: each block of 256 consecutive entries (one group) lists every number from 0 to 255 once; entry k of a block names the patch of sorted row k, whose level is k // 64.
All inputs are finite; a program needn't handle non-finite values.
Results may differ from a plain program's by a relative error of at most 0.0095.
Values may be sent and summed in bfloat16 or wider, within the bound.
No kernel may reach another device: no remote copies, remote signals or barrier semaphores. Data moves between devices by JAX's collectives and lax.ppermute only.
A program may use at most 256 MiB of HBM per device.

v0:
```python
import jax
import jax.numpy as jnp
from jax import lax
from jax.sharding import PartitionSpec as P


def gelu_slope(pre_act):
    return jax.jvp(jax.nn.gelu, (pre_act,), (jnp.ones_like(pre_act),))[1]


def contract_cols(left_side, right_side):
    return lax.dot_general(
        left_side, right_side, (((1,), (1,)), ((), ())), preferred_element_type=jnp.float32
    )


def contract_rows(left_side, right_side):
    return lax.dot_general(
        left_side, right_side, (((0,), (0,)), ((), ())), preferred_element_type=jnp.float32
    )


def bucket_pass(rows_part, cot_part, w_first, w_second, unit_ids, prefix_end):
    keep_mask = (unit_ids < prefix_end).astype(jnp.float32)[None, :]
    pre_act = jnp.dot(rows_part, w_first, preferred_element_type=jnp.float32)
    hidden = (jax.nn.gelu(pre_act) * keep_mask).astype(jnp.bfloat16)
    partial_out = jnp.dot(hidden, w_second, preferred_element_type=jnp.float32)
    back_hidden = contract_cols(cot_part, w_second)
    back_pre = (back_hidden * gelu_slope(pre_act) * keep_mask).astype(jnp.bfloat16)
    partial_in = contract_cols(back_pre, w_first)
    return (partial_out, partial_in, hidden, back_pre)


def shards(patches, ordering, w_in, w_out, cotangent):
    tp_count = lax.axis_size("tp")
    tp_rank = lax.axis_index("tp")
    group_rows = patches.shape[0]
    level_rows = group_rows // 4
    width = w_in.shape[0]
    shard_cols = w_in.shape[1]
    total_units = shard_cols * tp_count
    rows_all, cot_all = (
        lax.all_gather(patches, "tp", axis=1, tiled=True),
        lax.all_gather(cotangent, "tp", axis=1, tiled=True),
    )
    rows_sorted = jnp.take(rows_all, ordering, axis=0)
    cot_sorted = jnp.take(cot_all, ordering, axis=0)
    col_ids = jnp.arange(shard_cols, dtype=jnp.int32)
    out_blocks = []
    back_blocks = []
    hidden_blocks = []
    pre_blocks = []
    unit_ids = tp_rank * shard_cols + col_ids
    for level_idx in range(4):
        prefix_end = total_units >> level_idx
        first_row = level_idx * level_rows

        def active_pass(operands):
            return bucket_pass(operands[0], operands[1], w_in, w_out, unit_ids, prefix_end)

        def skipped_pass(operands):
            zero_rows = jnp.zeros((level_rows, width), jnp.float32)
            zero_cols = jnp.zeros((level_rows, shard_cols), jnp.bfloat16)
            return (zero_rows, zero_rows, zero_cols, zero_cols)

        results = lax.cond(
            tp_rank * shard_cols < prefix_end,
            active_pass,
            skipped_pass,
            (
                rows_sorted[first_row : first_row + level_rows],
                cot_sorted[first_row : first_row + level_rows],
            ),
        )
        out_blocks.append(results[0])
        back_blocks.append(results[1])
        hidden_blocks.append(results[2])
        pre_blocks.append(results[3])
    hidden_all = jnp.concatenate(hidden_blocks, axis=0)
    back_all = jnp.concatenate(pre_blocks, axis=0)
    sum_out = lax.psum_scatter(
        jnp.concatenate(out_blocks, axis=0).astype(jnp.bfloat16),
        "tp",
        scatter_dimension=1,
        tiled=True,
    ).astype(jnp.float32)
    sum_in = lax.psum_scatter(
        jnp.concatenate(back_blocks, axis=0).astype(jnp.bfloat16),
        "tp",
        scatter_dimension=1,
        tiled=True,
    ).astype(jnp.float32)
    inverse = (
        jnp.zeros((group_rows,), jnp.int32)
        .at[ordering]
        .set(jnp.arange(group_rows, dtype=jnp.int32))
    )
    mixed = jnp.take(sum_out, inverse, axis=0).astype(jnp.bfloat16)
    grad_patches = jnp.take(sum_in, inverse, axis=0).astype(jnp.bfloat16)
    term_in = contract_rows(rows_sorted, back_all)
    term_out = contract_rows(hidden_all, cot_sorted)
    grad_in, grad_out = (
        lax.psum_scatter(
            term_in.astype(jnp.bfloat16), "dp", scatter_dimension=0, tiled=True
        ).astype(jnp.float32),
        lax.psum_scatter(
            term_out.astype(jnp.bfloat16), "dp", scatter_dimension=1, tiled=True
        ).astype(jnp.float32),
    )
    return (mixed, grad_patches, grad_in, grad_out)


def solution(mesh):
    return jax.shard_map(
        shards,
        mesh=mesh,
        in_specs=(
            P(("rep", "dp"), "tp"),
            P(("rep", "dp")),
            P(None, "tp"),
            P("tp", None),
            P(("rep", "dp"), "tp"),
        ),
        out_specs=(
            P(("rep", "dp"), "tp"),
            P(("rep", "dp"), "tp"),
            P(("rep", "dp"), "tp"),
            P(("rep", "tp"), "dp"),
        ),
        check_vma=False,
    )
```

profile of v0, /device:TPU:0, one launch (start us, length us, event | category | flops | bytes accessed | tf_op | source)
XLA Modules:
  0.0 962.7 jit_solution(13934949358668106684)
XLA Ops:
  10.1 21.9 %all-gather.5.cloned.1.call-done = bf16[256,3072]{1,0:T(8,128)(2,1)} async-done(((bf16[256,768]{1,0:T(8,128)(2,1)}), bf16[256,3072]{1,0:T(8,128)(2,1)}) %all-gather.5.cloned.1.call-update) | async-done | bytes 1572880 | tf_op jit(solution)/shard_map/all_gather | solution.py:44
  37.9 15.3 %all-gather.3.cloned.1.call-done = bf16[256,3072]{1,0:T(8,128)(2,1)} async-done(((bf16[256,768]{1,0:T(8,128)(2,1)}), bf16[256,3072]{1,0:T(8,128)(2,1)}) %all-gather.3.cloned.1.call-update) | async-done | bytes 1572880 | tf_op jit(solution)/shard_map/all_gather | solution.py:43
  61.3 47.6 %conditional.7 = (bf16[64,3072]{1,0:T(8,128)(2,1)}, bf16[64,3072]{1,0:T(8,128)(2,1)}, bf16[64,3072]{1,0:T(8,128)(2,1)}, bf16[64,3072]{1,0:T(8,128)(2,1)S(1)}) conditional(s32[]{:T(128)} %convert_element_type.77, () %tuple.46, (bf16[256,3072]{1,0:T(8,128)(2,1)S(1)}, bf16[3072,3072]{1,0:T(8,128)(2,1)}, s32[3072]{0:T(1024)S(1)}, ...), branch_computations={%region_6.8_spmd, %region_7.9_spmd} | conditional | flops 4837939200 | bytes 80265248 | solution.py:66
  61.6 10.8 %multiply_convert_fusion.3 = (bf16[64,3072]{1,0:T(8,128)(2,1)}, f32[64,3072]{1,0:T(8,128)}) fusion(f32[3072]{0:T(1024)S(1)} %compare_convert_fusion.3, bf16[3072,3072]{1,0:T(8,128)(2,1)} %get-tuple-element.66, bf16[256,3072]{1,0:T(8,128)(2,1)S(1)} %get-tuple-element.65), kind=kOutput, calls=%fused_computation.88 | convolution fusion | flops 1209925632 | bytes 20459520 | tf_op jit(solution)/shard_map/cond/branch_1_fun/dot_general | solution.py:25
  72.4 13.1 %fusion.46 = bf16[64,3072]{1,0:T(8,128)(2,1)} fusion(bf16[3072,3072]{1,0:T(8,128)(2,1)} %get-tuple-element.68, f32[64,3072]{1,0:T(8,128)} %get-tuple-element.121, bf16[256,3072]{1,0:T(8,128)(2,1)S(1)} %get-tuple-element.69, f32[3072]{0:T(1024)S(1)} %compare_convert_fusion.3), kind=kOutput, calls=%fused_computation.73 | convolution fusion | flops 1211695104 | bytes 20459520 | tf_op jit(solution)/shard_map/cond/branch_1_fun/dot_general | solution.py:12
  85.5 12.3 %convolution_convert_fusion.6 = bf16[64,3072]{1,0:T(8,128)(2,1)S(1)} fusion(bf16[64,3072]{1,0:T(8,128)(2,1)} %fusion.46, bf16[3072,3072]{1,0:T(8,128)(2,1)} %get-tuple-element.66), kind=kOutput, calls=%fused_computation.74 | convolution fusion | flops 1208156160 | bytes 19660800 | tf_op jit(solution)/shard_map/cond/branch_1_fun/dot_general | solution.py:12
  97.9 10.7 %convolution_convert_fusion.7 = bf16[64,3072]{1,0:T(8,128)(2,1)} fusion(bf16[64,3072]{1,0:T(8,128)(2,1)} %get-tuple-element.130, bf16[3072,3072]{1,0:T(8,128)(2,1)} %get-tuple-element.68), kind=kOutput, calls=%fused_computation.75 | convolution fusion | flops 1208156160 | bytes 19660800 | tf_op jit(solution)/shard_map/cond/branch_1_fun/dot_general | solution.py:27
  108.9 48.1 %conditional.6 = (bf16[64,3072]{1,0:T(8,128)(2,1)}, bf16[64,3072]{1,0:T(8,128)(2,1)}, bf16[64,3072]{1,0:T(8,128)(2,1)}, bf16[64,3072]{1,0:T(8,128)(2,1)}) conditional(s32[]{:T(128)} %convert_element_type.76, () %tuple.45, (bf16[256,3072]{1,0:T(8,128)(2,1)S(1)}, bf16[3072,3072]{1,0:T(8,128)(2,1)}, s32[3072]{0:T(1024)S(1)}, ...), branch_computations={%region_4.6_spmd, %region_5.7_spmd} | conditional | flops 4837939200 | bytes 80314432 | solution.py:66
  109.0 10.8 %multiply_convert_fusion.2 = (bf16[64,3072]{1,0:T(8,128)(2,1)}, f32[64,3072]{1,0:T(8,128)}) fusion(f32[3072]{0:T(1024)S(1)} %compare_convert_fusion.2, bf16[3072,3072]{1,0:T(8,128)(2,1)} %get-tuple-element.61, bf16[256,3072]{1,0:T(8,128)(2,1)S(1)} %get-tuple-element.60), kind=kOutput, calls=%fused_computation.66 | convolution fusion | flops 1209925632 | bytes 20459520 | tf_op jit(solution)/shard_map/cond/branch_1_fun/dot_general | solution.py:25
  119.8 13.3 %fusion.31 = bf16[64,3072]{1,0:T(8,128)(2,1)} fusion(bf16[3072,3072]{1,0:T(8,128)(2,1)} %get-tuple-element.63, f32[64,3072]{1,0:T(8,128)} %get-tuple-element.119, bf16[256,3072]{1,0:T(8,128)(2,1)S(1)} %get-tuple-element.64, f32[3072]{0:T(1024)} %copy-done), kind=kOutput, calls=%fused_computation.51 | convolution fusion | flops 1211695104 | bytes 20459520 | tf_op jit(solution)/shard_map/cond/branch_1_fun/dot_general | solution.py:12
  133.1 13.1 %convolution_convert_fusion.4 = bf16[64,3072]{1,0:T(8,128)(2,1)} fusion(bf16[64,3072]{1,0:T(8,128)(2,1)} %fusion.31, bf16[3072,3072]{1,0:T(8,128)(2,1)} %get-tuple-element.61), kind=kOutput, calls=%fused_computation.52 | convolution fusion | flops 1208156160 | bytes 19660800 | tf_op jit(solution)/shard_map/cond/branch_1_fun/dot_general | solution.py:12
  157.0 48.3 %conditional.5 = (bf16[64,3072]{1,0:T(8,128)(2,1)}, bf16[64,3072]{1,0:T(8,128)(2,1)}, bf16[64,3072]{1,0:T(8,128)(2,1)}, bf16[64,3072]{1,0:T(8,128)(2,1)}) conditional(s32[]{:T(128)} %convert_element_type.75, () %tuple.44, (bf16[256,3072]{1,0:T(8,128)(2,1)S(1)}, bf16[3072,3072]{1,0:T(8,128)(2,1)}, s32[3072]{0:T(1024)S(1)}, ...), branch_computations={%region_2.4_spmd, %region_3.5_spmd} | conditional | flops 4837939200 | bytes 80314432 | solution.py:66
  157.0 10.9 %multiply_convert_fusion.1 = (bf16[64,3072]{1,0:T(8,128)(2,1)}, f32[64,3072]{1,0:T(8,128)}) fusion(f32[3072]{0:T(1024)S(1)} %compare_convert_fusion.1, bf16[3072,3072]{1,0:T(8,128)(2,1)} %get-tuple-element.56, bf16[256,3072]{1,0:T(8,128)(2,1)S(1)} %get-tuple-element.55), kind=kOutput, calls=%fused_computation.44 | convolution fusion | flops 1209925632 | bytes 20459520 | tf_op jit(solution)/shard_map/cond/branch_1_fun/dot_general | solution.py:25
  167.9 13.3 %fusion.16 = bf16[64,3072]{1,0:T(8,128)(2,1)} fusion(bf16[3072,3072]{1,0:T(8,128)(2,1)} %get-tuple-element.58, f32[64,3072]{1,0:T(8,128)} %get-tuple-element.117, bf16[256,3072]{1,0:T(8,128)(2,1)S(1)} %get-tuple-element.59, f32[3072]{0:T(1024)} %copy-done.1), kind=kOutput, calls=%fused_computation.29 | convolution fusion | flops 1211695104 | bytes 20459520 | tf_op jit(solution)/shard_map/cond/branch_1_fun/dot_general | solution.py:12
  181.1 13.1 %convolution_convert_fusion.2 = bf16[64,3072]{1,0:T(8,128)(2,1)} fusion(bf16[64,3072]{1,0:T(8,128)(2,1)} %fusion.16, bf16[3072,3072]{1,0:T(8,128)(2,1)} %get-tuple-element.56), kind=kOutput, calls=%fused_computation.30 | convolution fusion | flops 1208156160 | bytes 19660800 | tf_op jit(solution)/shard_map/cond/branch_1_fun/dot_general | solution.py:12
  194.2 10.7 %convolution_convert_fusion.3 = bf16[64,3072]{1,0:T(8,128)(2,1)} fusion(bf16[64,3072]{1,0:T(8,128)(2,1)} %get-tuple-element.146, bf16[3072,3072]{1,0:T(8,128)(2,1)} %get-tuple-element.58), kind=kOutput, calls=%fused_computation.31 | convolution fusion | flops 1208156160 | bytes 19660800 | tf_op jit(solution)/shard_map/cond/branch_1_fun/dot_general | solution.py:27
  205.3 48.1 %conditional.4 = (bf16[64,3072]{1,0:T(8,128)(2,1)}, bf16[64,3072]{1,0:T(8,128)(2,1)}, bf16[64,3072]{1,0:T(8,128)(2,1)}, bf16[64,3072]{1,0:T(8,128)(2,1)}) conditional(s32[]{:T(128)} %convert_element_type.74, () %tuple.42, (bf16[256,3072]{1,0:T(8,128)(2,1)S(1)}, bf16[3072,3072]{1,0:T(8,128)(2,1)}, s32[3072]{0:T(1024)S(1)}, ...), branch_computations={%region_0.0_spmd, %region_1.3_spmd} | conditional | flops 4837939200 | bytes 80314432 | solution.py:66
  205.3 10.9 %multiply_convert_fusion = (bf16[64,3072]{1,0:T(8,128)(2,1)}, f32[64,3072]{1,0:T(8,128)}) fusion(f32[3072]{0:T(1024)S(1)} %compare_convert_fusion, bf16[3072,3072]{1,0:T(8,128)(2,1)} %get-tuple-element.51, bf16[256,3072]{1,0:T(8,128)(2,1)S(1)} %get-tuple-element.50), kind=kOutput, calls=%fused_computation.22 | convolution fusion | flops 1209925632 | bytes 20459520 | tf_op jit(solution)/shard_map/cond/branch_1_fun/dot_general | solution.py:25
  216.2 13.3 %fusion.1 = bf16[64,3072]{1,0:T(8,128)(2,1)} fusion(bf16[3072,3072]{1,0:T(8,128)(2,1)} %get-tuple-element.53, f32[64,3072]{1,0:T(8,128)} %get-tuple-element.115, bf16[256,3072]{1,0:T(8,128)(2,1)S(1)} %get-tuple-element.54, f32[3072]{0:T(1024)} %copy-done.2), kind=kOutput, calls=%fused_computation.7 | convolution fusion | flops 1211695104 | bytes 20459520 | tf_op jit(solution)/shard_map/cond/branch_1_fun/dot_general | solution.py:12
  229.5 13.1 %convolution_convert_fusion = bf16[64,3072]{1,0:T(8,128)(2,1)} fusion(bf16[64,3072]{1,0:T(8,128)(2,1)} %fusion.1, bf16[3072,3072]{1,0:T(8,128)(2,1)} %get-tuple-element.51), kind=kOutput, calls=%fused_computation.8 | convolution fusion | flops 1208156160 | bytes 19660800 | tf_op jit(solution)/shard_map/cond/branch_1_fun/dot_general | solution.py:12
  242.5 10.8 %convolution_convert_fusion.1 = bf16[64,3072]{1,0:T(8,128)(2,1)} fusion(bf16[64,3072]{1,0:T(8,128)(2,1)} %get-tuple-element.154, bf16[3072,3072]{1,0:T(8,128)(2,1)} %get-tuple-element.53), kind=kOutput, calls=%fused_computation.9 | convolution fusion | flops 1208156160 | bytes 19660800 | tf_op jit(solution)/shard_map/cond/branch_1_fun/dot_general | solution.py:27
  286.7 28.9 %reduce-scatter.7.cloned.1.call-done = bf16[256,768]{1,0:T(8,128)(2,1)} async-done(((bf16[256,3072]{1,0:T(8,128)(2,1)}), bf16[256,768]{1,0:T(8,128)(2,1)}) %reduce-scatter.7.cloned.1.call-update) | async-done | bytes 393232 | tf_op jit(solution)/shard_map/reduce_scatter | solution.py:87
  319.2 312.5 %reduce-scatter.9.cloned.1.call-done = bf16[768,3072]{1,0:T(8,128)(2,1)} async-done(((bf16[3072,3072]{1,0:T(8,128)(2,1)}), bf16[768,3072]{1,0:T(8,128)(2,1)}) %reduce-scatter.9.cloned.1.call-update) | async-done | bytes 4718608 | tf_op jit(solution)/shard_map/reduce_scatter | solution.py:103
  639.0 309.9 %reduce-scatter.11.cloned.1.call-done = bf16[3072,768]{1,0:T(8,128)(2,1)} async-done(((bf16[3072,3072]{1,0:T(8,128)(2,1)}), bf16[3072,768]{1,0:T(8,128)(2,1)}) %reduce-scatter.11.cloned.1.call-update) | async-done | bytes 4718608 | tf_op jit(solution)/shard_map/reduce_scatter | solution.py:106
  (45 shorter events, 78.6 us)
Async XLA Ops:
  7.2 24.8 %all-gather.5.cloned.1.call-start = ((), (), s32[]{:S(2)}) async-start(), calls=%async_computation.5 | async-start | bytes 1966080 | tf_op jit(solution)/shard_map/all_gather | solution.py:44
  7.9 45.3 %all-gather.3.cloned.1.call-start = ((), (), s32[]{:S(2)}) async-start(), calls=%async_computation.4 | async-start | bytes 1966080 | tf_op jit(solution)/shard_map/all_gather | solution.py:43
  8.6 275.6 %reduce-scatter.5.cloned.1.call-start = ((), (), s32[]{:S(2)}) async-start(), calls=%async_computation.6 | async-start | bytes 1966080 | tf_op jit(solution)/shard_map/reduce_scatter | solution.py:81
  108.9 10.9 %copy-start = (f32[3072]{0:T(1024)}, f32[3072]{0:T(1024)S(1)}, u32[]{:S(2)}) copy-start(f32[3072]{0:T(1024)S(1)} %compare_convert_fusion.2) | copy-start | bytes 36868 | tf_op jit(solution)/shard_map/cond
  157.0 10.9 %copy-start.1 = (f32[3072]{0:T(1024)}, f32[3072]{0:T(1024)S(1)}, u32[]{:S(2)}) copy-start(f32[3072]{0:T(1024)S(1)} %compare_convert_fusion.1) | copy-start | bytes 36868 | tf_op jit(solution)/shard_map/cond
  205.3 10.9 %copy-start.2 = (f32[3072]{0:T(1024)}, f32[3072]{0:T(1024)S(1)}, u32[]{:S(2)}) copy-start(f32[3072]{0:T(1024)S(1)} %compare_convert_fusion) | copy-start | bytes 36868 | tf_op jit(solution)/shard_map/cond
  256.0 59.7 %reduce-scatter.7.cloned.1.call-start = ((), (), s32[]{:S(2)}) async-start(), calls=%async_computation.7 | async-start | bytes 1966080 | tf_op jit(solution)/shard_map/reduce_scatter | solution.py:87
  258.5 373.1 %reduce-scatter.9.cloned.1.call-start = ((), (), s32[]{:S(2)}) async-start(), calls=%async_computation.8 | async-start | bytes 23592960 | tf_op jit(solution)/shard_map/reduce_scatter | solution.py:103
  269.1 679.8 %reduce-scatter.11.cloned.1.call-start = ((), (), s32[]{:S(2)}) async-start(), calls=%async_computation.9 | async-start | bytes 23592960 | tf_op jit(solution)/shard_map/reduce_scatter | solution.py:106
Sparse Core Ops, SparseCore 0:
  9.6 22.3 all-gather.4
  33.5 19.6 all-gather.2
  256.1 28.1 reduce-scatter.4
  287.4 28.1 reduce-scatter.6
  317.8 313.7 reduce-scatter.8
  634.0 314.8 reduce-scatter.10
where the time goes:
time: 969 us; the launch traced here: 963 us
  waiting for transfers between devices  693 us (72%)
  matrix products  212 us (22%)
  other arithmetic  24 us (2%)
  local copies, waits for them, and re-layouts  18.1 us (2%)
  between operations  14.4 us (1%)
    reduce_scatter x1, waiting for transfers between devices, shards(): lax.psum_scatter(term_in.astype(jnp.bfloat16), 'dp', scatter_dimension=0,...  313 us
    reduce_scatter x1, waiting for transfers between devices, shards(): lax.psum_scatter(term_out.astype(jnp.bfloat16), 'dp', scatter_dimension=1...  310 us
    dot_general x8, matrix products, contract_cols(): lax.dot_general(left_side, right_side, (((1,), (1,)), ((), ())), preferre...  105 us
    dot_general x4, matrix products, bucket_pass(): pre_act = jnp.dot(rows_part, w_first, preferred_element_type=jnp.float32)  43.4 us
    dot_general x4, matrix products, bucket_pass(): partial_out = jnp.dot(hidden, w_second, preferred_element_type=jnp.float32)  42.8 us
    reduce_scatter x1, waiting for transfers between devices, shards(): lax.psum_scatter(jnp.concatenate(back_blocks, axis=0).astype(jnp.bfloat16...  28.9 us
    all_gather x1, waiting for transfers between devices, shards(): lax.all_gather(cotangent, 'tp', axis=1, tiled=True)  21.9 us
    dot_general x2, matrix products, contract_rows(): lax.dot_general(left_side, right_side, (((0,), (0,)), ((), ())), preferre...  21 us
  transfers between devices with their start and end apart: 6, of which 6 were waited for; matrix products, arithmetic and copies ran while one was open for 5% of the time, Pallas kernels for 0%

commit v1 on v0

v1 whole, which is shorter than its diff:
```python
import functools
import math

import jax
import jax.numpy as jnp
from jax import lax
from jax.experimental import pallas as pl
from jax.experimental.pallas import tpu as pltpu
from jax.sharding import PartitionSpec as P

LEVELS = 4
VMEM_BYTES = 60 * 1024 * 1024
ROOT = math.sqrt(2.0 / math.pi)


def contract_cols(left_side, right_side):
    return lax.dot_general(
        left_side, right_side, (((1,), (1,)), ((), ())), preferred_element_type=jnp.float32
    )


def contract_rows(left_side, right_side):
    return lax.dot_general(
        left_side, right_side, (((0,), (0,)), ((), ())), preferred_element_type=jnp.float32
    )


def gelu_and_slope(pre_act):
    square = pre_act * pre_act
    tanh = jnp.tanh(ROOT * pre_act * (1.0 + 0.044715 * square))
    half = 0.5 * (1.0 + tanh)
    slope = half + 0.5 * pre_act * (1.0 - tanh * tanh) * (ROOT * (1.0 + 0.134145 * square))
    return pre_act * half, slope


def fill(meta, blocks, x_full, c_full):
    rows = x_full.shape[0]
    for spot, block in enumerate(blocks):
        width = block.shape[1]
        at = pl.ds(pl.multiple_of(meta[3 + spot], 128), width)
        x_full[:, at] = block[:rows, :]
        c_full[:, at] = block[rows:, :]


def own_columns(meta, x_full, c_full, x_cols, c_cols):
    at = pl.ds(pl.multiple_of(meta[2], 128), x_cols.shape[1])
    x_cols[...] = x_full[:, at]
    c_cols[...] = c_full[:, at]


def activations(meta, x_full, c_full, w_first, w_second):
    rows = x_full.shape[0]
    units = w_first.shape[1]
    pre_act = jnp.dot(x_full[...], w_first[...], preferred_element_type=jnp.float32)
    back_hidden = contract_cols(c_full[...], w_second[...])
    hidden, slope = gelu_and_slope(pre_act)
    unit_ids = meta[0] + pl.program_id(0) * units + lax.broadcasted_iota(jnp.int32, (rows, units), 1)
    row_ids = lax.broadcasted_iota(jnp.int32, (rows, units), 0)
    keep = unit_ids < lax.shift_right_logical(meta[1], row_ids // (rows // LEVELS))
    hidden = jnp.where(keep, hidden, 0.0).astype(jnp.bfloat16)
    back_pre = jnp.where(keep, back_hidden * slope, 0.0).astype(jnp.bfloat16)
    return hidden, back_pre


def home_kernel(count, meta, *refs):
    blocks, (w_first, w_second) = refs[:count], refs[count : count + 2]
    parts, hidden_out, back_out, x_cols, c_cols, x_full, c_full, total_out, total_in = refs[count + 2 :]
    step = pl.program_id(0)
    rows = x_full.shape[0]

    @pl.when(step == 0)
    def _():
        fill(meta, blocks, x_full, c_full)
        own_columns(meta, x_full, c_full, x_cols, c_cols)

    hidden, back_pre = activations(meta, x_full, c_full, w_first, w_second)
    hidden_out[...] = hidden
    back_out[...] = back_pre
    share_out = jnp.dot(hidden, w_second[...], preferred_element_type=jnp.float32)
    share_in = contract_cols(back_pre, w_first[...])

    @pl.when(step == 0)
    def _():
        total_out[...] = share_out
        total_in[...] = share_in

    @pl.when(step > 0)
    def _():
        total_out[...] += share_out
        total_in[...] += share_in

    @pl.when(step == pl.num_programs(0) - 1)
    def _():
        for spot, block in enumerate(blocks):
            at = pl.ds(pl.multiple_of(meta[3 + spot], 128), block.shape[1])
            parts[spot, :rows, :] = total_out[:, at].astype(jnp.bfloat16)
            parts[spot, rows:, :] = total_in[:, at].astype(jnp.bfloat16)


def away_kernel(count, meta, *refs):
    blocks, (w_first, w_second) = refs[:count], refs[count : count + 2]
    hidden_out, back_out, x_cols, c_cols, x_full, c_full = refs[count + 2 :]

    @pl.when(pl.program_id(0) == 0)
    def _():
        fill(meta, blocks, x_full, c_full)
        own_columns(meta, x_full, c_full, x_cols, c_cols)

    hidden, back_pre = activations(meta, x_full, c_full, w_first, w_second)
    hidden_out[...] = hidden
    back_out[...] = back_pre


def last_kernel(count, others, meta, *refs):
    blocks, (w_first, w_second) = refs[:count], refs[count : count + 2]
    refs = refs[count + 2 :]
    past = [refs[4 * spot : 4 * spot + 4] for spot in range(others)]
    grad_in, grad_out, x_full, c_full, x_turned, c_all, hidden_all, back_all = refs[4 * others :]
    rows = x_full.shape[0]
    own = pl.ds(others * rows, rows)

    @pl.when(pl.program_id(0) == 0)
    def _():
        fill(meta, blocks, x_full, c_full)
        at = pl.ds(pl.multiple_of(meta[2], 128), c_all.shape[1])
        for spot in range(others):
            x_turned[:, pl.ds(spot * rows, rows)] = past[spot][2][...].T
            c_all[pl.ds(spot * rows, rows), :] = past[spot][3][...]
        x_turned[:, own] = x_full[:, at].T
        c_all[own, :] = c_full[:, at]

    hidden, back_pre = activations(meta, x_full, c_full, w_first, w_second)
    for spot in range(others):
        hidden_all[pl.ds(spot * rows, rows), :] = past[spot][0][...]
        back_all[pl.ds(spot * rows, rows), :] = past[spot][1][...]
    hidden_all[own, :] = hidden
    back_all[own, :] = back_pre
    grad_in[...] = jnp.dot(x_turned[...], back_all[...], preferred_element_type=jnp.float32)
    grad_out[...] = contract_rows(hidden_all[...], c_all[...])


def whole_spec(shape):
    zeros = (0,) * len(shape)
    return pl.BlockSpec(shape, lambda step, meta: zeros)


def unit_block(units):
    for size in (512, 384, 256, 128):
        if units % size == 0:
            return size
    return units


def run_kernel(kernel, meta, whole_in, unit_cols_in, w_in, w_out, outs, scratch, flops, order):
    units = w_in.shape[1]
    size = unit_block(units)
    cols = lambda rows: pl.BlockSpec((rows, size), lambda step, meta: (0, step))
    by_rows = lambda width: pl.BlockSpec((size, width), lambda step, meta: (step, 0))
    inputs, in_specs = [], []
    for kind, array in order:
        inputs.append(array)
        if kind == "whole":
            in_specs.append(whole_spec(array.shape))
        elif kind == "cols":
            in_specs.append(cols(array.shape[0]))
        else:
            in_specs.append(by_rows(array.shape[1]))
    out_specs = [
        whole_spec(shape) if kind == "whole" else cols(shape[0]) if kind == "cols" else by_rows(shape[1])
        for shape, _, kind in outs
    ]
    moved = sum(array.size * array.dtype.itemsize for array in inputs)
    moved += sum(math.prod(shape) * jnp.dtype(dtype).itemsize for shape, dtype, _ in outs)
    return pl.pallas_call(
        kernel,
        out_shape=[jax.ShapeDtypeStruct(shape, dtype) for shape, dtype, _ in outs],
        grid_spec=pltpu.PrefetchScalarGridSpec(
            num_scalar_prefetch=1,
            grid=(units // size,),
            in_specs=in_specs,
            out_specs=out_specs,
            scratch_shapes=scratch,
        ),
        compiler_params=pltpu.CompilerParams(
            dimension_semantics=("arbitrary",), vmem_limit_bytes=VMEM_BYTES
        ),
        cost_estimate=pl.CostEstimate(flops=flops, bytes_accessed=moved, transcendentals=0),
    )(meta, *inputs)


def home_pass(meta, blocks, w_in, w_out, n_dp):
    rows2, width = blocks[0].shape
    rows, (model, units) = rows2 // 2, w_in.shape
    own = model // n_dp
    order = [("whole", block) for block in blocks] + [("cols", w_in), ("rows", w_out)]
    bf16 = jnp.bfloat16
    return run_kernel(
        functools.partial(home_kernel, len(blocks)), meta, None, None, w_in, w_out,
        [
            ((len(blocks), rows2, width), bf16, "whole"),
            ((rows, units), bf16, "cols"),
            ((rows, units), bf16, "cols"),
            ((rows, own), bf16, "whole"),
            ((rows, own), bf16, "whole"),
        ],
        [pltpu.VMEM((rows, model), bf16)] * 2 + [pltpu.VMEM((rows, model), jnp.float32)] * 2,
        8 * rows * model * units,
        order,
    )


def away_pass(meta, blocks, w_in, w_out, n_dp):
    rows, (model, units) = blocks[0].shape[0] // 2, w_in.shape
    own = model // n_dp
    order = [("whole", block) for block in blocks] + [("cols", w_in), ("rows", w_out)]
    bf16 = jnp.bfloat16
    return run_kernel(
        functools.partial(away_kernel, len(blocks)), meta, None, None, w_in, w_out,
        [
            ((rows, units), bf16, "cols"),
            ((rows, units), bf16, "cols"),
            ((rows, own), bf16, "whole"),
            ((rows, own), bf16, "whole"),
        ],
        [pltpu.VMEM((rows, model), bf16)] * 2,
        4 * rows * model * units,
        order,
    )


def last_pass(meta, blocks, past, w_in, w_out, n_dp):
    rows, (model, units) = blocks[0].shape[0] // 2, w_in.shape
    own = model // n_dp
    size = unit_block(units)
    everyone = rows * (len(past) + 1)
    order = [("whole", block) for block in blocks] + [("cols", w_in), ("rows", w_out)]
    for hidden, back_pre, x_cols, c_cols in past:
        order += [("cols", hidden), ("cols", back_pre), ("whole", x_cols), ("whole", c_cols)]
    bf16 = jnp.bfloat16
    return run_kernel(
        functools.partial(last_kernel, len(blocks), len(past)), meta, None, None, w_in, w_out,
        [((own, units), jnp.float32, "cols"), ((units, own), jnp.float32, "rows")],
        [
            pltpu.VMEM((rows, model), bf16),
            pltpu.VMEM((rows, model), bf16),
            pltpu.VMEM((own, everyone), bf16),
            pltpu.VMEM((everyone, own), bf16),
            pltpu.VMEM((everyone, size), bf16),
            pltpu.VMEM((everyone, size), bf16),
        ],
        4 * rows * model * units + 4 * everyone * own * units,
        order,
    )


def shards(patches, ordering, w_in, w_out, cotangent):
    n_tp, n_dp = lax.axis_size("tp"), lax.axis_size("dp")
    tp_rank, dp_rank = lax.axis_index("tp"), lax.axis_index("dp")
    rows, width = patches.shape
    model, units = w_in.shape
    paired = n_tp == 4

    def across(array, bits):
        return lax.ppermute(array, "tp", [(rank, rank ^ bits) for rank in range(n_tp)])

    def onward(array):
        return lax.ppermute(array, "dp", [(rank, (rank + 1) % n_dp) for rank in range(n_dp)])

    def spread(chunk):
        if not paired:
            return [lax.all_gather(chunk, "tp", axis=1, tiled=True)]
        opposite = across(chunk, 2)
        return [chunk, across(chunk, 1), opposite, across(opposite, 1)]

    offsets = [tp_rank ^ spot for spot in range(4)] if paired else [0]
    meta = jnp.stack(
        [tp_rank * units, jnp.int32(units * n_tp), dp_rank * (model // n_dp)]
        + [jnp.int32(offset * width) for offset in offsets]
    ).astype(jnp.int32)

    pick = (ordering[:, None] == jnp.arange(rows, dtype=jnp.int32)[None, :]).astype(jnp.bfloat16)
    place = lambda array: jnp.dot(pick, array, preferred_element_type=jnp.float32).astype(jnp.bfloat16)
    chunk = jnp.concatenate([place(patches), place(cotangent)], axis=0)

    parts, *kept = home_pass(meta, spread(chunk), w_in, w_out, n_dp)
    past = [kept]
    for step in range(1, n_dp):
        chunk = onward(chunk)
        blocks = spread(chunk)
        if step < n_dp - 1:
            past.append(away_pass(meta, blocks, w_in, w_out, n_dp))
        else:
            grad_in, grad_out = last_pass(meta, blocks, past, w_in, w_out, n_dp)

    if paired:
        far = across(parts[3], 1).astype(jnp.float32) + parts[2].astype(jnp.float32)
        near = across(parts[1], 1).astype(jnp.float32) + parts[0].astype(jnp.float32)
        summed = near + across(far.astype(jnp.bfloat16), 2).astype(jnp.float32)
    else:
        summed = lax.psum_scatter(parts[0], "tp", scatter_dimension=1, tiled=True)
    summed = summed.astype(jnp.bfloat16)
    put_back = lambda array: contract_rows(pick, array).astype(jnp.bfloat16)
    return (put_back(summed[:rows]), put_back(summed[rows:]), grad_in, grad_out)


def solution(mesh):
    return jax.shard_map(
        shards,
        mesh=mesh,
        in_specs=(
            P(("rep", "dp"), "tp"),
            P(("rep", "dp")),
            P(None, "tp"),
            P("tp", None),
            P(("rep", "dp"), "tp"),
        ),
        out_specs=(
            P(("rep", "dp"), "tp"),
            P(("rep", "dp"), "tp"),
            P(("rep", "dp"), "tp"),
            P(("rep", "tp"), "dp"),
        ),
        check_vma=False,
    )
```

time: 969 us -> 176 us (0.18)
  waiting for transfers between devices: 693 us -> 46.5 us
  matrix products: 212 us -> 4.59 us
  Pallas kernels: 0 us -> 101 us
  other arithmetic: 24 us -> 2.77 us
  between operations: 14.4 us -> 0.96 us
  starting transfers between devices: 0.24 us -> 13.4 us
  local copies, waits for them, and re-layouts: 18.1 us -> 5.97 us
    reduce_scatter x4 -> x0, waiting for transfers between devices: 654 us -> none  [the longest x1 313 us: shards(): lax.psum_scatter(term_in.astype(jnp.bfloat16), 'dp', scatter_dimension=0,...]
    dot_general x16 -> x2, matrix products: 191 us -> 2.29 us  [shards(): jnp.dot(pick, array, preferred_element_type=jnp.float32)]
    pallas_call x0 -> x4, Pallas kernels: none -> 101 us  [run_kernel(): pl.pallas_call(kernel, out_shape=[jax.ShapeDtypeStruct(shape, dtype) for...]
    ppermute x0 -> x18, waiting for transfers between devices: none -> 46.5 us  [the longest x15 28.4 us: across(): lax.ppermute(array, 'tp', [(rank, rank ^ bits) for rank in range(n_tp)])]
    all_gather x2 -> x0, waiting for transfers between devices: 37.2 us -> none  [the longest x1 21.9 us: shards(): lax.all_gather(cotangent, 'tp', axis=1, tiled=True)]
    dot_general x2, matrix products: 21 us -> 2.3 us  [contract_rows(): lax.dot_general(left_side, right_side, (((0,), (0,)), ((), ())), preferre...]
    gather x4 -> x0, local copies, waits for them, and re-layouts: 16.7 us -> none  [the longest x1 5.91 us: shards(): cot_sorted = jnp.take(cot_all, ordering, axis=0)]
    ppermute x0 -> x18, starting transfers between devices: none -> 13.4 us  [the longest x15 10 us: across(): lax.ppermute(array, 'tp', [(rank, rank ^ bits) for rank in range(n_tp)])]
  transfers between devices with their start and end apart: 6 -> 18, of which waited for: 6 -> 5; matrix products, arithmetic and copies ran while one was open for 5% -> 4% of each run, Pallas kernels for 0% -> 40%
where the time goes in v1:
time: 176 us; the launch traced here: 175 us
  Pallas kernels  101 us (57%)
  waiting for transfers between devices  46.5 us (26%)
  starting transfers between devices  13.4 us (8%)
  local copies, waits for them, and re-layouts  5.97 us (3%)
  matrix products  4.59 us (3%)
  other arithmetic  2.77 us (2%)
    pallas_call x4, Pallas kernels, run_kernel(): pl.pallas_call(kernel, out_shape=[jax.ShapeDtypeStruct(shape, dtype) for...  101 us
    ppermute x15, waiting for transfers between devices, across(): lax.ppermute(array, 'tp', [(rank, rank ^ bits) for rank in range(n_tp)])  28.4 us
    ppermute x3, waiting for transfers between devices, onward(): lax.ppermute(array, 'dp', [(rank, (rank + 1) % n_dp) for rank in range(n_...  18.1 us
    ppermute x15, starting transfers between devices, across(): lax.ppermute(array, 'tp', [(rank, rank ^ bits) for rank in range(n_tp)])  10 us
    unnamed x18, local copies, waits for them, and re-layouts  3.65 us
  transfers between devices with their start and end apart: 18, of which 5 were waited for; matrix products, arithmetic and copies ran while one was open for 4% of the time, Pallas kernels for 40%

profile of v1, /device:TPU:0, one launch (start us, length us, event | category | flops | bytes accessed | tf_op | source)
XLA Modules:
  0.0 175.5 jit_solution(14512395155245909048)
XLA Ops:
  0.6 1.0 copy-done
  1.6 1.0 convolution_convert_fusion.3
  2.6 1.3 convolution_convert_fusion.2
  4.0 3.0 %collective-permute-start.1 = (bf16[512,768]{1,0:T(8,128)(2,1)S(1)}, bf16[512,768]{1,0:T(8,128)(2,1)S(1)}, u32[]{:S(2)}, u32[]{:S(2)}) collective-permute-start(bf16[512,768]{1,0:T(8,128)(2,1)S(1)} %pad_maximum_fusion.refs_0_), channel_id=1, source_target_pairs={{0,8},{4,12},{8,0},{12,4},{1,9},{5,13},{9,1},{13,5},{2,10},{6,14},... | collective-permute-start | bytes 2359304 | tf_op jit(solution)/shard_map/ppermute | solution.py:264
  7.0 1.6 collective-permute-start.6
  8.6 16.0 %collective-permute-done.1.refs_2_ = bf16[512,768]{1,0:T(8,128)(2,1)S(1)} collective-permute-done((bf16[512,768]{1,0:T(8,128)(2,1)S(1)}, bf16[512,768]{1,0:T(8,128)(2,1)S(1)}, u32[]{:S(2)}, u32[]{:S(2)}) %collective-permute-start.1) | collective-permute-done | bytes 786464 | tf_op jit(solution)/shard_map/ppermute | solution.py:264
  25.3 2.7 %collective-permute-done.6.refs_0_ = bf16[512,768]{1,0:T(8,128)(2,1)} collective-permute-done((bf16[512,768]{1,0:T(8,128)(2,1)S(1)}, bf16[512,768]{1,0:T(8,128)(2,1)}, u32[]{:S(2)}, u32[]{:S(2)}) %collective-permute-start.6) | collective-permute-done | bytes 786464 | tf_op jit(solution)/shard_map/ppermute | solution.py:267
  29.5 0.9 copy-done.8
  30.4 32.0 %shard_map.84 = (bf16[4,512,768]{2,1,0:T(8,128)(2,1)}, bf16[256,3072]{1,0:T(8,128)(2,1)}, bf16[256,3072]{1,0:T(8,128)(2,1)}, bf16[256,768]{1,0:T(8,128)(2,1)}, bf16[256,768]{1,0:T(8,128)(2,1)}) custom-call(s32[7]{0:T(128)} %stack.27.meta, bf16[512,768]{1,0:T(8,128)(2,1)} %copy-done.3, bf16[512,768]{1,0:T(8,128)(2,1)} %copy-done.7, ...), custom_call_target="tpu_custom_call" | custom-call | flops 19327352832 | bytes 47972352 | tf_op jit(solution)/shard_map/pallas_call | solution.py:174
  62.4 1.6 slice_bitcast_fusion.1
  64.7 1.7 collective-permute-start.8
  66.7 1.4 collective-permute-start.16
  68.1 1.1 fusion
  69.2 2.3 %collective-permute-start.5 = (bf16[512,768]{1,0:T(8,128)(2,1)}, bf16[512,768]{1,0:T(8,128)(2,1)}, u32[]{:S(2)}, u32[]{:S(2)}) collective-permute-start(bf16[512,768]{1,0:T(8,128)(2,1)} %fusion), channel_id=1, source_target_pairs={{0,8},{4,12},{8,0},{12,4},{1,9},{5,13},{9,1},{13,5},{2,10},{6,14},... | collective-permute-start | bytes 2359304 | tf_op jit(solution)/shard_map/ppermute | solution.py:264
  71.5 15.3 %collective-permute-done.8.refs_0_ = bf16[512,768]{1,0:T(8,128)(2,1)} collective-permute-done((bf16[512,768]{1,0:T(8,128)(2,1)}, bf16[512,768]{1,0:T(8,128)(2,1)}, u32[]{:S(2)}, u32[]{:S(2)}) %collective-permute-start.8) | collective-permute-done | bytes 786464 | tf_op jit(solution)/shard_map/ppermute | solution.py:267
  86.9 1.5 collective-permute-start.10
  88.4 19.3 %shard_map.85 = (bf16[256,3072]{1,0:T(8,128)(2,1)}, bf16[256,3072]{1,0:T(8,128)(2,1)}, bf16[256,768]{1,0:T(8,128)(2,1)}, bf16[256,768]{1,0:T(8,128)(2,1)}) custom-call(s32[7]{0:T(128)} %stack.27.meta, bf16[512,768]{1,0:T(8,128)(2,1)} %collective-permute-done.6.refs_0_, bf16[512,768]{1,0:T(8,128)(2,1)} %collective-permute-done.12.refs_1_, ...), custom_call_target="tpu_custom_call" | custom-call | flops 9663676416 | bytes 44826624 | tf_op jit(solution)/shard_map/pallas_call | solution.py:174
  108.3 12.1 %collective-permute-done.10.refs_2_ = bf16[512,768]{1,0:T(8,128)(2,1)} collective-permute-done((bf16[512,768]{1,0:T(8,128)(2,1)}, bf16[512,768]{1,0:T(8,128)(2,1)}, u32[]{:S(2)}, u32[]{:S(2)}) %collective-permute-start.10) | collective-permute-done | bytes 786464 | tf_op jit(solution)/shard_map/ppermute | solution.py:264
  120.4 1.7 fusion.2
  122.1 1.2 convolution_convert_fusion
  123.2 1.1 convolution_convert_fusion.1
  124.4 0.9 copy-done.4
  125.3 19.3 %shard_map.86 = (bf16[256,3072]{1,0:T(8,128)(2,1)}, bf16[256,3072]{1,0:T(8,128)(2,1)}, bf16[256,768]{1,0:T(8,128)(2,1)}, bf16[256,768]{1,0:T(8,128)(2,1)}) custom-call(s32[7]{0:T(128)} %stack.27.meta, bf16[512,768]{1,0:T(8,128)(2,1)} %collective-permute-done.7.refs_0_, bf16[512,768]{1,0:T(8,128)(2,1)} %collective-permute-done.15.refs_1_, ...), custom_call_target="tpu_custom_call" | custom-call | flops 9663676416 | bytes 44826624 | tf_op jit(solution)/shard_map/pallas_call | solution.py:174
  144.6 30.7 %shard_map.87 = (f32[768,3072]{1,0:T(8,128)}, f32[3072,768]{1,0:T(8,128)}) custom-call(s32[7]{0:T(128)} %stack.27.meta, bf16[512,768]{1,0:T(8,128)(2,1)} %collective-permute-done.8.refs_0_, bf16[512,768]{1,0:T(8,128)(2,1)} %collective-permute-done.9.refs_1_, bf16[512,768]{1,0:T(8,128)(2,1)} %collective-permute-done.10.refs_2_, ...), custom_call_target="tpu_custom_call" | custom-call | flops 19327352832 | bytes 71565312 | tf_op jit(solution)/shard_map/pallas_call | solution.py:174
  (43 shorter events, 3.8 us)
Async XLA Ops:
  0.6 1.0 copy-start
  4.0 24.6 %copy-start.3 = (bf16[512,768]{1,0:T(8,128)(2,1)}, bf16[512,768]{1,0:T(8,128)(2,1)S(1)}, u32[]{:S(2)}) copy-start(bf16[512,768]{1,0:T(8,128)(2,1)S(1)} %pad_maximum_fusion.refs_0_) | copy-start | bytes 2359300
  4.0 20.6 %collective-permute-start.1 = (bf16[512,768]{1,0:T(8,128)(2,1)S(1)}, bf16[512,768]{1,0:T(8,128)(2,1)S(1)}, u32[]{:S(2)}, u32[]{:S(2)}) collective-permute-start(bf16[512,768]{1,0:T(8,128)(2,1)S(1)} %pad_maximum_fusion.refs_0_), channel_id=1, source_target_pairs={{0,8},{4,12},{8,0},{12,4},{1,9},{5,13},{9,1},{13,5},{2,10},{6,14},... | collective-permute-start | bytes 2359304 | tf_op jit(solution)/shard_map/ppermute | solution.py:264
  7.0 21.0 %collective-permute-start.6 = (bf16[512,768]{1,0:T(8,128)(2,1)S(1)}, bf16[512,768]{1,0:T(8,128)(2,1)}, u32[]{:S(2)}, u32[]{:S(2)}) collective-permute-start(bf16[512,768]{1,0:T(8,128)(2,1)S(1)} %pad_maximum_fusion.refs_0_), channel_id=1, source_target_pairs={{0,1},{1,2},{2,3},{3,0},{4,5},{5,6},{6,7},{7,4},{8,9},{9,10},{10,1... | collective-permute-start | bytes 2359304 | tf_op jit(solution)/shard_map/ppermute | solution.py:267
  8.6 20.0 %collective-permute-start = (bf16[512,768]{1,0:T(8,128)(2,1)S(1)}, bf16[512,768]{1,0:T(8,128)(2,1)S(1)}, u32[]{:S(2)}, u32[]{:S(2)}) collective-permute-start(bf16[512,768]{1,0:T(8,128)(2,1)S(1)} %pad_maximum_fusion.refs_0_), channel_id=1, source_target_pairs={{0,4},{4,0},{8,12},{12,8},{1,5},{5,1},{9,13},{13,9},{2,6},{6,2},{1... | collective-permute-start | bytes 2359304 | tf_op jit(solution)/shard_map/ppermute | solution.py:264
  24.6 4.0 %copy-start.6 = (bf16[512,768]{1,0:T(8,128)(2,1)}, bf16[512,768]{1,0:T(8,128)(2,1)S(1)}, u32[]{:S(2)}) copy-start(bf16[512,768]{1,0:T(8,128)(2,1)S(1)} %collective-permute-done.1.refs_2_) | copy-start | bytes 2359300
  24.6 4.0 %collective-permute-start.2 = (bf16[512,768]{1,0:T(8,128)(2,1)S(1)}, bf16[512,768]{1,0:T(8,128)(2,1)S(1)}, u32[]{:S(2)}, u32[]{:S(2)}) collective-permute-start(bf16[512,768]{1,0:T(8,128)(2,1)S(1)} %collective-permute-done.1.refs_2_), channel_id=1, source_target_pairs={{0,4},{4,0},{8,12},{12,8},{1,5},{5,1},{9,13},{13,9},{2,6},{6,2},{1... | collective-permute-start | bytes 2359304 | tf_op jit(solution)/shard_map/ppermute | solution.py:264
  28.0 36.6 %collective-permute-start.13 = (bf16[512,768]{1,0:T(8,128)(2,1)}, bf16[512,768]{1,0:T(8,128)(2,1)}, u32[]{:S(2)}, u32[]{:S(2)}) collective-permute-start(bf16[512,768]{1,0:T(8,128)(2,1)} %collective-permute-done.6.refs_0_), channel_id=1, source_target_pairs={{0,8},{4,12},{8,0},{12,4},{1,9},{5,13},{9,1},{13,5},{2,10},{6,14},... | collective-permute-start | bytes 2359304 | tf_op jit(solution)/shard_map/ppermute | solution.py:264
  28.5 36.2 %collective-permute-start.7 = (bf16[512,768]{1,0:T(8,128)(2,1)}, bf16[512,768]{1,0:T(8,128)(2,1)}, u32[]{:S(2)}, u32[]{:S(2)}) collective-permute-start(bf16[512,768]{1,0:T(8,128)(2,1)} %collective-permute-done.6.refs_0_), channel_id=1, source_target_pairs={{0,1},{1,2},{2,3},{3,0},{4,5},{5,6},{6,7},{7,4},{8,9},{9,10},{10,1... | collective-permute-start | bytes 2359304 | tf_op jit(solution)/shard_map/ppermute | solution.py:267
  62.4 5.8 %copy-start.2 = (bf16[4,512,768]{2,1,0:T(8,128)(2,1)S(1)}, bf16[4,512,768]{2,1,0:T(8,128)(2,1)}, u32[]{:S(2)}) copy-start(bf16[4,512,768]{2,1,0:T(8,128)(2,1)} %get-tuple-element.19) | copy-start | bytes 9437188
  64.0 2.7 %collective-permute-start.4 = (bf16[512,768]{1,0:T(8,128)(2,1)S(1)}, bf16[512,768]{1,0:T(8,128)(2,1)S(1)}, u32[]{:S(2)}, u32[]{:S(2)}) collective-permute-start(bf16[512,768]{1,0:T(8,128)(2,1)S(1)} %get-tuple-element.35), channel_id=1, source_target_pairs={{0,4},{4,0},{8,12},{12,8},{1,5},{5,1},{9,13},{13,9},{2,6},{6,2},{1... | collective-permute-start | bytes 2359304 | tf_op jit(solution)/shard_map/ppermute | solution.py:264
  64.1 5.1 %collective-permute-start.12 = (bf16[512,768]{1,0:T(8,128)(2,1)}, bf16[512,768]{1,0:T(8,128)(2,1)}, u32[]{:S(2)}, u32[]{:S(2)}) collective-permute-start(bf16[512,768]{1,0:T(8,128)(2,1)} %collective-permute-done.6.refs_0_), channel_id=1, source_target_pairs={{0,4},{4,0},{8,12},{12,8},{1,5},{5,1},{9,13},{13,9},{2,6},{6,2},{1... | collective-permute-start | bytes 2359304 | tf_op jit(solution)/shard_map/ppermute | solution.py:264
  64.6 4.6 %collective-permute-start.14 = (bf16[512,768]{1,0:T(8,128)(2,1)}, bf16[512,768]{1,0:T(8,128)(2,1)}, u32[]{:S(2)}, u32[]{:S(2)}) collective-permute-start(bf16[512,768]{1,0:T(8,128)(2,1)} %collective-permute-done.13.refs_2_), channel_id=1, source_target_pairs={{0,4},{4,0},{8,12},{12,8},{1,5},{5,1},{9,13},{13,9},{2,6},{6,2},{1... | collective-permute-start | bytes 2359304 | tf_op jit(solution)/shard_map/ppermute | solution.py:264
  64.7 22.2 %collective-permute-start.8 = (bf16[512,768]{1,0:T(8,128)(2,1)}, bf16[512,768]{1,0:T(8,128)(2,1)}, u32[]{:S(2)}, u32[]{:S(2)}) collective-permute-start(bf16[512,768]{1,0:T(8,128)(2,1)} %collective-permute-done.7.refs_0_), channel_id=1, source_target_pairs={{0,1},{1,2},{2,3},{3,0},{4,5},{5,6},{6,7},{7,4},{8,9},{9,10},{10,1... | collective-permute-start | bytes 2359304 | tf_op jit(solution)/shard_map/ppermute | solution.py:267
  66.4 41.4 %collective-permute-start.3 = (bf16[512,768]{1,0:T(8,128)(2,1)S(1)}, bf16[512,768]{1,0:T(8,128)(2,1)}, u32[]{:S(2)}, u32[]{:S(2)}) collective-permute-start(bf16[512,768]{1,0:T(8,128)(2,1)S(1)} %get-tuple-element.34), channel_id=1, source_target_pairs={{0,4},{4,0},{8,12},{12,8},{1,5},{5,1},{9,13},{13,9},{2,6},{6,2},{1... | collective-permute-start | bytes 2359304 | tf_op jit(solution)/shard_map/ppermute | solution.py:264
  66.7 41.0 %collective-permute-start.16 = (bf16[512,768]{1,0:T(8,128)(2,1)}, bf16[512,768]{1,0:T(8,128)(2,1)}, u32[]{:S(2)}, u32[]{:S(2)}) collective-permute-start(bf16[512,768]{1,0:T(8,128)(2,1)} %collective-permute-done.7.refs_0_), channel_id=1, source_target_pairs={{0,8},{4,12},{8,0},{12,4},{1,9},{5,13},{9,1},{13,5},{2,10},{6,14},... | collective-permute-start | bytes 2359304 | tf_op jit(solution)/shard_map/ppermute | solution.py:264
  69.2 55.2 %collective-permute-start.15 = (bf16[512,768]{1,0:T(8,128)(2,1)}, bf16[512,768]{1,0:T(8,128)(2,1)}, u32[]{:S(2)}, u32[]{:S(2)}) collective-permute-start(bf16[512,768]{1,0:T(8,128)(2,1)} %collective-permute-done.7.refs_0_), channel_id=1, source_target_pairs={{0,4},{4,0},{8,12},{12,8},{1,5},{5,1},{9,13},{13,9},{2,6},{6,2},{1... | collective-permute-start | bytes 2359304 | tf_op jit(solution)/shard_map/ppermute | solution.py:264
  69.2 51.2 %collective-permute-start.5 = (bf16[512,768]{1,0:T(8,128)(2,1)}, bf16[512,768]{1,0:T(8,128)(2,1)}, u32[]{:S(2)}, u32[]{:S(2)}) collective-permute-start(bf16[512,768]{1,0:T(8,128)(2,1)} %fusion), channel_id=1, source_target_pairs={{0,8},{4,12},{8,0},{12,4},{1,9},{5,13},{9,1},{13,5},{2,10},{6,14},... | collective-permute-start | bytes 2359304 | tf_op jit(solution)/shard_map/ppermute | solution.py:264
  86.9 33.5 %collective-permute-start.10 = (bf16[512,768]{1,0:T(8,128)(2,1)}, bf16[512,768]{1,0:T(8,128)(2,1)}, u32[]{:S(2)}, u32[]{:S(2)}) collective-permute-start(bf16[512,768]{1,0:T(8,128)(2,1)} %collective-permute-done.8.refs_0_), channel_id=1, source_target_pairs={{0,8},{4,12},{8,0},{12,4},{1,9},{5,13},{9,1},{13,5},{2,10},{6,14},... | collective-permute-start | bytes 2359304 | tf_op jit(solution)/shard_map/ppermute | solution.py:264
  107.7 14.4 %copy-start.5 = (s32[256]{0:T(256)S(1)}, s32[256]{0:T(256)}, u32[]{:S(2)}) copy-start(s32[256]{0:T(256)} %param.6) | copy-start | bytes 3076
  107.7 36.8 %collective-permute-start.9 = (bf16[512,768]{1,0:T(8,128)(2,1)}, bf16[512,768]{1,0:T(8,128)(2,1)}, u32[]{:S(2)}, u32[]{:S(2)}) collective-permute-start(bf16[512,768]{1,0:T(8,128)(2,1)} %collective-permute-done.8.refs_0_), channel_id=1, source_target_pairs={{0,4},{4,0},{8,12},{12,8},{1,5},{5,1},{9,13},{13,9},{2,6},{6,2},{1... | collective-permute-start | bytes 2359304 | tf_op jit(solution)/shard_map/ppermute | solution.py:264
  107.8 16.6 %collective-permute-start.17 = (bf16[512,768]{1,0:T(8,128)(2,1)}, bf16[512,768]{1,0:T(8,128)(2,1)S(1)}, u32[]{:S(2)}, u32[]{:S(2)}) collective-permute-start(bf16[512,768]{1,0:T(8,128)(2,1)} %collective-permute-done.16.refs_2_), channel_id=1, source_target_pairs={{0,4},{4,0},{8,12},{12,8},{1,5},{5,1},{9,13},{13,9},{2,6},{6,2},{1... | collective-permute-start | bytes 2359304 | tf_op jit(solution)/shard_map/ppermute | solution.py:264
  120.4 24.2 %collective-permute-start.11 = (bf16[512,768]{1,0:T(8,128)(2,1)}, bf16[512,768]{1,0:T(8,128)(2,1)}, u32[]{:S(2)}, u32[]{:S(2)}) collective-permute-start(bf16[512,768]{1,0:T(8,128)(2,1)} %collective-permute-done.10.refs_2_), channel_id=1, source_target_pairs={{0,4},{4,0},{8,12},{12,8},{1,5},{5,1},{9,13},{13,9},{2,6},{6,2},{1... | collective-permute-start | bytes 2359304 | tf_op jit(solution)/shard_map/ppermute | solution.py:264
  144.6 30.8 %copy-start.1 = (bf16[256,768]{1,0:T(8,128)(2,1)S(1)}, bf16[256,768]{1,0:T(8,128)(2,1)}, u32[]{:S(2)}) copy-start(bf16[256,768]{1,0:T(8,128)(2,1)} %param.5) | copy-start | bytes 1179652
  (3 other events, 2.7 us)

commit v2 on v0

v2 whole, which is shorter than its diff:
```python
import functools
import math

import jax
import jax.numpy as jnp
from jax import lax
from jax.experimental import pallas as pl
from jax.experimental.pallas import tpu as pltpu
from jax.sharding import PartitionSpec as P

LEVELS = 4
MIB = 1024 * 1024
LIM = 23
FIXED = 5
ROOT = math.sqrt(2.0 / math.pi)


def contract_cols(left_side, right_side):
    return lax.dot_general(
        left_side, right_side, (((1,), (1,)), ((), ())), preferred_element_type=jnp.float32
    )


def contract_rows(left_side, right_side):
    return lax.dot_general(
        left_side, right_side, (((0,), (0,)), ((), ())), preferred_element_type=jnp.float32
    )


def gelu_and_slope(pre_act):
    square = pre_act * pre_act
    tanh = jnp.tanh(ROOT * pre_act * (1.0 + 0.044715 * square))
    half = 0.5 * (1.0 + tanh)
    slope = half + 0.5 * pre_act * (1.0 - tanh * tanh) * (ROOT * (1.0 + 0.134145 * square))
    return pre_act * half, slope


def unpack(pieces, at, x_out, c_out, to):
    level = x_out.shape[0] // LEVELS
    first = 0
    for piece in pieces:
        for start in range(0, piece.shape[0], 2 * level):
            x_out[first : first + level, to] = piece[start : start + level, at]
            c_out[first : first + level, to] = piece[start + level : start + 2 * level, at]
            first += level


def fill(meta, blocks, x_full, c_full, base=0, spots=None):
    for spot, pieces in enumerate(blocks):
        if spots is None or spot in spots:
            to = pl.ds(pl.multiple_of(meta[FIXED + spot] - base, 128), pieces[0].shape[1])
            unpack(pieces, slice(None), x_full, c_full, to)


def fill_late(meta, begun, blocks, x_full, c_full):
    if begun:
        fill(meta, blocks, x_full, c_full, meta[4], (2, 3))
    else:
        fill(meta, blocks, x_full, c_full)


def own_columns(meta, blocks, x_cols, c_cols):
    width = x_cols.shape[1]
    start = meta[2] * width
    for spot, pieces in enumerate(blocks):
        wide = pieces[0].shape[1]
        begin = meta[FIXED + spot]

        @pl.when((start >= begin) & (start < begin + wide))
        def _():
            at = pl.ds(pl.multiple_of(start - begin, 128), width) if width < wide else slice(None)
            unpack(pieces, at, x_cols, c_cols, slice(None))


def unit_slice(size, first=0):
    return pl.ds(pl.multiple_of(first + pl.program_id(0) * size, 128), size)


def views(weights):
    if len(weights) == 1:
        half = weights[0].shape[0] // 2
        return weights[0].at[pl.ds(0, half), :], weights[0].at[pl.ds(half, half), :]
    return weights


def products(x_full, c_full, first, weights, units):
    w_first, w_second = weights
    deep = pl.ds(first if isinstance(first, int) else pl.multiple_of(first, 128), x_full.shape[1])
    at = unit_slice(units)
    pre_act = jnp.dot(x_full[...], w_first[deep, at], preferred_element_type=jnp.float32)
    return pre_act, contract_cols(c_full[...], w_second[at, deep])


def activations(meta, pre_act, back_hidden):
    rows, units = pre_act.shape
    hidden, slope = gelu_and_slope(pre_act)
    back_pre = back_hidden * slope
    level = rows // LEVELS
    unit_ids = meta[0] + pl.program_id(0) * units + lax.broadcasted_iota(jnp.int32, (level, units), 1)
    keep = [unit_ids < lax.shift_right_logical(meta[1], level_idx) for level_idx in range(LEVELS)]
    cut = lambda array: jnp.concatenate(
        [
            jnp.where(keep[level_idx], array[level_idx * level : (level_idx + 1) * level], 0.0)
            for level_idx in range(LEVELS)
        ],
        axis=0,
    ).astype(jnp.bfloat16)
    return cut(hidden), cut(back_pre)


def sort_kernel(ordering, patches, cotangent, chunk):
    rows = patches.shape[0]
    level = rows // LEVELS
    patch_ids = lax.broadcasted_iota(jnp.int32, (rows, rows), 0)
    pick = (patch_ids == ordering[...]).astype(jnp.float32).astype(jnp.bfloat16)
    for spot, array in enumerate((patches, cotangent)):
        placed = contract_rows(pick, array[...]).astype(jnp.bfloat16)
        for level_idx in range(LEVELS):
            start = (2 * level_idx + spot) * level
            chunk[start : start + level, :] = placed[level_idx * level : (level_idx + 1) * level]


def restore_kernel(count, ordering, *refs):
    shares, (mixed, grad_patches) = refs[:count], refs[count:]
    rows = mixed.shape[0]
    level = rows // LEVELS
    total = sum(share[...].astype(jnp.float32) for share in shares).astype(jnp.bfloat16)
    patch_ids = lax.broadcasted_iota(jnp.int32, (rows, rows), 0)
    pick = (patch_ids == ordering[...]).astype(jnp.float32).astype(jnp.bfloat16)
    for spot, out in enumerate((mixed, grad_patches)):
        placed = jnp.concatenate(
            [total[(2 * idx + spot) * level : (2 * idx + spot + 1) * level] for idx in range(LEVELS)], axis=0
        )
        out[...] = jnp.dot(pick, placed, preferred_element_type=jnp.float32).astype(jnp.bfloat16)


def split_refs(refs, counts):
    groups = []
    for count in counts:
        groups.append(refs[:count])
        refs = refs[count:]
    return groups, refs


def open_kernel(counts, meta, *refs):
    blocks, (w_in, w_out, weights, pre_out, back_out, x_full, c_full, arrived) = split_refs(refs, counts)
    model, units = w_in.shape[0], pre_out.shape[1]

    def copies(step):
        cols = pl.ds(pl.multiple_of(step * units, 128), units)
        rows = pl.ds(pl.multiple_of(model + step * units, 128), units)
        return (
            pltpu.make_async_copy(w_in.at[:, cols], weights.at[pl.ds(0, model), cols], arrived.at[0, step]),
            pltpu.make_async_copy(w_out.at[cols, :], weights.at[rows, :], arrived.at[1, step]),
        )

    @pl.when(pl.program_id(0) == 0)
    def _():
        for step in range(w_in.shape[1] // units):
            for copy in copies(step):
                copy.start()
        fill(meta, blocks, x_full, c_full, meta[3])

    for copy in copies(pl.program_id(0)):
        copy.wait()
    pre_out[...], back_out[...] = products(x_full, c_full, meta[3], views([weights]), units)


def begin_kernel(counts, held, meta, *refs):
    blocks, refs = split_refs(refs, counts)
    weights, (pre_out, back_out, x_full, c_full) = refs[:held], refs[held:]

    @pl.when(pl.program_id(0) == 0)
    def _():
        fill(meta, blocks, x_full, c_full, meta[3])

    pre_out[...], back_out[...] = products(x_full, c_full, meta[3], views(weights), pre_out.shape[1])


def home_kernel(counts, held, begun, meta, *refs):
    blocks, refs = split_refs(refs, counts)
    (weights, begun, parts), refs = split_refs(refs, (held, begun, len(counts)))
    hidden_out, back_out, x_cols, c_cols, x_full, c_full, total_out, total_in = refs
    step = pl.program_id(0)
    rows, units = hidden_out.shape
    model = total_out.shape[1]
    level = rows // LEVELS

    @pl.when(step == 0)
    def _():
        fill_late(meta, begun, blocks, x_full, c_full)
        own_columns(meta, blocks, x_cols, c_cols)

    hidden, back_pre = late_products(meta, x_full, c_full, begun, weights, units)
    hidden_out[...] = hidden
    back_out[...] = back_pre
    w_first, w_second = views(weights)
    at = unit_slice(units)
    wide = model // 4
    shares = lambda cols: (
        jnp.dot(hidden, w_second[at, cols], preferred_element_type=jnp.float32),
        contract_cols(back_pre, w_first[cols, at]),
    )

    @pl.when(step == 0)
    def _():
        for first in range(0, model, wide):
            cols = pl.ds(first, wide)
            total_out[:, cols], total_in[:, cols] = shares(cols)

    @pl.when(step > 0)
    def _():
        for first in range(0, model, wide):
            cols = pl.ds(first, wide)
            more_out, more_in = shares(cols)
            total_out[:, cols] += more_out
            total_in[:, cols] += more_in

    @pl.when(step == pl.num_programs(0) - 1)
    def _():
        for spot, part in enumerate(parts):
            cols = pl.ds(pl.multiple_of(meta[FIXED + spot], 128), part.shape[1])
            for level_idx in range(LEVELS):
                here = pl.ds(level_idx * level, level)
                start = 2 * level_idx * level
                part[start : start + level, :] = total_out[here, cols].astype(jnp.bfloat16)
                part[start + level : start + 2 * level, :] = total_in[here, cols].astype(jnp.bfloat16)


def late_products(meta, x_full, c_full, begun, weights, units):
    if not begun:
        return activations(meta, *products(x_full, c_full, 0, views(weights), units))
    pre_act, back_hidden = products(x_full, c_full, meta[4], views(weights), units)
    return activations(meta, pre_act + begun[0][...], back_hidden + begun[1][...])


def away_kernel(counts, held, meta, *refs):
    blocks, refs = split_refs(refs, counts)
    weights, (hidden_out, back_out, x_cols, c_cols, x_full, c_full) = refs[:held], refs[held:]

    @pl.when(pl.program_id(0) == 0)
    def _():
        fill(meta, blocks, x_full, c_full)
        own_columns(meta, blocks, x_cols, c_cols)

    hidden_out[...], back_out[...] = late_products(meta, x_full, c_full, (), weights, hidden_out.shape[1])


def last_kernel(counts, held, begun, others, meta, *refs):
    blocks, refs = split_refs(refs, counts)
    (weights, begun, *past), refs = split_refs(refs, (held, begun) + (4,) * others)
    grad_in, grad_out, x_full, c_full, x_cols, x_turned, c_all, hidden_all, back_all = refs
    rows = x_full.shape[0]
    own = pl.ds(others * rows, rows)

    @pl.when(pl.program_id(0) == 0)
    def _():
        for spot in range(others):
            x_turned[:, pl.ds(spot * rows, rows)] = past[spot][2][...].T
            c_all[pl.ds(spot * rows, rows), :] = past[spot][3][...]
        fill_late(meta, begun, blocks, x_full, c_full)
        own_columns(meta, blocks, x_cols, c_all.at[own, :])
        x_turned[:, own] = x_cols[...].T

    hidden, back_pre = late_products(meta, x_full, c_full, begun, weights, hidden_all.shape[1])
    for spot in range(others):
        hidden_all[pl.ds(spot * rows, rows), :] = past[spot][0][...]
        back_all[pl.ds(spot * rows, rows), :] = past[spot][1][...]
    hidden_all[own, :] = hidden
    back_all[own, :] = back_pre
    grad_in[...] = jnp.dot(x_turned[...], back_all[...], preferred_element_type=jnp.float32)
    grad_out[...] = contract_rows(hidden_all[...], c_all[...])


def unit_block(units, most):
    for size in (768, 512, 384, 256, 128):
        if size <= most and units % size == 0:
            return size
    return units


def run_kernel(kernel, name, meta, size, units, inputs, outs, scratch, flops, limit):
    def spec(shape, kind):
        zeros = (0,) * len(shape)
        if kind == "whole":
            return pl.BlockSpec(shape, lambda step, meta: zeros, pipeline_mode=pl.Buffered(1))
        if kind == "cols":
            return pl.BlockSpec((shape[0], size), lambda step, meta: (0, step))
        if kind == "rows":
            return pl.BlockSpec((size, shape[1]), lambda step, meta: (step, 0))
        return pl.BlockSpec(memory_space=pltpu.VMEM if kind == "vmem" else pl.ANY)

    resident = lambda array, kind: pltpu.with_memory_space_constraint(array, pltpu.VMEM if kind == "vmem" else pltpu.HBM)
    shape_of = lambda shape, dtype, kind: (
        pltpu.VMEM(shape, dtype) if kind == "vmem" else jax.ShapeDtypeStruct(shape, dtype)
    )
    moved = sum(array.size * array.dtype.itemsize for array, kind in inputs if kind != "vmem")
    moved += sum(math.prod(shape) * jnp.dtype(dtype).itemsize for shape, dtype, kind in outs if kind != "vmem")
    return pl.pallas_call(
        kernel,
        name=name,
        out_shape=[shape_of(*out) for out in outs],
        grid_spec=pltpu.PrefetchScalarGridSpec(
            num_scalar_prefetch=1,
            grid=(units // size,),
            in_specs=[spec(array.shape, kind) for array, kind in inputs],
            out_specs=[spec(shape, kind) for shape, _, kind in outs],
            scratch_shapes=scratch,
        ),
        compiler_params=pltpu.CompilerParams(dimension_semantics=("arbitrary",), vmem_limit_bytes=limit * MIB),
        cost_estimate=pl.CostEstimate(flops=flops, bytes_accessed=moved, transcendentals=0),
    )(meta, *[resident(*pair) for pair in inputs])


def shards(patches, ordering, w_in, w_out, cotangent):
    n_tp, n_dp = lax.axis_size("tp"), lax.axis_size("dp")
    tp_rank, dp_rank = lax.axis_index("tp"), lax.axis_index("dp")
    rows, width = patches.shape
    model, units = w_in.shape
    own = model // n_dp
    bf16, f32 = jnp.bfloat16, jnp.float32
    paired = n_tp == 4 and model == units
    swap = lambda bits: [(rank, rank ^ bits) for rank in range(n_tp)]
    cross = lambda array, pairs: lax.ppermute(array, "tp", pairs)
    onward = lambda array: lax.ppermute(array, "dp", [(rank, (rank + 1) % n_dp) for rank in range(n_dp)])
    after = lambda array, done: lax.optimization_barrier((array, done))[0]

    def near_of(chunk):
        if not paired:
            return [[lax.all_gather(chunk, "tp", axis=1, tiled=True)]]
        return [[chunk], [cross(chunk, swap(1))]]

    def opposite_of(chunk):
        return cross(chunk, swap(2)) if paired else None

    def rest_of(opposite, done):
        if not paired:
            return []
        opposite = after(opposite, done)
        return [[opposite], [cross(opposite, swap(1))]]

    offsets = [tp_rank ^ spot for spot in range(4)] if paired else [0]
    pair = tp_rank // 2 * 2
    meta = jnp.stack(
        [tp_rank * units, jnp.int32(units * n_tp), dp_rank, pair * width, (pair ^ 2) * width]
        + [jnp.int32(offset * width) for offset in offsets]
    ).astype(jnp.int32)
    size = unit_block(units, 512)
    flat = lambda blocks: [(piece, "vmem" if spot >= 2 else "whole") for spot, pieces in enumerate(blocks) for piece in pieces]
    counts_of = lambda blocks: tuple(len(pieces) for pieces in blocks)
    kept_outs = [((rows, units), bf16, "cols")] * 2 + [((rows, own), bf16, "whole")] * 2
    partial_outs = [((rows, units), f32, "cols")] * 2
    full = [pltpu.VMEM((rows, model), bf16)] * 2
    half = [pltpu.VMEM((rows, model // 2), bf16)] * 2 if paired else full
    share = lambda columns: 4 * rows * columns * units

    in_hbm = lambda array: pltpu.with_memory_space_constraint(array, pltpu.HBM)
    small = pltpu.CompilerParams(vmem_limit_bytes=LIM * MIB)
    chunk = pl.pallas_call(
        sort_kernel, name="sort_rows", out_shape=jax.ShapeDtypeStruct((2 * rows, width), bf16), compiler_params=small
    )(ordering[None, :], in_hbm(patches), in_hbm(cotangent))

    near = near_of(chunk)
    opposite = opposite_of(chunk)
    coming = onward(chunk)
    if paired:
        weights, *begun = run_kernel(
            functools.partial(open_kernel, counts_of(near)), "open_group", meta, size, units,
            flat(near) + [(w_in, "any"), (w_out, "any")],
            [((2 * model, units), bf16, "vmem")] + partial_outs,
            half + [pltpu.SemaphoreType.DMA((2, units // size))],
            share(model // 2),
            LIM,
        )
        held, done = [(weights, "vmem")], begun[0]
    else:
        held, done, begun = [(w_in, "vmem"), (w_out, "vmem")], meta, []
    chunk = after(coming, done)
    blocks = near + rest_of(opposite, done)
    opposite = opposite_of(chunk)
    coming = onward(chunk)
    *parts, hidden, back_pre, x_cols, c_cols = run_kernel(
        functools.partial(home_kernel, counts_of(blocks), len(held), len(begun)), "home_group", meta, size, units,
        flat(blocks) + held + [(array, "cols") for array in begun],
        [((2 * rows, width if paired else model), bf16, "whole")] * len(blocks) + kept_outs,
        half + [pltpu.VMEM((rows, model), f32)] * 2,
        share(2 * model - model // 2 * len(begun) // 2),
        LIM,
    )
    past = [(hidden, back_pre, x_cols, c_cols)]
    if paired:
        swapped = [cross(parts[1], swap(1)), cross(parts[3], swap(1))]
    for step in range(1, n_dp):
        done = past[-1][0]
        near = near_of(chunk)
        blocks = near + rest_of(opposite, done)
        if step < n_dp - 1:
            chunk = after(coming, done)
            opposite = opposite_of(chunk)
            if step < n_dp - 2:
                coming = onward(chunk)
            past.append(
                run_kernel(
                    functools.partial(away_kernel, counts_of(blocks), len(held)), "away_group", meta, size, units,
                    flat(blocks) + held, kept_outs, full, share(model), LIM,
                )
            )
    begun = []
    if paired:
        begun = run_kernel(
            functools.partial(begin_kernel, counts_of(near), len(held)), "begin_last", meta, size, units,
            flat(near) + held, partial_outs, half, share(model // 2), LIM,
        )
    last_size = unit_block(units, 256)
    everyone = rows * n_dp
    grad_in, grad_out = run_kernel(
        functools.partial(last_kernel, counts_of(blocks), len(held), len(begun), len(past)), "last_group",
        meta, last_size, units,
        flat(blocks) + held + [(array, "cols") for array in begun]
        + [pair for kept in past for pair in zip(kept, ("cols", "cols", "whole", "whole"))],
        [((own, units), f32, "cols"), ((units, own), f32, "rows")],
        half + [
            pltpu.VMEM((rows, own), bf16),
            pltpu.VMEM((own, everyone), bf16),
            pltpu.VMEM((everyone, own), bf16),
            pltpu.VMEM((everyone, last_size), bf16),
            pltpu.VMEM((everyone, last_size), bf16),
        ],
        share(model - model // 2 * len(begun) // 2) + 4 * everyone * own * units,
        LIM,
    )
    if paired:
        far = (after(swapped[1], begun[0]).astype(f32) + parts[2].astype(f32)).astype(bf16)
        sums = [parts[0], swapped[0], cross(far, swap(2))]
    else:
        sums = [lax.psum_scatter(parts[0], "tp", scatter_dimension=1, tiled=True)]
    mixed, grad_patches = pl.pallas_call(
        functools.partial(restore_kernel, len(sums)), name="restore_rows",
        out_shape=[jax.ShapeDtypeStruct((rows, width), bf16)] * 2,
        compiler_params=small,
    )(ordering[None, :], *[in_hbm(after(array, grad_in)) for array in sums])
    return (mixed, grad_patches, grad_in, grad_out)


def solution(mesh):
    return jax.shard_map(
        shards,
        mesh=mesh,
        in_specs=(
            P(("rep", "dp"), "tp"),
            P(("rep", "dp")),
            P(None, "tp"),
            P("tp", None),
            P(("rep", "dp"), "tp"),
        ),
        out_specs=(
            P(("rep", "dp"), "tp"),
            P(("rep", "dp"), "tp"),
            P(("rep", "dp"), "tp"),
            P(("rep", "tp"), "dp"),
        ),
        check_vma=False,
    )
```

time: 969 us -> 137 us (0.14)
  waiting for transfers between devices: 693 us -> 9.22 us
  matrix products: 212 us -> 0 us
  Pallas kernels: 0 us -> 109 us
  other arithmetic: 24 us -> 1.32 us
  local copies, waits for them, and re-layouts: 18.1 us -> 3.34 us
  between operations: 14.4 us -> 0.77 us
  starting transfers between devices: 0.24 us -> 12.4 us
    reduce_scatter x4 -> x0, waiting for transfers between devices: 654 us -> none  [the longest x1 313 us: shards(): lax.psum_scatter(term_in.astype(jnp.bfloat16), 'dp', scatter_dimension=0,...]
    dot_general x18 -> x0, matrix products: 212 us -> none  [the longest x8 105 us: contract_cols(): lax.dot_general(left_side, right_side, (((1,), (1,)), ((), ())), preferre...]
    pallas_call x0 -> x8, Pallas kernels: none -> 109 us  [the longest x6 105 us: run_kernel(): pl.pallas_call(kernel, name=name, out_shape=[shape_of(*out) for out in ou...]
    all_gather x2 -> x0, waiting for transfers between devices: 37.2 us -> none  [the longest x1 21.9 us: shards(): lax.all_gather(cotangent, 'tp', axis=1, tiled=True)]
    gather x4 -> x0, local copies, waits for them, and re-layouts: 16.7 us -> none  [the longest x1 5.91 us: shards(): cot_sorted = jnp.take(cot_all, ordering, axis=0)]
    convert_element_type x7 -> x1, other arithmetic: 15.3 us -> 1.32 us  [shards(): (after(swapped[1], begun[0]).astype(f32) + parts[2].astype(f32)).astype(b...]
    ppermute x0 -> x18, starting transfers between devices: none -> 12.4 us  [the longest x15 9.1 us: shards(): cross = lambda array, pairs: lax.ppermute(array, 'tp', pairs)]
  transfers between devices with their start and end apart: 6 -> 18, of which waited for: 6 -> 5; matrix products, arithmetic and copies ran while one was open for 5% -> 1% of each run, Pallas kernels for 0% -> 77%
where the time goes in v2:
time: 137 us; the launch traced here: 136 us
  Pallas kernels  109 us (80%)
  starting transfers between devices  12.4 us (9%)
  waiting for transfers between devices  9.22 us (7%)
  local copies, waits for them, and re-layouts  3.34 us (2%)
    pallas_call x6, Pallas kernels, run_kernel(): pl.pallas_call(kernel, name=name, out_shape=[shape_of(*out) for out in ou...  105 us
    ppermute x15, starting transfers between devices, shards(): cross = lambda array, pairs: lax.ppermute(array, 'tp', pairs)  9.1 us
    ppermute x15, waiting for transfers between devices, shards(): cross = lambda array, pairs: lax.ppermute(array, 'tp', pairs)  7.49 us
    ppermute x3, starting transfers between devices, shards(): lax.ppermute(array, 'dp', [(rank, (rank + 1) % n_dp) for rank in range(n_...  3.28 us
    pallas_call x1, Pallas kernels, shards(): pl.pallas_call(functools.partial(restore_kernel, len(sums)), name='restor...  2.91 us
    unnamed x20, local copies, waits for them, and re-layouts  2.74 us
  transfers between devices with their start and end apart: 18, of which 5 were waited for; matrix products, arithmetic and copies ran while one was open for 1% of the time, Pallas kernels for 77%

profile of v2, /device:TPU:0, one launch (start us, length us, event | category | flops | bytes accessed | tf_op | source)
XLA Modules:
  0.0 136.0 jit_solution(12423401135081421684)
XLA Ops:
  0.6 0.7 copy-done.1
  1.3 1.5 %sort_rows.1.refs_0_ = bf16[512,768]{1,0:T(8,128)(2,1)S(1)} custom-call(s32[1,256]{1,0:T(1,128)S(1)} %bitcast.9, bf16[256,768]{1,0:T(8,128)(2,1)} %patches.1, bf16[256,768]{1,0:T(8,128)(2,1)} %cotangent.1), custom_call_target="tpu_custom_call" | custom-call | tf_op jit(solution)/shard_map/sort_rows/pallas_call | solution.py:359
  2.9 0.5 collective-permute-start
  3.4 2.6 %collective-permute-start.1 = (bf16[512,768]{1,0:T(8,128)(2,1)S(1)}, bf16[512,768]{1,0:T(8,128)(2,1)S(1)}, u32[]{:S(2)}, u32[]{:S(2)}) collective-permute-start(bf16[512,768]{1,0:T(8,128)(2,1)S(1)} %sort_rows.1.refs_0_), channel_id=1, source_target_pairs={{0,8},{4,12},{8,0},{12,4},{1,9},{5,13},{9,1},{13,5},{2,10},{6,14},... | collective-permute-start | bytes 2359304 | tf_op jit(solution)/shard_map/ppermute | solution.py:324
  6.0 1.6 %collective-permute-start.3 = (bf16[512,768]{1,0:T(8,128)(2,1)S(1)}, bf16[512,768]{1,0:T(8,128)(2,1)S(1)}, u32[]{:S(2)}, u32[]{:S(2)}) collective-permute-start(bf16[512,768]{1,0:T(8,128)(2,1)S(1)} %sort_rows.1.refs_0_), channel_id=1, source_target_pairs={{0,1},{1,2},{2,3},{3,0},{4,5},{5,6},{6,7},{7,4},{8,9},{9,10},{10,1... | collective-permute-start | bytes 2359304 | tf_op jit(solution)/shard_map/ppermute | solution.py:325
  7.5 0.6 stack.35.meta
  8.1 17.6 %open_group.1 = (bf16[6144,3072]{1,0:T(8,128)(2,1)S(1)}, f32[256,3072]{1,0:T(8,128)}, f32[256,3072]{1,0:T(8,128)}) custom-call(s32[9]{0:T(128)} %stack.35.meta, bf16[512,768]{1,0:T(8,128)(2,1)} %copy-done, bf16[512,768]{1,0:T(8,128)(2,1)} %collective-permute-done.refs_1_, bf16[3072,3072]{1,0:T(8,128)(2,1)} %refs_2_.1, bf16[3072,3072]{1,0:T(8,128)(2,1)} %refs_3_.1), custom_call_target="tpu_custom_call" | custom-call | flops 4831838208 | bytes 45613056 | tf_op jit(solution)/shard_map/open_group/pallas_call | solution.py:299
  25.8 1.6 %collective-permute-done.3.refs_0_ = bf16[512,768]{1,0:T(8,128)(2,1)S(1)} collective-permute-done((bf16[512,768]{1,0:T(8,128)(2,1)S(1)}, bf16[512,768]{1,0:T(8,128)(2,1)S(1)}, u32[]{:S(2)}, u32[]{:S(2)}) %collective-permute-start.3) | collective-permute-done | bytes 786464 | tf_op jit(solution)/shard_map/ppermute | solution.py:325
  28.1 23.2 %home_group.1 = (bf16[512,768]{1,0:T(8,128)(2,1)}, bf16[512,768]{1,0:T(8,128)(2,1)}, bf16[512,768]{1,0:T(8,128)(2,1)}, bf16[512,768]{1,0:T(8,128)(2,1)}, bf16[25...) custom-call(s32[9]{0:T(128)} %stack.35.meta, ...), custom_call_target="tpu_custom_call" | custom-call | flops 14495514624 | bytes 14942208 | tf_op jit(solution)/shard_map/home_group/pallas_call | solution.py:299
  51.8 1.5 %collective-permute-start.5 = (bf16[512,768]{1,0:T(8,128)(2,1)S(1)}, bf16[512,768]{1,0:T(8,128)(2,1)S(1)}, u32[]{:S(2)}, u32[]{:S(2)}) collective-permute-start(bf16[512,768]{1,0:T(8,128)(2,1)S(1)} %collective-permute-done.4.refs_0_), channel_id=1, source_target_pairs={{0,1},{1,2},{2,3},{3,0},{4,5},{5,6},{6,7},{7,4},{8,9},{9,10},{10,1... | collective-permute-start | bytes 2359304 | tf_op jit(solution)/shard_map/ppermute | solution.py:325
  53.3 1.3 collective-permute-start.12
  54.6 14.6 %away_group.2 = (bf16[256,3072]{1,0:T(8,128)(2,1)}, bf16[256,3072]{1,0:T(8,128)(2,1)}, bf16[256,768]{1,0:T(8,128)(2,1)}, bf16[256,768]{1,0:T(8,128)(2,1)}) custom-call(s32[9]{0:T(128)} %stack.35.meta, bf16[512,768]{1,0:T(8,128)(2,1)} %copy-done.8, bf16[512,768]{1,0:T(8,128)(2,1)} %collective-permute-done.6.refs_1_, ...), custom_call_target="tpu_custom_call" | custom-call | flops 9663676416 | bytes 5505024 | tf_op jit(solution)/shard_map/away_group/pallas_call | solution.py:299
  69.3 3.4 %collective-permute-done.12.refs_2_ = bf16[512,768]{1,0:T(8,128)(2,1)S(1)} collective-permute-done((bf16[512,768]{1,0:T(8,128)(2,1)S(1)}, bf16[512,768]{1,0:T(8,128)(2,1)S(1)}, u32[]{:S(2)}, u32[]{:S(2)}) %collective-permute-start.12) | collective-permute-done | bytes 786464 | tf_op jit(solution)/shard_map/ppermute | solution.py:324
  73.3 1.3 collective-permute-start.10
  74.6 1.4 %collective-permute-done.13.refs_3_ = bf16[512,768]{1,0:T(8,128)(2,1)S(1)} collective-permute-done((bf16[512,768]{1,0:T(8,128)(2,1)S(1)}, bf16[512,768]{1,0:T(8,128)(2,1)S(1)}, u32[]{:S(2)}, u32[]{:S(2)}) %collective-permute-start.13) | collective-permute-done | bytes 786464 | tf_op jit(solution)/shard_map/ppermute | solution.py:324
  76.1 14.6 %away_group.3 = (bf16[256,3072]{1,0:T(8,128)(2,1)}, bf16[256,3072]{1,0:T(8,128)(2,1)}, bf16[256,768]{1,0:T(8,128)(2,1)}, bf16[256,768]{1,0:T(8,128)(2,1)}) custom-call(s32[9]{0:T(128)} %stack.35.meta, bf16[512,768]{1,0:T(8,128)(2,1)} %copy-done.9, bf16[512,768]{1,0:T(8,128)(2,1)} %collective-permute-done.11.refs_1_, ...), custom_call_target="tpu_custom_call" | custom-call | flops 9663676416 | bytes 5505024 | tf_op jit(solution)/shard_map/away_group/pallas_call | solution.py:299
  90.7 2.6 %collective-permute-done.10.refs_2_ = bf16[512,768]{1,0:T(8,128)(2,1)S(1)} collective-permute-done((bf16[512,768]{1,0:T(8,128)(2,1)S(1)}, bf16[512,768]{1,0:T(8,128)(2,1)S(1)}, u32[]{:S(2)}, u32[]{:S(2)}) %collective-permute-start.10) | collective-permute-done | bytes 786464 | tf_op jit(solution)/shard_map/ppermute | solution.py:324
  93.8 0.9 copy-done.4
  94.7 9.0 %begin_last.1 = (f32[256,3072]{1,0:T(8,128)}, f32[256,3072]{1,0:T(8,128)}) custom-call(s32[9]{0:T(128)} %stack.35.meta, bf16[512,768]{1,0:T(8,128)(2,1)} %copy-done.3, bf16[512,768]{1,0:T(8,128)(2,1)} %copy-done.4, bf16[6144,3072]{1,0:T(8,128)(2,1)S(1)} %get-tuple-element.42.refs_4_.refs_2_), custom_call_target="tpu_custom_call" | custom-call | flops 4831838208 | bytes 7864320 | tf_op jit(solution)/shard_map/begin_last/pallas_call | solution.py:299
  103.7 1.3 add_convert_fusion
  105.0 1.4 %collective-permute-start.17 = (bf16[512,768]{1,0:T(8,128)(2,1)S(1)}, bf16[512,768]{1,0:T(8,128)(2,1)S(1)}, u32[]{:S(2)}, u32[]{:S(2)}) collective-permute-start(bf16[512,768]{1,0:T(8,128)(2,1)S(1)} %add_convert_fusion), channel_id=1, source_target_pairs={{0,8},{4,12},{8,0},{12,4},{1,9},{5,13},{9,1},{13,5},{2,10},{6,14},... | collective-permute-start | bytes 2359304 | tf_op jit(solution)/shard_map/ppermute | solution.py:324
  106.4 25.5 %last_group.1 = (f32[768,3072]{1,0:T(8,128)}, f32[3072,768]{1,0:T(8,128)}) custom-call(s32[9]{0:T(128)} %stack.35.meta, bf16[512,768]{1,0:T(8,128)(2,1)} %copy-done.3, bf16[512,768]{1,0:T(8,128)(2,1)} %copy-done.4, bf16[512,768]{1,0:T(8,128)(2,1)S(1)} %collective-permute-done.10.refs_2_, bf16[512,768]{1,0:T(8,128)(2,1)S(1)} %collective-permute-done.14.refs_3_, ...), custom_call_target="tpu_custom_call" | custom-call | flops 14495514624 | bytes 38535168 | tf_op jit(solution)/shard_map/last_group/pallas_call | solution.py:299
  131.9 0.9 copy-done.7
  133.1 2.9 %restore_rows.1 = (bf16[256,768]{1,0:T(8,128)(2,1)}, bf16[256,768]{1,0:T(8,128)(2,1)}) custom-call(s32[1,256]{1,0:T(1,128)S(1)} %bitcast.10, bf16[512,768]{1,0:T(8,128)(2,1)} %get-tuple-element.66.refs_0_, bf16[512,768]{1,0:T(8,128)(2,1)} %copy-done.6, bf16[512,768]{1,0:T(8,128)(2,1)} %copy-done.7), custom_call_target="tpu_custom_call" | custom-call | tf_op jit(solution)/shard_map/restore_rows/pallas_call | solution.py:437
  (42 shorter events, 2.6 us)
Async XLA Ops:
  2.8 5.3 %copy-start = (bf16[512,768]{1,0:T(8,128)(2,1)}, bf16[512,768]{1,0:T(8,128)(2,1)S(1)}, u32[]{:S(2)}) copy-start(bf16[512,768]{1,0:T(8,128)(2,1)S(1)} %sort_rows.1.refs_0_) | copy-start | bytes 2359300
  2.9 5.3 %collective-permute-start = (bf16[512,768]{1,0:T(8,128)(2,1)S(1)}, bf16[512,768]{1,0:T(8,128)(2,1)}, u32[]{:S(2)}, u32[]{:S(2)}) collective-permute-start(bf16[512,768]{1,0:T(8,128)(2,1)S(1)} %sort_rows.1.refs_0_), channel_id=1, source_target_pairs={{0,4},{4,0},{8,12},{12,8},{1,5},{5,1},{9,13},{13,9},{2,6},{6,2},{1... | collective-permute-start | bytes 2359304 | tf_op jit(solution)/shard_map/ppermute | solution.py:324
  3.4 22.3 %collective-permute-start.1 = (bf16[512,768]{1,0:T(8,128)(2,1)S(1)}, bf16[512,768]{1,0:T(8,128)(2,1)S(1)}, u32[]{:S(2)}, u32[]{:S(2)}) collective-permute-start(bf16[512,768]{1,0:T(8,128)(2,1)S(1)} %sort_rows.1.refs_0_), channel_id=1, source_target_pairs={{0,8},{4,12},{8,0},{12,4},{1,9},{5,13},{9,1},{13,5},{2,10},{6,14},... | collective-permute-start | bytes 2359304 | tf_op jit(solution)/shard_map/ppermute | solution.py:324
  6.0 21.5 %collective-permute-start.3 = (bf16[512,768]{1,0:T(8,128)(2,1)S(1)}, bf16[512,768]{1,0:T(8,128)(2,1)S(1)}, u32[]{:S(2)}, u32[]{:S(2)}) collective-permute-start(bf16[512,768]{1,0:T(8,128)(2,1)S(1)} %sort_rows.1.refs_0_), channel_id=1, source_target_pairs={{0,1},{1,2},{2,3},{3,0},{4,5},{5,6},{6,7},{7,4},{8,9},{9,10},{10,1... | collective-permute-start | bytes 2359304 | tf_op jit(solution)/shard_map/ppermute | solution.py:325
  25.7 2.4 %collective-permute-start.2 = (bf16[512,768]{1,0:T(8,128)(2,1)S(1)}, bf16[512,768]{1,0:T(8,128)(2,1)S(1)}, u32[]{:S(2)}, u32[]{:S(2)}) collective-permute-start(bf16[512,768]{1,0:T(8,128)(2,1)S(1)} %collective-permute-done.1.refs_2_), channel_id=1, source_target_pairs={{0,4},{4,0},{8,12},{12,8},{1,5},{5,1},{9,13},{13,9},{2,6},{6,2},{1... | collective-permute-start | bytes 2359304 | tf_op jit(solution)/shard_map/ppermute | solution.py:324
  27.4 23.9 %copy-start.8 = (bf16[512,768]{1,0:T(8,128)(2,1)}, bf16[512,768]{1,0:T(8,128)(2,1)S(1)}, u32[]{:S(2)}) copy-start(bf16[512,768]{1,0:T(8,128)(2,1)S(1)} %collective-permute-done.3.refs_0_) | copy-start | bytes 2359300
  27.4 23.9 %collective-permute-start.7 = (bf16[512,768]{1,0:T(8,128)(2,1)S(1)}, bf16[512,768]{1,0:T(8,128)(2,1)S(1)}, u32[]{:S(2)}, u32[]{:S(2)}) collective-permute-start(bf16[512,768]{1,0:T(8,128)(2,1)S(1)} %collective-permute-done.3.refs_0_), channel_id=1, source_target_pairs={{0,8},{4,12},{8,0},{12,4},{1,9},{5,13},{9,1},{13,5},{2,10},{6,14},... | collective-permute-start | bytes 2359304 | tf_op jit(solution)/shard_map/ppermute | solution.py:324
  27.9 26.7 %collective-permute-start.6 = (bf16[512,768]{1,0:T(8,128)(2,1)S(1)}, bf16[512,768]{1,0:T(8,128)(2,1)}, u32[]{:S(2)}, u32[]{:S(2)}) collective-permute-start(bf16[512,768]{1,0:T(8,128)(2,1)S(1)} %collective-permute-done.3.refs_0_), channel_id=1, source_target_pairs={{0,4},{4,0},{8,12},{12,8},{1,5},{5,1},{9,13},{13,9},{2,6},{6,2},{1... | collective-permute-start | bytes 2359304 | tf_op jit(solution)/shard_map/ppermute | solution.py:324
  27.9 23.8 %collective-permute-start.4 = (bf16[512,768]{1,0:T(8,128)(2,1)S(1)}, bf16[512,768]{1,0:T(8,128)(2,1)S(1)}, u32[]{:S(2)}, u32[]{:S(2)}) collective-permute-start(bf16[512,768]{1,0:T(8,128)(2,1)S(1)} %collective-permute-done.3.refs_0_), channel_id=1, source_target_pairs={{0,1},{1,2},{2,3},{3,0},{4,5},{5,6},{6,7},{7,4},{8,9},{9,10},{10,1... | collective-permute-start | bytes 2359304 | tf_op jit(solution)/shard_map/ppermute | solution.py:325
  51.4 3.2 %collective-permute-start.8 = (bf16[512,768]{1,0:T(8,128)(2,1)S(1)}, bf16[512,768]{1,0:T(8,128)(2,1)S(1)}, u32[]{:S(2)}, u32[]{:S(2)}) collective-permute-start(bf16[512,768]{1,0:T(8,128)(2,1)S(1)} %collective-permute-done.7.refs_2_), channel_id=1, source_target_pairs={{0,4},{4,0},{8,12},{12,8},{1,5},{5,1},{9,13},{13,9},{2,6},{6,2},{1... | collective-permute-start | bytes 2359304 | tf_op jit(solution)/shard_map/ppermute | solution.py:324
  51.8 17.5 %copy-start.9 = (bf16[512,768]{1,0:T(8,128)(2,1)}, bf16[512,768]{1,0:T(8,128)(2,1)S(1)}, u32[]{:S(2)}) copy-start(bf16[512,768]{1,0:T(8,128)(2,1)S(1)} %collective-permute-done.4.refs_0_) | copy-start | bytes 2359300
  51.8 21.5 %collective-permute-start.5 = (bf16[512,768]{1,0:T(8,128)(2,1)S(1)}, bf16[512,768]{1,0:T(8,128)(2,1)S(1)}, u32[]{:S(2)}, u32[]{:S(2)}) collective-permute-start(bf16[512,768]{1,0:T(8,128)(2,1)S(1)} %collective-permute-done.4.refs_0_), channel_id=1, source_target_pairs={{0,1},{1,2},{2,3},{3,0},{4,5},{5,6},{6,7},{7,4},{8,9},{9,10},{10,1... | collective-permute-start | bytes 2359304 | tf_op jit(solution)/shard_map/ppermute | solution.py:325
  53.3 19.4 %collective-permute-start.12 = (bf16[512,768]{1,0:T(8,128)(2,1)S(1)}, bf16[512,768]{1,0:T(8,128)(2,1)S(1)}, u32[]{:S(2)}, u32[]{:S(2)}) collective-permute-start(bf16[512,768]{1,0:T(8,128)(2,1)S(1)} %collective-permute-done.4.refs_0_), channel_id=1, source_target_pairs={{0,8},{4,12},{8,0},{12,4},{1,9},{5,13},{9,1},{13,5},{2,10},{6,14},... | collective-permute-start | bytes 2359304 | tf_op jit(solution)/shard_map/ppermute | solution.py:324
  54.6 20.0 %collective-permute-start.11 = (bf16[512,768]{1,0:T(8,128)(2,1)S(1)}, bf16[512,768]{1,0:T(8,128)(2,1)}, u32[]{:S(2)}, u32[]{:S(2)}) collective-permute-start(bf16[512,768]{1,0:T(8,128)(2,1)S(1)} %collective-permute-done.4.refs_0_), channel_id=1, source_target_pairs={{0,4},{4,0},{8,12},{12,8},{1,5},{5,1},{9,13},{13,9},{2,6},{6,2},{1... | collective-permute-start | bytes 2359304 | tf_op jit(solution)/shard_map/ppermute | solution.py:324
  72.7 3.4 %collective-permute-start.13 = (bf16[512,768]{1,0:T(8,128)(2,1)S(1)}, bf16[512,768]{1,0:T(8,128)(2,1)S(1)}, u32[]{:S(2)}, u32[]{:S(2)}) collective-permute-start(bf16[512,768]{1,0:T(8,128)(2,1)S(1)} %collective-permute-done.12.refs_2_), channel_id=1, source_target_pairs={{0,4},{4,0},{8,12},{12,8},{1,5},{5,1},{9,13},{13,9},{2,6},{6,2},{1... | collective-permute-start | bytes 2359304 | tf_op jit(solution)/shard_map/ppermute | solution.py:324
  72.7 31.0 %collective-permute-start.16 = (bf16[512,768]{1,0:T(8,128)(2,1)}, bf16[512,768]{1,0:T(8,128)(2,1)}, u32[]{:S(2)}, u32[]{:S(2)}) collective-permute-start(bf16[512,768]{1,0:T(8,128)(2,1)} %get-tuple-element.69), channel_id=1, source_target_pairs={{0,4},{4,0},{8,12},{12,8},{1,5},{5,1},{9,13},{13,9},{2,6},{6,2},{1... | collective-permute-start | bytes 2359304 | tf_op jit(solution)/shard_map/ppermute | solution.py:324
  73.3 17.4 %copy-start.3 = (bf16[512,768]{1,0:T(8,128)(2,1)}, bf16[512,768]{1,0:T(8,128)(2,1)S(1)}, u32[]{:S(2)}) copy-start(bf16[512,768]{1,0:T(8,128)(2,1)S(1)} %collective-permute-done.5.refs_0_) | copy-start | bytes 2359300
  73.3 20.5 %collective-permute-start.9 = (bf16[512,768]{1,0:T(8,128)(2,1)S(1)}, bf16[512,768]{1,0:T(8,128)(2,1)S(1)}, u32[]{:S(2)}, u32[]{:S(2)}) collective-permute-start(bf16[512,768]{1,0:T(8,128)(2,1)S(1)} %collective-permute-done.5.refs_0_), channel_id=1, source_target_pairs={{0,4},{4,0},{8,12},{12,8},{1,5},{5,1},{9,13},{13,9},{2,6},{6,2},{1... | collective-permute-start | bytes 2359304 | tf_op jit(solution)/shard_map/ppermute | solution.py:324
  73.3 20.0 %collective-permute-start.10 = (bf16[512,768]{1,0:T(8,128)(2,1)S(1)}, bf16[512,768]{1,0:T(8,128)(2,1)S(1)}, u32[]{:S(2)}, u32[]{:S(2)}) collective-permute-start(bf16[512,768]{1,0:T(8,128)(2,1)S(1)} %collective-permute-done.5.refs_0_), channel_id=1, source_target_pairs={{0,8},{4,12},{8,0},{12,4},{1,9},{5,13},{9,1},{13,5},{2,10},{6,14},... | collective-permute-start | bytes 2359304 | tf_op jit(solution)/shard_map/ppermute | solution.py:324
  93.3 13.1 %collective-permute-start.14 = (bf16[512,768]{1,0:T(8,128)(2,1)S(1)}, bf16[512,768]{1,0:T(8,128)(2,1)S(1)}, u32[]{:S(2)}, u32[]{:S(2)}) collective-permute-start(bf16[512,768]{1,0:T(8,128)(2,1)S(1)} %collective-permute-done.10.refs_2_), channel_id=1, source_target_pairs={{0,4},{4,0},{8,12},{12,8},{1,5},{5,1},{9,13},{13,9},{2,6},{6,2},{1... | collective-permute-start | bytes 2359304 | tf_op jit(solution)/shard_map/ppermute | solution.py:324
  93.3 10.4 %copy-start.5 = (bf16[512,768]{1,0:T(8,128)(2,1)S(1)}, bf16[512,768]{1,0:T(8,128)(2,1)}, u32[]{:S(2)}) copy-start(bf16[512,768]{1,0:T(8,128)(2,1)} %get-tuple-element.71) | copy-start | bytes 2359300
  93.3 38.6 %collective-permute-start.15 = (bf16[512,768]{1,0:T(8,128)(2,1)}, bf16[512,768]{1,0:T(8,128)(2,1)S(1)}, u32[]{:S(2)}, u32[]{:S(2)}) collective-permute-start(bf16[512,768]{1,0:T(8,128)(2,1)} %get-tuple-element.67), channel_id=1, source_target_pairs={{0,4},{4,0},{8,12},{12,8},{1,5},{5,1},{9,13},{13,9},{2,6},{6,2},{1... | collective-permute-start | bytes 2359304 | tf_op jit(solution)/shard_map/ppermute | solution.py:324
  105.0 26.9 %collective-permute-start.17 = (bf16[512,768]{1,0:T(8,128)(2,1)S(1)}, bf16[512,768]{1,0:T(8,128)(2,1)S(1)}, u32[]{:S(2)}, u32[]{:S(2)}) collective-permute-start(bf16[512,768]{1,0:T(8,128)(2,1)S(1)} %add_convert_fusion), channel_id=1, source_target_pairs={{0,8},{4,12},{8,0},{12,4},{1,9},{5,13},{9,1},{13,5},{2,10},{6,14},... | collective-permute-start | bytes 2359304 | tf_op jit(solution)/shard_map/ppermute | solution.py:324
  106.4 26.7 %copy-start.2 = (s32[256]{0:T(256)S(1)}, s32[256]{0:T(256)}, u32[]{:S(2)}) copy-start(s32[256]{0:T(256)} %param.6) | copy-start | bytes 3076
  (4 other events, 3.6 us)

commit v3 on v2

--- a/solution.py
+++ b/solution.py
@@ -166,17 +166,6 @@
     pre_out[...], back_out[...] = products(x_full, c_full, meta[3], views([weights]), units)
 
 
-def begin_kernel(counts, held, meta, *refs):
-    blocks, refs = split_refs(refs, counts)
-    weights, (pre_out, back_out, x_full, c_full) = refs[:held], refs[held:]
-
-    @pl.when(pl.program_id(0) == 0)
-    def _():
-        fill(meta, blocks, x_full, c_full, meta[3])
-
-    pre_out[...], back_out[...] = products(x_full, c_full, meta[3], views(weights), pre_out.shape[1])
-
-
 def home_kernel(counts, held, begun, meta, *refs):
     blocks, refs = split_refs(refs, counts)
     (weights, begun, parts), refs = split_refs(refs, (held, begun, len(counts)))
@@ -246,9 +235,9 @@
     hidden_out[...], back_out[...] = late_products(meta, x_full, c_full, (), weights, hidden_out.shape[1])
 
 
-def last_kernel(counts, held, begun, others, meta, *refs):
+def last_kernel(counts, held, others, meta, *refs):
     blocks, refs = split_refs(refs, counts)
-    (weights, begun, *past), refs = split_refs(refs, (held, begun) + (4,) * others)
+    (weights, *past), refs = split_refs(refs, (held,) + (4,) * others)
     grad_in, grad_out, x_full, c_full, x_cols, x_turned, c_all, hidden_all, back_all = refs
     rows = x_full.shape[0]
     own = pl.ds(others * rows, rows)
@@ -258,11 +247,11 @@
         for spot in range(others):
             x_turned[:, pl.ds(spot * rows, rows)] = past[spot][2][...].T
             c_all[pl.ds(spot * rows, rows), :] = past[spot][3][...]
-        fill_late(meta, begun, blocks, x_full, c_full)
+        fill(meta, blocks, x_full, c_full)
         own_columns(meta, blocks, x_cols, c_all.at[own, :])
         x_turned[:, own] = x_cols[...].T
 
-    hidden, back_pre = late_products(meta, x_full, c_full, begun, weights, hidden_all.shape[1])
+    hidden, back_pre = late_products(meta, x_full, c_full, (), weights, hidden_all.shape[1])
     for spot in range(others):
         hidden_all[pl.ds(spot * rows, rows), :] = past[spot][0][...]
         back_all[pl.ds(spot * rows, rows), :] = past[spot][1][...]
@@ -273,7 +262,7 @@
 
 
 def unit_block(units, most):
-    for size in (768, 512, 384, 256, 128):
+    for size in (1536, 768, 512, 384, 256, 128):
         if size <= most and units % size == 0:
             return size
     return units
@@ -308,7 +297,7 @@
             scratch_shapes=scratch,
         ),
         compiler_params=pltpu.CompilerParams(dimension_semantics=("arbitrary",), vmem_limit_bytes=limit * MIB),
-        cost_estimate=pl.CostEstimate(flops=flops, bytes_accessed=moved, transcendentals=0),
+        cost_estimate=pl.CostEstimate(flops=flops // 16, bytes_accessed=moved // 16, transcendentals=0),
     )(meta, *[resident(*pair) for pair in inputs])
 
 
@@ -323,6 +312,8 @@
     swap = lambda bits: [(rank, rank ^ bits) for rank in range(n_tp)]
     cross = lambda array, pairs: lax.ppermute(array, "tp", pairs)
     onward = lambda array: lax.ppermute(array, "dp", [(rank, (rank + 1) % n_dp) for rank in range(n_dp)])
+    back = lambda array: lax.ppermute(array, "dp", [(rank, (rank - 1) % n_dp) for rank in range(n_dp)])
+    turned = paired and n_dp > 3
     after = lambda array, done: lax.optimization_barrier((array, done))[0]
 
     def near_of(chunk):
@@ -331,13 +322,13 @@
         return [[chunk], [cross(chunk, swap(1))]]
 
     def opposite_of(chunk):
-        return cross(chunk, swap(2)) if paired else None
+        return [cross(chunk, swap(2))] if paired else []
 
     def rest_of(opposite, done):
         if not paired:
             return []
-        opposite = after(opposite, done)
-        return [[opposite], [cross(opposite, swap(1))]]
+        opposite = [after(piece, done) for piece in opposite]
+        return [opposite, [cross(piece, swap(1)) for piece in opposite]]
 
     offsets = [tp_rank ^ spot for spot in range(4)] if paired else [0]
     pair = tp_rank // 2 * 2
@@ -345,7 +336,7 @@
         [tp_rank * units, jnp.int32(units * n_tp), dp_rank, pair * width, (pair ^ 2) * width]
         + [jnp.int32(offset * width) for offset in offsets]
     ).astype(jnp.int32)
-    size = unit_block(units, 512)
+    size, away_size = unit_block(units, 512), unit_block(units, 1536)
     flat = lambda blocks: [(piece, "vmem" if spot >= 2 else "whole") for spot, pieces in enumerate(blocks) for piece in pieces]
     counts_of = lambda blocks: tuple(len(pieces) for pieces in blocks)
     kept_outs = [((rows, units), bf16, "cols")] * 2 + [((rows, own), bf16, "whole")] * 2
@@ -362,6 +353,7 @@
 
     near = near_of(chunk)
     opposite = opposite_of(chunk)
+    own_opposite = opposite[0] if paired else None
     coming = onward(chunk)
     if paired:
         weights, *begun = run_kernel(
@@ -388,49 +380,45 @@
         LIM,
     )
     past = [(hidden, back_pre, x_cols, c_cols)]
-    if paired:
-        swapped = [cross(parts[1], swap(1)), cross(parts[3], swap(1))]
     for step in range(1, n_dp):
         done = past[-1][0]
         near = near_of(chunk)
         blocks = near + rest_of(opposite, done)
         if step < n_dp - 1:
             chunk = after(coming, done)
-            opposite = opposite_of(chunk)
-            if step < n_dp - 2:
+            if not turned or step < n_dp - 2:
+                opposite = opposite_of(chunk)
+            else:
+                opposite = far_coming
+            if turned and step == n_dp - 3:
+                coming, far_coming = onward(chunk), [back(after(own_opposite, done))]
+            elif step < n_dp - 2:
                 coming = onward(chunk)
             past.append(
                 run_kernel(
-                    functools.partial(away_kernel, counts_of(blocks), len(held)), "away_group", meta, size, units,
+                    functools.partial(away_kernel, counts_of(blocks), len(held)), "away_group", meta, away_size, units,
                     flat(blocks) + held, kept_outs, full, share(model), LIM,
                 )
             )
-    begun = []
-    if paired:
-        begun = run_kernel(
-            functools.partial(begin_kernel, counts_of(near), len(held)), "begin_last", meta, size, units,
-            flat(near) + held, partial_outs, half, share(model // 2), LIM,
-        )
-    last_size = unit_block(units, 256)
     everyone = rows * n_dp
     grad_in, grad_out = run_kernel(
-        functools.partial(last_kernel, counts_of(blocks), len(held), len(begun), len(past)), "last_group",
-        meta, last_size, units,
-        flat(blocks) + held + [(array, "cols") for array in begun]
-        + [pair for kept in past for pair in zip(kept, ("cols", "cols", "whole", "whole"))],
+        functools.partial(last_kernel, counts_of(blocks), len(held), len(past)), "last_group",
+        meta, size, units,
+        flat(blocks) + held + [pair for kept in past for pair in zip(kept, ("cols", "cols", "whole", "whole"))],
         [((own, units), f32, "cols"), ((units, own), f32, "rows")],
-        half + [
+        full + [
             pltpu.VMEM((rows, own), bf16),
             pltpu.VMEM((own, everyone), bf16),
             pltpu.VMEM((everyone, own), bf16),
-            pltpu.VMEM((everyone, last_size), bf16),
-            pltpu.VMEM((everyone, last_size), bf16),
+            pltpu.VMEM((everyone, size), bf16),
+            pltpu.VMEM((everyone, size), bf16),
         ],
-        share(model - model // 2 * len(begun) // 2) + 4 * everyone * own * units,
+        share(model) + 4 * everyone * own * units,
         LIM,
     )
     if paired:
-        far = (after(swapped[1], begun[0]).astype(f32) + parts[2].astype(f32)).astype(bf16)
+        swapped = [cross(after(part, past[-2][0]), swap(1)) for part in parts[1::2]]
+        far = (after(swapped[1], past[-1][0]).astype(f32) + parts[2].astype(f32)).astype(bf16)
         sums = [parts[0], swapped[0], cross(far, swap(2))]
     else:
         sums = [lax.psum_scatter(parts[0], "tp", scatter_dimension=1, tiled=True)]
@@ -438,7 +426,7 @@
         functools.partial(restore_kernel, len(sums)), name="restore_rows",
         out_shape=[jax.ShapeDtypeStruct((rows, width), bf16)] * 2,
         compiler_params=small,
-    )(ordering[None, :], *[in_hbm(after(array, grad_in)) for array in sums])
+    )(ordering[None, :], *[after(array, grad_in) for array in sums])
     return (mixed, grad_patches, grad_in, grad_out)
 
 

time: 137 us -> 126 us (0.920)
  Pallas kernels: 109 us -> 98.6 us
  waiting for transfers between devices: 9.22 us -> 6.33 us
  starting transfers between devices: 12.4 us -> 14.4 us
    pallas_call x6 -> x5, Pallas kernels: 105 us -> 95.8 us  [run_kernel(): pl.pallas_call(kernel, name=name, out_shape=[shape_of(*out) for out in ou...]
    ppermute x15 -> x14, waiting for transfers between devices: 7.49 us -> 2.38 us  [shards(): cross = lambda array, pairs: lax.ppermute(array, 'tp', pairs)]
    ppermute x0 -> x1, waiting for transfers between devices: none -> 2.94 us  [shards(): lax.ppermute(array, 'dp', [(rank, (rank - 1) % n_dp) for rank in range(n_...]
    ppermute x0 -> x1, starting transfers between devices: none -> 2.81 us  [shards(): lax.ppermute(array, 'dp', [(rank, (rank - 1) % n_dp) for rank in range(n_...]
    ppermute x15 -> x14, starting transfers between devices: 9.1 us -> 7.46 us  [shards(): cross = lambda array, pairs: lax.ppermute(array, 'tp', pairs)]
    pallas_call x1, Pallas kernels: 2.91 us -> 1.3 us  [shards(): pl.pallas_call(functools.partial(restore_kernel, len(sums)), name='restor...]
    unnamed x20 -> x16, local copies, waits for them, and re-layouts: 2.74 us -> 2.47 us
  transfers between devices with their start and end apart: 18 -> 18, of which waited for: 5 -> 5; matrix products, arithmetic and copies ran while one was open for 1% -> 2% of each run, Pallas kernels for 77% -> 76%
where the time goes in v3:
time: 126 us
  Pallas kernels  98.6 us (78%)
  starting transfers between devices  14.4 us (11%)
  waiting for transfers between devices  6.33 us (5%)
  local copies, waits for them, and re-layouts  3.15 us (2%)
  other arithmetic  2.2 us (2%)
    pallas_call x5, Pallas kernels, run_kernel(): pl.pallas_call(kernel, name=name, out_shape=[shape_of(*out) for out in ou...  95.8 us
    ppermute x14, starting transfers between devices, shards(): cross = lambda array, pairs: lax.ppermute(array, 'tp', pairs)  7.46 us
    ppermute x3, starting transfers between devices, shards(): lax.ppermute(array, 'dp', [(rank, (rank + 1) % n_dp) for rank in range(n_...  4.16 us
    ppermute x1, waiting for transfers between devices, shards(): lax.ppermute(array, 'dp', [(rank, (rank - 1) % n_dp) for rank in range(n_...  2.94 us
    ppermute x1, starting transfers between devices, shards(): lax.ppermute(array, 'dp', [(rank, (rank - 1) % n_dp) for rank in range(n_...  2.81 us
  transfers between devices with their start and end apart: 18, of which 5 were waited for; matrix products, arithmetic and copies ran while one was open for 2% of the time, Pallas kernels for 76%

profile of v3, /device:TPU:0, one launch (start us, length us, event | category | flops | bytes accessed | tf_op | source)
XLA Modules:
  0.0 125.5 jit_solution(8837958133781629393)
XLA Ops:
  0.6 0.7 copy-done.2
  1.3 1.5 %sort_rows.1.refs_0_ = bf16[512,768]{1,0:T(8,128)(2,1)S(1)} custom-call(s32[1,256]{1,0:T(1,128)S(1)} %bitcast.9, bf16[256,768]{1,0:T(8,128)(2,1)} %patches.1, bf16[256,768]{1,0:T(8,128)(2,1)} %cotangent.1), custom_call_target="tpu_custom_call" | custom-call | tf_op jit(solution)/shard_map/sort_rows/pallas_call | solution.py:350
  2.9 0.5 collective-permute-start
  3.4 2.6 %collective-permute-start.1 = (bf16[512,768]{1,0:T(8,128)(2,1)S(1)}, bf16[512,768]{1,0:T(8,128)(2,1)S(1)}, u32[]{:S(2)}, u32[]{:S(2)}) collective-permute-start(bf16[512,768]{1,0:T(8,128)(2,1)S(1)} %sort_rows.1.refs_0_), channel_id=1, source_target_pairs={{0,8},{4,12},{8,0},{12,4},{1,9},{5,13},{9,1},{13,5},{2,10},{6,14},... | collective-permute-start | bytes 2359304 | tf_op jit(solution)/shard_map/ppermute | solution.py:313
  6.0 1.6 %collective-permute-start.3 = (bf16[512,768]{1,0:T(8,128)(2,1)S(1)}, bf16[512,768]{1,0:T(8,128)(2,1)S(1)}, u32[]{:S(2)}, u32[]{:S(2)}) collective-permute-start(bf16[512,768]{1,0:T(8,128)(2,1)S(1)} %sort_rows.1.refs_0_), channel_id=1, source_target_pairs={{0,1},{1,2},{2,3},{3,0},{4,5},{5,6},{6,7},{7,4},{8,9},{9,10},{10,1... | collective-permute-start | bytes 2359304 | tf_op jit(solution)/shard_map/ppermute | solution.py:314
  7.5 0.7 stack.35.meta
  8.2 0.9 copy-done.4
  9.1 17.6 %open_group.1 = (bf16[6144,3072]{1,0:T(8,128)(2,1)S(1)}, f32[256,3072]{1,0:T(8,128)}, f32[256,3072]{1,0:T(8,128)}) custom-call(s32[9]{0:T(128)} %stack.35.meta, bf16[512,768]{1,0:T(8,128)(2,1)} %copy-done, bf16[512,768]{1,0:T(8,128)(2,1)} %copy-done.4, bf16[3072,3072]{1,0:T(8,128)(2,1)} %refs_2_.1, bf16[3072,3072]{1,0:T(8,128)(2,1)} %refs_3_.1), custom_call_target="tpu_custom_call" | custom-call | flops 301989888 | bytes 2850816 | tf_op jit(solution)/shard_map/open_group/pallas_call | solution.py:288
  26.8 0.7 collective-permute-done.3.refs_0_
  27.9 1.0 collective-permute-start.4
  29.1 23.2 %home_group.1 = (bf16[512,768]{1,0:T(8,128)(2,1)}, bf16[512,768]{1,0:T(8,128)(2,1)}, bf16[512,768]{1,0:T(8,128)(2,1)}, bf16[512,768]{1,0:T(8,128)(2,1)}, bf16[25...) custom-call(s32[9]{0:T(128)} %stack.35.meta, ...), custom_call_target="tpu_custom_call" | custom-call | flops 905969664 | bytes 933888 | tf_op jit(solution)/shard_map/home_group/pallas_call | solution.py:288
  52.8 1.3 %collective-permute-start.12 = (bf16[512,768]{1,0:T(8,128)(2,1)}, bf16[512,768]{1,0:T(8,128)(2,1)S(1)}, u32[]{:S(2)}, u32[]{:S(2)}) collective-permute-start(bf16[512,768]{1,0:T(8,128)(2,1)} %collective-permute-done.4.refs_0_), channel_id=1, source_target_pairs={{0,8},{4,12},{8,0},{12,4},{1,9},{5,13},{9,1},{13,5},{2,10},{6,14},... | collective-permute-start | bytes 2359304 | tf_op jit(solution)/shard_map/ppermute | solution.py:313
  54.1 1.6 %collective-permute-start.5 = (bf16[512,768]{1,0:T(8,128)(2,1)}, bf16[512,768]{1,0:T(8,128)(2,1)}, u32[]{:S(2)}, u32[]{:S(2)}) collective-permute-start(bf16[512,768]{1,0:T(8,128)(2,1)} %collective-permute-done.4.refs_0_), channel_id=1, source_target_pairs={{0,1},{1,2},{2,3},{3,0},{4,5},{5,6},{6,7},{7,4},{8,9},{9,10},{10,1... | collective-permute-start | bytes 2359304 | tf_op jit(solution)/shard_map/ppermute | solution.py:314
  55.7 0.9 copy-done.7
  56.6 13.7 %away_group.2 = (bf16[256,3072]{1,0:T(8,128)(2,1)}, bf16[256,3072]{1,0:T(8,128)(2,1)}, bf16[256,768]{1,0:T(8,128)(2,1)}, bf16[256,768]{1,0:T(8,128)(2,1)}) custom-call(s32[9]{0:T(128)} %stack.35.meta, bf16[512,768]{1,0:T(8,128)(2,1)} %copy-done.6, bf16[512,768]{1,0:T(8,128)(2,1)} %copy-done.7, bf16[512,768]{1,0:T(8,128)(2,1)S(1)} %collective-permute-done.7.refs_2_, ...), custom_call_target="tpu_custom_call" | custom-call | flops 603979776 | bytes 344064 | tf_op jit(solution)/shard_map/away_group/pallas_call | solution.py:288
  70.3 2.2 %collective-permute-done.12.refs_2_ = bf16[512,768]{1,0:T(8,128)(2,1)S(1)} collective-permute-done((bf16[512,768]{1,0:T(8,128)(2,1)}, bf16[512,768]{1,0:T(8,128)(2,1)S(1)}, u32[]{:S(2)}, u32[]{:S(2)}) %collective-permute-start.12) | collective-permute-done | bytes 786464 | tf_op jit(solution)/shard_map/ppermute | solution.py:313
  72.5 0.5 collective-permute-start.16
  73.0 2.8 %collective-permute-start.10 = (bf16[512,768]{1,0:T(8,128)(2,1)S(1)}, bf16[512,768]{1,0:T(8,128)(2,1)S(1)}, u32[]{:S(2)}, u32[]{:S(2)}) collective-permute-start(bf16[512,768]{1,0:T(8,128)(2,1)S(1)} %collective-permute-done.1.refs_2_), channel_id=1, source_target_pairs={{0,3},{1,0},{2,1},{3,2},{4,7},{5,4},{6,5},{7,6},{8,11},{9,8},{10,9... | collective-permute-start | bytes 2359304 | tf_op jit(solution)/shard_map/ppermute | solution.py:315
  76.2 13.7 %away_group.3 = (bf16[256,3072]{1,0:T(8,128)(2,1)}, bf16[256,3072]{1,0:T(8,128)(2,1)}, bf16[256,768]{1,0:T(8,128)(2,1)}, bf16[256,768]{1,0:T(8,128)(2,1)}) custom-call(s32[9]{0:T(128)} %stack.35.meta, bf16[512,768]{1,0:T(8,128)(2,1)} %collective-permute-done.4.refs_0_, bf16[512,768]{1,0:T(8,128)(2,1)} %collective-permute-done.11.refs_1_, ...), custom_call_target="tpu_custom_call" | custom-call | flops 603979776 | bytes 344064 | tf_op jit(solution)/shard_map/away_group/pallas_call | solution.py:288
  90.0 2.9 %collective-permute-done.10.refs_2_ = bf16[512,768]{1,0:T(8,128)(2,1)S(1)} collective-permute-done((bf16[512,768]{1,0:T(8,128)(2,1)S(1)}, bf16[512,768]{1,0:T(8,128)(2,1)S(1)}, u32[]{:S(2)}, u32[]{:S(2)}) %collective-permute-start.10) | collective-permute-done | bytes 786464 | tf_op jit(solution)/shard_map/ppermute | solution.py:315
  92.9 2.2 %add_convert_fusion = bf16[512,768]{1,0:T(8,128)(2,1)} fusion(bf16[512,768]{1,0:T(8,128)(2,1)S(1)} %copy-done.5, bf16[512,768]{1,0:T(8,128)(2,1)} %collective-permute-done.16), kind=kLoop, calls=%fused_computation | loop fusion | flops 1572864 | bytes 2359296 | tf_op jit(solution)/shard_map/convert_element_type | solution.py:421
  95.1 1.2 collective-permute-start.17
  96.6 27.6 %last_group.1 = (f32[768,3072]{1,0:T(8,128)}, f32[3072,768]{1,0:T(8,128)}) custom-call(s32[9]{0:T(128)} %stack.35.meta, bf16[512,768]{1,0:T(8,128)(2,1)} %collective-permute-done.5.refs_0_, bf16[512,768]{1,0:T(8,128)(2,1)} %collective-permute-done.9.refs_1_, bf16[512,768]{1,0:T(8,128)(2,1)S(1)} %collective-permute-done.10.refs_2_, ...), custom_call_target="tpu_custom_call" | custom-call | flops 1207959552 | bytes 2015232 | tf_op jit(solution)/shard_map/last_group/pallas_call | solution.py:288
  124.2 1.3 %restore_rows.1 = (bf16[256,768]{1,0:T(8,128)(2,1)}, bf16[256,768]{1,0:T(8,128)(2,1)}) custom-call(s32[1,256]{1,0:T(1,128)S(1)} %bitcast.10, bf16[512,768]{1,0:T(8,128)(2,1)S(1)} %copy-done.1, bf16[512,768]{1,0:T(8,128)(2,1)S(1)} %collective-permute-done.15.refs_1_, bf16[512,768]{1,0:T(8,128)(2,1)S(1)} %collective-permute-done.17.refs_2_), custom_call_target="tpu_custom_call" | custom-call | tf_op jit(solution)/shard_map/restore_rows/pallas_call | solution.py:425
  (37 shorter events, 1.8 us)
Async XLA Ops:
  2.8 5.4 %copy-start = (bf16[512,768]{1,0:T(8,128)(2,1)}, bf16[512,768]{1,0:T(8,128)(2,1)S(1)}, u32[]{:S(2)}) copy-start(bf16[512,768]{1,0:T(8,128)(2,1)S(1)} %sort_rows.1.refs_0_) | copy-start | bytes 2359300
  2.9 5.4 %collective-permute-start = (bf16[512,768]{1,0:T(8,128)(2,1)S(1)}, bf16[512,768]{1,0:T(8,128)(2,1)S(1)}, u32[]{:S(2)}, u32[]{:S(2)}) collective-permute-start(bf16[512,768]{1,0:T(8,128)(2,1)S(1)} %sort_rows.1.refs_0_), channel_id=1, source_target_pairs={{0,4},{4,0},{8,12},{12,8},{1,5},{5,1},{9,13},{13,9},{2,6},{6,2},{1... | collective-permute-start | bytes 2359304 | tf_op jit(solution)/shard_map/ppermute | solution.py:313
  3.4 23.3 %collective-permute-start.1 = (bf16[512,768]{1,0:T(8,128)(2,1)S(1)}, bf16[512,768]{1,0:T(8,128)(2,1)S(1)}, u32[]{:S(2)}, u32[]{:S(2)}) collective-permute-start(bf16[512,768]{1,0:T(8,128)(2,1)S(1)} %sort_rows.1.refs_0_), channel_id=1, source_target_pairs={{0,8},{4,12},{8,0},{12,4},{1,9},{5,13},{9,1},{13,5},{2,10},{6,14},... | collective-permute-start | bytes 2359304 | tf_op jit(solution)/shard_map/ppermute | solution.py:313
  6.0 21.5 %collective-permute-start.3 = (bf16[512,768]{1,0:T(8,128)(2,1)S(1)}, bf16[512,768]{1,0:T(8,128)(2,1)S(1)}, u32[]{:S(2)}, u32[]{:S(2)}) collective-permute-start(bf16[512,768]{1,0:T(8,128)(2,1)S(1)} %sort_rows.1.refs_0_), channel_id=1, source_target_pairs={{0,1},{1,2},{2,3},{3,0},{4,5},{5,6},{6,7},{7,4},{8,9},{9,10},{10,1... | collective-permute-start | bytes 2359304 | tf_op jit(solution)/shard_map/ppermute | solution.py:314
  8.2 0.9 copy-start.4
  26.7 2.4 %collective-permute-start.2 = (bf16[512,768]{1,0:T(8,128)(2,1)S(1)}, bf16[512,768]{1,0:T(8,128)(2,1)S(1)}, u32[]{:S(2)}, u32[]{:S(2)}) collective-permute-start(bf16[512,768]{1,0:T(8,128)(2,1)S(1)} %collective-permute-done.1.refs_2_), channel_id=1, source_target_pairs={{0,4},{4,0},{8,12},{12,8},{1,5},{5,1},{9,13},{13,9},{2,6},{6,2},{1... | collective-permute-start | bytes 2359304 | tf_op jit(solution)/shard_map/ppermute | solution.py:313
  27.4 24.8 %copy-start.6 = (bf16[512,768]{1,0:T(8,128)(2,1)}, bf16[512,768]{1,0:T(8,128)(2,1)S(1)}, u32[]{:S(2)}) copy-start(bf16[512,768]{1,0:T(8,128)(2,1)S(1)} %collective-permute-done.3.refs_0_) | copy-start | bytes 2359300
  27.4 24.8 %collective-permute-start.7 = (bf16[512,768]{1,0:T(8,128)(2,1)S(1)}, bf16[512,768]{1,0:T(8,128)(2,1)S(1)}, u32[]{:S(2)}, u32[]{:S(2)}) collective-permute-start(bf16[512,768]{1,0:T(8,128)(2,1)S(1)} %collective-permute-done.3.refs_0_), channel_id=1, source_target_pairs={{0,8},{4,12},{8,0},{12,4},{1,9},{5,13},{9,1},{13,5},{2,10},{6,14},... | collective-permute-start | bytes 2359304 | tf_op jit(solution)/shard_map/ppermute | solution.py:313
  27.9 24.8 %collective-permute-start.4 = (bf16[512,768]{1,0:T(8,128)(2,1)S(1)}, bf16[512,768]{1,0:T(8,128)(2,1)}, u32[]{:S(2)}, u32[]{:S(2)}) collective-permute-start(bf16[512,768]{1,0:T(8,128)(2,1)S(1)} %collective-permute-done.3.refs_0_), channel_id=1, source_target_pairs={{0,1},{1,2},{2,3},{3,0},{4,5},{5,6},{6,7},{7,4},{8,9},{9,10},{10,1... | collective-permute-start | bytes 2359304 | tf_op jit(solution)/shard_map/ppermute | solution.py:314
  29.0 26.7 %collective-permute-start.6 = (bf16[512,768]{1,0:T(8,128)(2,1)S(1)}, bf16[512,768]{1,0:T(8,128)(2,1)S(1)}, u32[]{:S(2)}, u32[]{:S(2)}) collective-permute-start(bf16[512,768]{1,0:T(8,128)(2,1)S(1)} %collective-permute-done.3.refs_0_), channel_id=1, source_target_pairs={{0,4},{4,0},{8,12},{12,8},{1,5},{5,1},{9,13},{13,9},{2,6},{6,2},{1... | collective-permute-start | bytes 2359304 | tf_op jit(solution)/shard_map/ppermute | solution.py:313
  52.3 3.4 %collective-permute-start.8 = (bf16[512,768]{1,0:T(8,128)(2,1)S(1)}, bf16[512,768]{1,0:T(8,128)(2,1)S(1)}, u32[]{:S(2)}, u32[]{:S(2)}) collective-permute-start(bf16[512,768]{1,0:T(8,128)(2,1)S(1)} %collective-permute-done.7.refs_2_), channel_id=1, source_target_pairs={{0,4},{4,0},{8,12},{12,8},{1,5},{5,1},{9,13},{13,9},{2,6},{6,2},{1... | collective-permute-start | bytes 2359304 | tf_op jit(solution)/shard_map/ppermute | solution.py:313
  52.8 19.8 %collective-permute-start.12 = (bf16[512,768]{1,0:T(8,128)(2,1)}, bf16[512,768]{1,0:T(8,128)(2,1)S(1)}, u32[]{:S(2)}, u32[]{:S(2)}) collective-permute-start(bf16[512,768]{1,0:T(8,128)(2,1)} %collective-permute-done.4.refs_0_), channel_id=1, source_target_pairs={{0,8},{4,12},{8,0},{12,4},{1,9},{5,13},{9,1},{13,5},{2,10},{6,14},... | collective-permute-start | bytes 2359304 | tf_op jit(solution)/shard_map/ppermute | solution.py:313
  54.1 22.1 %collective-permute-start.11 = (bf16[512,768]{1,0:T(8,128)(2,1)}, bf16[512,768]{1,0:T(8,128)(2,1)}, u32[]{:S(2)}, u32[]{:S(2)}) collective-permute-start(bf16[512,768]{1,0:T(8,128)(2,1)} %collective-permute-done.4.refs_0_), channel_id=1, source_target_pairs={{0,4},{4,0},{8,12},{12,8},{1,5},{5,1},{9,13},{13,9},{2,6},{6,2},{1... | collective-permute-start | bytes 2359304 | tf_op jit(solution)/shard_map/ppermute | solution.py:313
  54.1 22.1 %collective-permute-start.5 = (bf16[512,768]{1,0:T(8,128)(2,1)}, bf16[512,768]{1,0:T(8,128)(2,1)}, u32[]{:S(2)}, u32[]{:S(2)}) collective-permute-start(bf16[512,768]{1,0:T(8,128)(2,1)} %collective-permute-done.4.refs_0_), channel_id=1, source_target_pairs={{0,1},{1,2},{2,3},{3,0},{4,5},{5,6},{6,7},{7,4},{8,9},{9,10},{10,1... | collective-permute-start | bytes 2359304 | tf_op jit(solution)/shard_map/ppermute | solution.py:314
  72.5 3.7 %collective-permute-start.13 = (bf16[512,768]{1,0:T(8,128)(2,1)S(1)}, bf16[512,768]{1,0:T(8,128)(2,1)S(1)}, u32[]{:S(2)}, u32[]{:S(2)}) collective-permute-start(bf16[512,768]{1,0:T(8,128)(2,1)S(1)} %collective-permute-done.12.refs_2_), channel_id=1, source_target_pairs={{0,4},{4,0},{8,12},{12,8},{1,5},{5,1},{9,13},{13,9},{2,6},{6,2},{1... | collective-permute-start | bytes 2359304 | tf_op jit(solution)/shard_map/ppermute | solution.py:313
  72.5 20.4 %copy-start.5 = (bf16[512,768]{1,0:T(8,128)(2,1)S(1)}, bf16[512,768]{1,0:T(8,128)(2,1)}, u32[]{:S(2)}) copy-start(bf16[512,768]{1,0:T(8,128)(2,1)} %get-tuple-element.73) | copy-start | bytes 2359300
  72.5 17.4 %collective-permute-start.16 = (bf16[512,768]{1,0:T(8,128)(2,1)}, bf16[512,768]{1,0:T(8,128)(2,1)}, u32[]{:S(2)}, u32[]{:S(2)}) collective-permute-start(bf16[512,768]{1,0:T(8,128)(2,1)} %get-tuple-element.71), channel_id=1, source_target_pairs={{0,4},{4,0},{8,12},{12,8},{1,5},{5,1},{9,13},{13,9},{2,6},{6,2},{1... | collective-permute-start | bytes 2359304 | tf_op jit(solution)/shard_map/ppermute | solution.py:313
  73.0 19.9 %collective-permute-start.10 = (bf16[512,768]{1,0:T(8,128)(2,1)S(1)}, bf16[512,768]{1,0:T(8,128)(2,1)S(1)}, u32[]{:S(2)}, u32[]{:S(2)}) collective-permute-start(bf16[512,768]{1,0:T(8,128)(2,1)S(1)} %collective-permute-done.1.refs_2_), channel_id=1, source_target_pairs={{0,3},{1,0},{2,1},{3,2},{4,7},{5,4},{6,5},{7,6},{8,11},{9,8},{10,9... | collective-permute-start | bytes 2359304 | tf_op jit(solution)/shard_map/ppermute | solution.py:315
  76.2 20.4 %collective-permute-start.9 = (bf16[512,768]{1,0:T(8,128)(2,1)}, bf16[512,768]{1,0:T(8,128)(2,1)}, u32[]{:S(2)}, u32[]{:S(2)}) collective-permute-start(bf16[512,768]{1,0:T(8,128)(2,1)} %collective-permute-done.5.refs_0_), channel_id=1, source_target_pairs={{0,4},{4,0},{8,12},{12,8},{1,5},{5,1},{9,13},{13,9},{2,6},{6,2},{1... | collective-permute-start | bytes 2359304 | tf_op jit(solution)/shard_map/ppermute | solution.py:313
  92.9 3.7 %collective-permute-start.14 = (bf16[512,768]{1,0:T(8,128)(2,1)S(1)}, bf16[512,768]{1,0:T(8,128)(2,1)S(1)}, u32[]{:S(2)}, u32[]{:S(2)}) collective-permute-start(bf16[512,768]{1,0:T(8,128)(2,1)S(1)} %collective-permute-done.10.refs_2_), channel_id=1, source_target_pairs={{0,4},{4,0},{8,12},{12,8},{1,5},{5,1},{9,13},{13,9},{2,6},{6,2},{1... | collective-permute-start | bytes 2359304 | tf_op jit(solution)/shard_map/ppermute | solution.py:313
  95.1 29.0 %collective-permute-start.17 = (bf16[512,768]{1,0:T(8,128)(2,1)}, bf16[512,768]{1,0:T(8,128)(2,1)S(1)}, u32[]{:S(2)}, u32[]{:S(2)}) collective-permute-start(bf16[512,768]{1,0:T(8,128)(2,1)} %add_convert_fusion), channel_id=1, source_target_pairs={{0,8},{4,12},{8,0},{12,4},{1,9},{5,13},{9,1},{13,5},{2,10},{6,14},... | collective-permute-start | bytes 2359304 | tf_op jit(solution)/shard_map/ppermute | solution.py:313
  96.3 27.8 %collective-permute-start.15 = (bf16[512,768]{1,0:T(8,128)(2,1)}, bf16[512,768]{1,0:T(8,128)(2,1)S(1)}, u32[]{:S(2)}, u32[]{:S(2)}) collective-permute-start(bf16[512,768]{1,0:T(8,128)(2,1)} %get-tuple-element.68), channel_id=1, source_target_pairs={{0,4},{4,0},{8,12},{12,8},{1,5},{5,1},{9,13},{13,9},{2,6},{6,2},{1... | collective-permute-start | bytes 2359304 | tf_op jit(solution)/shard_map/ppermute | solution.py:313
  96.6 27.6 %copy-start.1 = (bf16[512,768]{1,0:T(8,128)(2,1)S(1)}, bf16[512,768]{1,0:T(8,128)(2,1)}, u32[]{:S(2)}) copy-start(bf16[512,768]{1,0:T(8,128)(2,1)} %get-tuple-element.66.refs_0_) | copy-start | bytes 2359300
  96.6 27.6 %copy-start.3 = (s32[256]{0:T(256)S(1)}, s32[256]{0:T(256)}, u32[]{:S(2)}) copy-start(s32[256]{0:T(256)} %param.6) | copy-start | bytes 3076
  (2 other events, 1.6 us)

commit v4 on v3

--- a/solution.py
+++ b/solution.py
@@ -35,41 +35,63 @@
     return pre_act * half, slope
 
 
-def unpack(pieces, at, x_out, c_out, to):
-    level = x_out.shape[0] // LEVELS
-    first = 0
+def unpack(pieces, at, x_out, c_out, to, level, stride, offset=0):
+    first = offset
     for piece in pieces:
         for start in range(0, piece.shape[0], 2 * level):
             x_out[first : first + level, to] = piece[start : start + level, at]
             c_out[first : first + level, to] = piece[start + level : start + 2 * level, at]
-            first += level
-
-
-def fill(meta, blocks, x_full, c_full, base=0, spots=None):
-    for spot, pieces in enumerate(blocks):
-        if spots is None or spot in spots:
-            to = pl.ds(pl.multiple_of(meta[FIXED + spot] - base, 128), pieces[0].shape[1])
-            unpack(pieces, slice(None), x_full, c_full, to)
-
-
-def fill_late(meta, begun, blocks, x_full, c_full):
-    if begun:
-        fill(meta, blocks, x_full, c_full, meta[4], (2, 3))
-    else:
-        fill(meta, blocks, x_full, c_full)
-
-
-def own_columns(meta, blocks, x_cols, c_cols):
+            first += stride
+
+
+def fill(meta, blocks, spot, base, x_part, c_part):
+    level = x_part.shape[0] // LEVELS
+    for more, pieces in enumerate(blocks):
+        to = pl.ds(pl.multiple_of(meta[FIXED + spot + more] - base, 128), pieces[0].shape[1])
+        unpack(pieces, slice(None), x_part, c_part, to, level, level)
+
+
+def own_columns(meta, blocks, first_spot, x_cols, c_cols, level, stride, offset=0):
     width = x_cols.shape[1]
     start = meta[2] * width
     for spot, pieces in enumerate(blocks):
         wide = pieces[0].shape[1]
-        begin = meta[FIXED + spot]
+        begin = meta[FIXED + first_spot + spot]
 
         @pl.when((start >= begin) & (start < begin + wide))
         def _():
             at = pl.ds(pl.multiple_of(start - begin, 128), width) if width < wide else slice(None)
-            unpack(pieces, at, x_cols, c_cols, slice(None))
+            unpack(pieces, at, x_cols, c_cols, slice(None), level, stride, offset)
+
+
+def landings(refs, raw, arrived):
+    return [pltpu.make_async_copy(ref, raw.at[spot], arrived.at[spot]) for spot, ref in enumerate(refs)]
+
+
+def level_landings(meta, refs, x_full, c_full, arrived):
+    level = x_full.shape[0] // LEVELS
+    copies = []
+    for spot, ref in enumerate(refs):
+        to = pl.ds(pl.multiple_of(meta[FIXED + spot], 128), ref.shape[1])
+        for level_idx in range(LEVELS):
+            for side, part in enumerate((x_full, c_full)):
+                copies.append(
+                    pltpu.make_async_copy(
+                        ref.at[pl.ds((2 * level_idx + side) * level, level), :],
+                        part.at[pl.ds(level_idx * level, level), to],
+                        arrived.at[spot, level_idx, side],
+                    )
+                )
+    return copies
+
+
+def full_columns(meta, x_full, c_full, x_cols, c_cols, level, stride, offset=0):
+    width = x_cols.shape[1]
+    at = pl.ds(pl.multiple_of(meta[2] * width, 128), width)
+    for level_idx in range(LEVELS):
+        here, to = pl.ds(level_idx * level, level), pl.ds(offset + level_idx * stride, level)
+        x_cols[to, :] = x_full[here, at]
+        c_cols[to, :] = c_full[here, at]
 
 
 def unit_slice(size, first=0):
@@ -159,31 +181,57 @@
         for step in range(w_in.shape[1] // units):
             for copy in copies(step):
                 copy.start()
-        fill(meta, blocks, x_full, c_full, meta[3])
+        fill(meta, blocks, 0, meta[3], x_full, c_full)
 
     for copy in copies(pl.program_id(0)):
         copy.wait()
     pre_out[...], back_out[...] = products(x_full, c_full, meta[3], views([weights]), units)
 
 
-def home_kernel(counts, held, begun, meta, *refs):
-    blocks, refs = split_refs(refs, counts)
-    (weights, begun, parts), refs = split_refs(refs, (held, begun, len(counts)))
-    hidden_out, back_out, x_cols, c_cols, x_full, c_full, total_out, total_in = refs
+def all_products(meta, near, late, x_full, c_full, weights, units, at_near):
+    @pl.when(pl.program_id(0) == 0)
+    def _():
+        for copy in near:
+            copy.start()
+        fill(meta, late, 2, 0, x_full, c_full)
+        for copy in near:
+            copy.wait()
+        at_near()
+
+    return activations(meta, *products(x_full, c_full, 0, weights, units))
+
+
+def home_kernel(near_count, counts, held, begun, meta, *refs):
+    near, refs = refs[:near_count], refs[near_count:]
+    late, refs = split_refs(refs, counts)
+    (weights, begun, parts), refs = split_refs(refs, (held, begun, near_count + len(counts)))
+    hidden_out, back_out, x_cols, c_cols, raw, arrived, x_part, c_part, total_out, total_in = refs
+    blocks = [[raw.at[spot]] for spot in range(near_count)]
+    near = landings(near, raw, arrived)
     step = pl.program_id(0)
     rows, units = hidden_out.shape
     model = total_out.shape[1]
     level = rows // LEVELS
+    weights = views(weights)
 
     @pl.when(step == 0)
     def _():
-        fill_late(meta, begun, blocks, x_full, c_full)
-        own_columns(meta, blocks, x_cols, c_cols)
-
-    hidden, back_pre = late_products(meta, x_full, c_full, begun, weights, units)
+        for copy in near:
+            copy.start()
+        if begun:
+            fill(meta, late, 2, meta[4], x_part, c_part)
+        else:
+            for copy in near:
+                copy.wait()
+            fill(meta, blocks, 0, meta[3], x_part, c_part)
+
+    pre_act, back_hidden = products(x_part, c_part, meta[4] if begun else meta[3], weights, units)
+    if begun:
+        pre_act, back_hidden = pre_act + begun[0][...], back_hidden + begun[1][...]
+    hidden, back_pre = activations(meta, pre_act, back_hidden)
     hidden_out[...] = hidden
     back_out[...] = back_pre
-    w_first, w_second = views(weights)
+    w_first, w_second = weights
     at = unit_slice(units)
     wide = model // 4
     shares = lambda cols: (
@@ -207,6 +255,10 @@
 
     @pl.when(step == pl.num_programs(0) - 1)
     def _():
+        if begun:
+            for copy in near:
+                copy.wait()
+        own_columns(meta, blocks + late, 0, x_cols, c_cols, level, level)
         for spot, part in enumerate(parts):
             cols = pl.ds(pl.multiple_of(meta[FIXED + spot], 128), part.shape[1])
             for level_idx in range(LEVELS):
@@ -216,30 +268,25 @@
                 part[start + level : start + 2 * level, :] = total_in[here, cols].astype(jnp.bfloat16)
 
 
-def late_products(meta, x_full, c_full, begun, weights, units):
-    if not begun:
-        return activations(meta, *products(x_full, c_full, 0, views(weights), units))
-    pre_act, back_hidden = products(x_full, c_full, meta[4], views(weights), units)
-    return activations(meta, pre_act + begun[0][...], back_hidden + begun[1][...])
-
-
-def away_kernel(counts, held, meta, *refs):
-    blocks, refs = split_refs(refs, counts)
-    weights, (hidden_out, back_out, x_cols, c_cols, x_full, c_full) = refs[:held], refs[held:]
-
-    @pl.when(pl.program_id(0) == 0)
-    def _():
-        fill(meta, blocks, x_full, c_full)
-        own_columns(meta, blocks, x_cols, c_cols)
-
-    hidden_out[...], back_out[...] = late_products(meta, x_full, c_full, (), weights, hidden_out.shape[1])
-
-
-def last_kernel(counts, held, others, meta, *refs):
-    blocks, refs = split_refs(refs, counts)
+def away_kernel(near_count, counts, held, meta, *refs):
+    near, refs = refs[:near_count], refs[near_count:]
+    late, refs = split_refs(refs, counts)
+    weights, (hidden_out, back_out, x_cols, c_cols, arrived, x_full, c_full) = refs[:held], refs[held:]
+    near = level_landings(meta, near, x_full, c_full, arrived)
+    level = hidden_out.shape[0] // LEVELS
+    hidden_out[...], back_out[...] = all_products(
+        meta, near, late, x_full, c_full, views(weights), hidden_out.shape[1],
+        lambda: full_columns(meta, x_full, c_full, x_cols, c_cols, level, level),
+    )
+
+
+def last_kernel(near_count, counts, held, others, meta, *refs):
+    near, refs = refs[:near_count], refs[near_count:]
+    late, refs = split_refs(refs, counts)
     (weights, *past), refs = split_refs(refs, (held,) + (4,) * others)
-    grad_in, grad_out, x_full, c_full, x_cols, x_turned, c_all, hidden_all, back_all = refs
+    grad_in, grad_out, x_full, c_full, x_cols, c_all, x_turned, hidden_all, back_all = refs
     rows = x_full.shape[0]
+    level = rows // LEVELS
     own = pl.ds(others * rows, rows)
 
     @pl.when(pl.program_id(0) == 0)
@@ -247,11 +294,14 @@
         for spot in range(others):
             x_turned[:, pl.ds(spot * rows, rows)] = past[spot][2][...].T
             c_all[pl.ds(spot * rows, rows), :] = past[spot][3][...]
-        fill(meta, blocks, x_full, c_full)
-        own_columns(meta, blocks, x_cols, c_all.at[own, :])
+        fill(meta, [[ref] for ref in near], 0, 0, x_full, c_full)
+        fill(meta, late, 2, 0, x_full, c_full)
+        full_columns(meta, x_full, c_full, x_cols, c_all.at[own, :], level, level)
         x_turned[:, own] = x_cols[...].T
 
-    hidden, back_pre = late_products(meta, x_full, c_full, (), weights, hidden_all.shape[1])
+    hidden, back_pre = activations(
+        meta, *products(x_full, c_full, 0, views(weights), hidden_all.shape[1])
+    )
     for spot in range(others):
         hidden_all[pl.ds(spot * rows, rows), :] = past[spot][0][...]
         back_all[pl.ds(spot * rows, rows), :] = past[spot][1][...]
@@ -331,25 +381,28 @@
         return [opposite, [cross(piece, swap(1)) for piece in opposite]]
 
     offsets = [tp_rank ^ spot for spot in range(4)] if paired else [0]
-    pair = tp_rank // 2 * 2
+    pair = tp_rank // 2 * 2 if paired else 0
     meta = jnp.stack(
-        [tp_rank * units, jnp.int32(units * n_tp), dp_rank, pair * width, (pair ^ 2) * width]
+        [tp_rank * units, jnp.int32(units * n_tp), dp_rank, jnp.int32(pair * width), jnp.int32((pair ^ 2) * width)]
         + [jnp.int32(offset * width) for offset in offsets]
     ).astype(jnp.int32)
     size, away_size = unit_block(units, 512), unit_block(units, 1536)
-    flat = lambda blocks: [(piece, "vmem" if spot >= 2 else "whole") for spot, pieces in enumerate(blocks) for piece in pieces]
+    flat = lambda blocks, kind: [(piece, kind) for pieces in blocks for piece in pieces]
     counts_of = lambda blocks: tuple(len(pieces) for pieces in blocks)
     kept_outs = [((rows, units), bf16, "cols")] * 2 + [((rows, own), bf16, "whole")] * 2
     partial_outs = [((rows, units), f32, "cols")] * 2
     full = [pltpu.VMEM((rows, model), bf16)] * 2
-    half = [pltpu.VMEM((rows, model // 2), bf16)] * 2 if paired else full
+    half = [pltpu.VMEM((rows, model // 2 if paired else model), bf16)] * 2
+    n_near = 2 if paired else 1
+    level_landing = [pltpu.SemaphoreType.DMA((n_near, LEVELS, 2))]
+    landing = [pltpu.VMEM((n_near, 2 * rows, width if paired else model), bf16), pltpu.SemaphoreType.DMA((n_near,))]
     share = lambda columns: 4 * rows * columns * units
 
     in_hbm = lambda array: pltpu.with_memory_space_constraint(array, pltpu.HBM)
     small = pltpu.CompilerParams(vmem_limit_bytes=LIM * MIB)
     chunk = pl.pallas_call(
         sort_kernel, name="sort_rows", out_shape=jax.ShapeDtypeStruct((2 * rows, width), bf16), compiler_params=small
-    )(ordering[None, :], in_hbm(patches), in_hbm(cotangent))
+    )(in_hbm(ordering[None, :]), in_hbm(patches), in_hbm(cotangent))
 
     near = near_of(chunk)
     opposite = opposite_of(chunk)
@@ -358,7 +411,7 @@
     if paired:
         weights, *begun = run_kernel(
             functools.partial(open_kernel, counts_of(near)), "open_group", meta, size, units,
-            flat(near) + [(w_in, "any"), (w_out, "any")],
+            flat(near, "whole") + [(w_in, "any"), (w_out, "any")],
             [((2 * model, units), bf16, "vmem")] + partial_outs,
             half + [pltpu.SemaphoreType.DMA((2, units // size))],
             share(model // 2),
@@ -368,14 +421,14 @@
     else:
         held, done, begun = [(w_in, "vmem"), (w_out, "vmem")], meta, []
     chunk = after(coming, done)
-    blocks = near + rest_of(opposite, done)
+    late = rest_of(opposite, done)
     opposite = opposite_of(chunk)
     coming = onward(chunk)
     *parts, hidden, back_pre, x_cols, c_cols = run_kernel(
-        functools.partial(home_kernel, counts_of(blocks), len(held), len(begun)), "home_group", meta, size, units,
-        flat(blocks) + held + [(array, "cols") for array in begun],
-        [((2 * rows, width if paired else model), bf16, "whole")] * len(blocks) + kept_outs,
-        half + [pltpu.VMEM((rows, model), f32)] * 2,
+        functools.partial(home_kernel, n_near, counts_of(late), len(held), len(begun)), "home_group", meta, size, units,
+        flat(near, "any") + flat(late, "vmem") + held + [(array, "cols") for array in begun],
+        [((2 * rows, width if paired else model), bf16, "whole")] * len(offsets) + kept_outs,
+        landing + half + [pltpu.VMEM((rows, model), f32)] * 2,
         share(2 * model - model // 2 * len(begun) // 2),
         LIM,
     )
@@ -383,7 +436,7 @@
     for step in range(1, n_dp):
         done = past[-1][0]
         near = near_of(chunk)
-        blocks = near + rest_of(opposite, done)
+        late = rest_of(opposite, done)
         if step < n_dp - 1:
             chunk = after(coming, done)
             if not turned or step < n_dp - 2:
@@ -391,25 +444,27 @@
             else:
                 opposite = far_coming
             if turned and step == n_dp - 3:
-                coming, far_coming = onward(chunk), [back(after(own_opposite, done))]
+                coming = onward(chunk)
+                far_coming = [back(after(own_opposite, done))]
             elif step < n_dp - 2:
                 coming = onward(chunk)
             past.append(
                 run_kernel(
-                    functools.partial(away_kernel, counts_of(blocks), len(held)), "away_group", meta, away_size, units,
-                    flat(blocks) + held, kept_outs, full, share(model), LIM,
+                    functools.partial(away_kernel, n_near, counts_of(late), len(held)), "away_group",
+                    meta, away_size, units, flat(near, "any") + flat(late, "vmem") + held, kept_outs,
+                    level_landing + full, share(model), LIM,
                 )
             )
     everyone = rows * n_dp
     grad_in, grad_out = run_kernel(
-        functools.partial(last_kernel, counts_of(blocks), len(held), len(past)), "last_group",
-        meta, size, units,
-        flat(blocks) + held + [pair for kept in past for pair in zip(kept, ("cols", "cols", "whole", "whole"))],
+        functools.partial(last_kernel, n_near, counts_of(late), len(held), len(past)), "last_group", meta, size, units,
+        flat(near, "whole") + flat(late, "vmem") + held
+        + [pair for kept in past for pair in zip(kept, ("cols", "cols", "whole", "whole"))],
         [((own, units), f32, "cols"), ((units, own), f32, "rows")],
         full + [
             pltpu.VMEM((rows, own), bf16),
+            pltpu.VMEM((everyone, own), bf16),
             pltpu.VMEM((own, everyone), bf16),
-            pltpu.VMEM((everyone, own), bf16),
             pltpu.VMEM((everyone, size), bf16),
             pltpu.VMEM((everyone, size), bf16),
         ],

time: 126 us -> 125 us (level)
  transfers between devices with their start and end apart: 18 -> 18, of which waited for: 5 -> 5; matrix products, arithmetic and copies ran while one was open for 2% -> 2% of each run, Pallas kernels for 76% -> 77%
where the time goes in v4:
time: 125 us; the launch traced here: 124 us
  Pallas kernels  97.9 us (78%)
  starting transfers between devices  14.4 us (12%)
  waiting for transfers between devices  6.41 us (5%)
  local copies, waits for them, and re-layouts  2.48 us (2%)
  other arithmetic  2.2 us (2%)
    pallas_call x5, Pallas kernels, run_kernel(): pl.pallas_call(kernel, name=name, out_shape=[shape_of(*out) for out in ou...  95 us
    ppermute x14, starting transfers between devices, shards(): cross = lambda array, pairs: lax.ppermute(array, 'tp', pairs)  7.46 us
    ppermute x3, starting transfers between devices, shards(): lax.ppermute(array, 'dp', [(rank, (rank + 1) % n_dp) for rank in range(n_...  4.17 us
    ppermute x1, waiting for transfers between devices, shards(): lax.ppermute(array, 'dp', [(rank, (rank - 1) % n_dp) for rank in range(n_...  3.01 us
    ppermute x1, starting transfers between devices, shards(): lax.ppermute(array, 'dp', [(rank, (rank - 1) % n_dp) for rank in range(n_...  2.8 us
  transfers between devices with their start and end apart: 18, of which 5 were waited for; matrix products, arithmetic and copies ran while one was open for 2% of the time, Pallas kernels for 77%

profile of v4, /device:TPU:0, one launch (start us, length us, event | category | flops | bytes accessed | tf_op | source)
XLA Modules:
  0.0 124.2 jit_solution(13456230205875742629)
XLA Ops:
  0.6 1.5 %sort_rows.1.refs_0_ = bf16[512,768]{1,0:T(8,128)(2,1)S(1)} custom-call(s32[1,256]{1,0:T(1,128)} %bitcast.9, bf16[256,768]{1,0:T(8,128)(2,1)} %patches.1, bf16[256,768]{1,0:T(8,128)(2,1)} %cotangent.1), custom_call_target="tpu_custom_call" | custom-call | tf_op jit(solution)/shard_map/sort_rows/pallas_call | solution.py:403
  2.2 0.5 collective-permute-start
  2.7 2.6 %collective-permute-start.1 = (bf16[512,768]{1,0:T(8,128)(2,1)S(1)}, bf16[512,768]{1,0:T(8,128)(2,1)S(1)}, u32[]{:S(2)}, u32[]{:S(2)}) collective-permute-start(bf16[512,768]{1,0:T(8,128)(2,1)S(1)} %sort_rows.1.refs_0_), channel_id=1, source_target_pairs={{0,8},{4,12},{8,0},{12,4},{1,9},{5,13},{9,1},{13,5},{2,10},{6,14},... | collective-permute-start | bytes 2359304 | tf_op jit(solution)/shard_map/ppermute | solution.py:363
  5.3 1.6 %collective-permute-start.3 = (bf16[512,768]{1,0:T(8,128)(2,1)S(1)}, bf16[512,768]{1,0:T(8,128)(2,1)S(1)}, u32[]{:S(2)}, u32[]{:S(2)}) collective-permute-start(bf16[512,768]{1,0:T(8,128)(2,1)S(1)} %sort_rows.1.refs_0_), channel_id=1, source_target_pairs={{0,1},{1,2},{2,3},{3,0},{4,5},{5,6},{6,7},{7,4},{8,9},{9,10},{10,1... | collective-permute-start | bytes 2359304 | tf_op jit(solution)/shard_map/ppermute | solution.py:364
  6.9 0.7 stack.35.meta
  7.6 0.9 copy-done.3
  8.5 17.6 %open_group.1 = (bf16[6144,3072]{1,0:T(8,128)(2,1)S(1)}, f32[256,3072]{1,0:T(8,128)}, f32[256,3072]{1,0:T(8,128)}) custom-call(s32[9]{0:T(128)} %stack.35.meta, bf16[512,768]{1,0:T(8,128)(2,1)} %copy-done, bf16[512,768]{1,0:T(8,128)(2,1)} %copy-done.3, bf16[3072,3072]{1,0:T(8,128)(2,1)} %refs_2_.1, bf16[3072,3072]{1,0:T(8,128)(2,1)} %refs_3_.1), custom_call_target="tpu_custom_call" | custom-call | flops 301989888 | bytes 2850816 | tf_op jit(solution)/shard_map/open_group/pallas_call | solution.py:338
  26.1 0.6 collective-permute-done.3.refs_0_
  26.8 0.5 collective-permute-start.7
  27.3 1.0 collective-permute-start.4
  28.4 22.7 %home_group.1 = (bf16[512,768]{1,0:T(8,128)(2,1)}, bf16[512,768]{1,0:T(8,128)(2,1)}, bf16[512,768]{1,0:T(8,128)(2,1)}, bf16[512,768]{1,0:T(8,128)(2,1)}, bf16[25...) custom-call(s32[9]{0:T(128)} %stack.35.meta, ...), custom_call_target="tpu_custom_call" | custom-call | flops 905969664 | bytes 933888 | tf_op jit(solution)/shard_map/home_group/pallas_call | solution.py:338
  51.6 1.3 %collective-permute-start.12 = (bf16[512,768]{1,0:T(8,128)(2,1)}, bf16[512,768]{1,0:T(8,128)(2,1)S(1)}, u32[]{:S(2)}, u32[]{:S(2)}) collective-permute-start(bf16[512,768]{1,0:T(8,128)(2,1)} %collective-permute-done.4.refs_0_), channel_id=1, source_target_pairs={{0,8},{4,12},{8,0},{12,4},{1,9},{5,13},{9,1},{13,5},{2,10},{6,14},... | collective-permute-start | bytes 2359304 | tf_op jit(solution)/shard_map/ppermute | solution.py:363
  52.9 1.6 %collective-permute-start.5 = (bf16[512,768]{1,0:T(8,128)(2,1)}, bf16[512,768]{1,0:T(8,128)(2,1)}, u32[]{:S(2)}, u32[]{:S(2)}) collective-permute-start(bf16[512,768]{1,0:T(8,128)(2,1)} %collective-permute-done.4.refs_0_), channel_id=1, source_target_pairs={{0,1},{1,2},{2,3},{3,0},{4,5},{5,6},{6,7},{7,4},{8,9},{9,10},{10,1... | collective-permute-start | bytes 2359304 | tf_op jit(solution)/shard_map/ppermute | solution.py:364
  54.5 0.9 copy-done.6
  55.4 13.7 %away_group.2 = (bf16[256,3072]{1,0:T(8,128)(2,1)}, bf16[256,3072]{1,0:T(8,128)(2,1)}, bf16[256,768]{1,0:T(8,128)(2,1)}, bf16[256,768]{1,0:T(8,128)(2,1)}) custom-call(s32[9]{0:T(128)} %stack.35.meta, bf16[512,768]{1,0:T(8,128)(2,1)} %copy-done.5, bf16[512,768]{1,0:T(8,128)(2,1)} %copy-done.6, bf16[512,768]{1,0:T(8,128)(2,1)S(1)} %collective-permute-done.7.refs_2_, ...), custom_call_target="tpu_custom_call" | custom-call | flops 603979776 | bytes 344064 | tf_op jit(solution)/shard_map/away_group/pallas_call | solution.py:338
  69.1 2.2 %collective-permute-done.12.refs_2_ = bf16[512,768]{1,0:T(8,128)(2,1)S(1)} collective-permute-done((bf16[512,768]{1,0:T(8,128)(2,1)}, bf16[512,768]{1,0:T(8,128)(2,1)S(1)}, u32[]{:S(2)}, u32[]{:S(2)}) %collective-permute-start.12) | collective-permute-done | bytes 786464 | tf_op jit(solution)/shard_map/ppermute | solution.py:363
  71.3 0.5 collective-permute-start.16
  71.8 2.8 %collective-permute-start.10 = (bf16[512,768]{1,0:T(8,128)(2,1)S(1)}, bf16[512,768]{1,0:T(8,128)(2,1)S(1)}, u32[]{:S(2)}, u32[]{:S(2)}) collective-permute-start(bf16[512,768]{1,0:T(8,128)(2,1)S(1)} %collective-permute-done.1.refs_2_), channel_id=1, source_target_pairs={{0,3},{1,0},{2,1},{3,2},{4,7},{5,4},{6,5},{7,6},{8,11},{9,8},{10,9... | collective-permute-start | bytes 2359304 | tf_op jit(solution)/shard_map/ppermute | solution.py:365
  75.0 13.7 %away_group.3 = (bf16[256,3072]{1,0:T(8,128)(2,1)}, bf16[256,3072]{1,0:T(8,128)(2,1)}, bf16[256,768]{1,0:T(8,128)(2,1)}, bf16[256,768]{1,0:T(8,128)(2,1)}) custom-call(s32[9]{0:T(128)} %stack.35.meta, bf16[512,768]{1,0:T(8,128)(2,1)} %collective-permute-done.4.refs_0_, bf16[512,768]{1,0:T(8,128)(2,1)} %collective-permute-done.11.refs_1_, ...), custom_call_target="tpu_custom_call" | custom-call | flops 603979776 | bytes 344064 | tf_op jit(solution)/shard_map/away_group/pallas_call | solution.py:338
  88.7 3.0 %collective-permute-done.10.refs_2_ = bf16[512,768]{1,0:T(8,128)(2,1)S(1)} collective-permute-done((bf16[512,768]{1,0:T(8,128)(2,1)S(1)}, bf16[512,768]{1,0:T(8,128)(2,1)S(1)}, u32[]{:S(2)}, u32[]{:S(2)}) %collective-permute-start.10) | collective-permute-done | bytes 786464 | tf_op jit(solution)/shard_map/ppermute | solution.py:365
  91.7 2.2 %add_convert_fusion = bf16[512,768]{1,0:T(8,128)(2,1)} fusion(bf16[512,768]{1,0:T(8,128)(2,1)S(1)} %copy-done.4, bf16[512,768]{1,0:T(8,128)(2,1)} %collective-permute-done.16), kind=kLoop, calls=%fused_computation | loop fusion | flops 1572864 | bytes 2359296 | tf_op jit(solution)/shard_map/convert_element_type | solution.py:476
  93.9 1.2 collective-permute-start.17
  95.4 27.4 %last_group.1 = (f32[768,3072]{1,0:T(8,128)}, f32[3072,768]{1,0:T(8,128)}) custom-call(s32[9]{0:T(128)} %stack.35.meta, bf16[512,768]{1,0:T(8,128)(2,1)} %collective-permute-done.5.refs_0_, bf16[512,768]{1,0:T(8,128)(2,1)} %collective-permute-done.9.refs_1_, bf16[512,768]{1,0:T(8,128)(2,1)S(1)} %collective-permute-done.10.refs_2_, ...), custom_call_target="tpu_custom_call" | custom-call | flops 1207959552 | bytes 2015232 | tf_op jit(solution)/shard_map/last_group/pallas_call | solution.py:338
  122.9 1.3 %restore_rows.1 = (bf16[256,768]{1,0:T(8,128)(2,1)}, bf16[256,768]{1,0:T(8,128)(2,1)}) custom-call(s32[1,256]{1,0:T(1,128)S(1)} %bitcast.10, bf16[512,768]{1,0:T(8,128)(2,1)S(1)} %copy-done.1, bf16[512,768]{1,0:T(8,128)(2,1)S(1)} %collective-permute-done.15.refs_1_, bf16[512,768]{1,0:T(8,128)(2,1)S(1)} %collective-permute-done.17.refs_2_), custom_call_target="tpu_custom_call" | custom-call | tf_op jit(solution)/shard_map/restore_rows/pallas_call | solution.py:480
  (35 shorter events, 1.3 us)
Async XLA Ops:
  2.2 5.4 %copy-start = (bf16[512,768]{1,0:T(8,128)(2,1)}, bf16[512,768]{1,0:T(8,128)(2,1)S(1)}, u32[]{:S(2)}) copy-start(bf16[512,768]{1,0:T(8,128)(2,1)S(1)} %sort_rows.1.refs_0_) | copy-start | bytes 2359300
  2.2 5.4 %collective-permute-start = (bf16[512,768]{1,0:T(8,128)(2,1)S(1)}, bf16[512,768]{1,0:T(8,128)(2,1)S(1)}, u32[]{:S(2)}, u32[]{:S(2)}) collective-permute-start(bf16[512,768]{1,0:T(8,128)(2,1)S(1)} %sort_rows.1.refs_0_), channel_id=1, source_target_pairs={{0,4},{4,0},{8,12},{12,8},{1,5},{5,1},{9,13},{13,9},{2,6},{6,2},{1... | collective-permute-start | bytes 2359304 | tf_op jit(solution)/shard_map/ppermute | solution.py:363
  2.7 23.3 %collective-permute-start.1 = (bf16[512,768]{1,0:T(8,128)(2,1)S(1)}, bf16[512,768]{1,0:T(8,128)(2,1)S(1)}, u32[]{:S(2)}, u32[]{:S(2)}) collective-permute-start(bf16[512,768]{1,0:T(8,128)(2,1)S(1)} %sort_rows.1.refs_0_), channel_id=1, source_target_pairs={{0,8},{4,12},{8,0},{12,4},{1,9},{5,13},{9,1},{13,5},{2,10},{6,14},... | collective-permute-start | bytes 2359304 | tf_op jit(solution)/shard_map/ppermute | solution.py:363
  5.3 21.5 %collective-permute-start.3 = (bf16[512,768]{1,0:T(8,128)(2,1)S(1)}, bf16[512,768]{1,0:T(8,128)(2,1)S(1)}, u32[]{:S(2)}, u32[]{:S(2)}) collective-permute-start(bf16[512,768]{1,0:T(8,128)(2,1)S(1)} %sort_rows.1.refs_0_), channel_id=1, source_target_pairs={{0,1},{1,2},{2,3},{3,0},{4,5},{5,6},{6,7},{7,4},{8,9},{9,10},{10,1... | collective-permute-start | bytes 2359304 | tf_op jit(solution)/shard_map/ppermute | solution.py:364
  7.6 0.9 copy-start.3
  26.0 2.4 %collective-permute-start.2 = (bf16[512,768]{1,0:T(8,128)(2,1)S(1)}, bf16[512,768]{1,0:T(8,128)(2,1)S(1)}, u32[]{:S(2)}, u32[]{:S(2)}) collective-permute-start(bf16[512,768]{1,0:T(8,128)(2,1)S(1)} %collective-permute-done.1.refs_2_), channel_id=1, source_target_pairs={{0,4},{4,0},{8,12},{12,8},{1,5},{5,1},{9,13},{13,9},{2,6},{6,2},{1... | collective-permute-start | bytes 2359304 | tf_op jit(solution)/shard_map/ppermute | solution.py:363
  26.8 24.3 %copy-start.5 = (bf16[512,768]{1,0:T(8,128)(2,1)}, bf16[512,768]{1,0:T(8,128)(2,1)S(1)}, u32[]{:S(2)}) copy-start(bf16[512,768]{1,0:T(8,128)(2,1)S(1)} %collective-permute-done.3.refs_0_) | copy-start | bytes 2359300
  26.8 24.3 %collective-permute-start.7 = (bf16[512,768]{1,0:T(8,128)(2,1)S(1)}, bf16[512,768]{1,0:T(8,128)(2,1)S(1)}, u32[]{:S(2)}, u32[]{:S(2)}) collective-permute-start(bf16[512,768]{1,0:T(8,128)(2,1)S(1)} %collective-permute-done.3.refs_0_), channel_id=1, source_target_pairs={{0,8},{4,12},{8,0},{12,4},{1,9},{5,13},{9,1},{13,5},{2,10},{6,14},... | collective-permute-start | bytes 2359304 | tf_op jit(solution)/shard_map/ppermute | solution.py:363
  27.3 24.3 %collective-permute-start.4 = (bf16[512,768]{1,0:T(8,128)(2,1)S(1)}, bf16[512,768]{1,0:T(8,128)(2,1)}, u32[]{:S(2)}, u32[]{:S(2)}) collective-permute-start(bf16[512,768]{1,0:T(8,128)(2,1)S(1)} %collective-permute-done.3.refs_0_), channel_id=1, source_target_pairs={{0,1},{1,2},{2,3},{3,0},{4,5},{5,6},{6,7},{7,4},{8,9},{9,10},{10,1... | collective-permute-start | bytes 2359304 | tf_op jit(solution)/shard_map/ppermute | solution.py:364
  28.3 26.2 %collective-permute-start.6 = (bf16[512,768]{1,0:T(8,128)(2,1)S(1)}, bf16[512,768]{1,0:T(8,128)(2,1)S(1)}, u32[]{:S(2)}, u32[]{:S(2)}) collective-permute-start(bf16[512,768]{1,0:T(8,128)(2,1)S(1)} %collective-permute-done.3.refs_0_), channel_id=1, source_target_pairs={{0,4},{4,0},{8,12},{12,8},{1,5},{5,1},{9,13},{13,9},{2,6},{6,2},{1... | collective-permute-start | bytes 2359304 | tf_op jit(solution)/shard_map/ppermute | solution.py:363
  51.1 3.4 %collective-permute-start.8 = (bf16[512,768]{1,0:T(8,128)(2,1)S(1)}, bf16[512,768]{1,0:T(8,128)(2,1)S(1)}, u32[]{:S(2)}, u32[]{:S(2)}) collective-permute-start(bf16[512,768]{1,0:T(8,128)(2,1)S(1)} %collective-permute-done.7.refs_2_), channel_id=1, source_target_pairs={{0,4},{4,0},{8,12},{12,8},{1,5},{5,1},{9,13},{13,9},{2,6},{6,2},{1... | collective-permute-start | bytes 2359304 | tf_op jit(solution)/shard_map/ppermute | solution.py:363
  51.6 19.8 %collective-permute-start.12 = (bf16[512,768]{1,0:T(8,128)(2,1)}, bf16[512,768]{1,0:T(8,128)(2,1)S(1)}, u32[]{:S(2)}, u32[]{:S(2)}) collective-permute-start(bf16[512,768]{1,0:T(8,128)(2,1)} %collective-permute-done.4.refs_0_), channel_id=1, source_target_pairs={{0,8},{4,12},{8,0},{12,4},{1,9},{5,13},{9,1},{13,5},{2,10},{6,14},... | collective-permute-start | bytes 2359304 | tf_op jit(solution)/shard_map/ppermute | solution.py:363
  52.9 22.1 %collective-permute-start.11 = (bf16[512,768]{1,0:T(8,128)(2,1)}, bf16[512,768]{1,0:T(8,128)(2,1)}, u32[]{:S(2)}, u32[]{:S(2)}) collective-permute-start(bf16[512,768]{1,0:T(8,128)(2,1)} %collective-permute-done.4.refs_0_), channel_id=1, source_target_pairs={{0,4},{4,0},{8,12},{12,8},{1,5},{5,1},{9,13},{13,9},{2,6},{6,2},{1... | collective-permute-start | bytes 2359304 | tf_op jit(solution)/shard_map/ppermute | solution.py:363
  52.9 22.1 %collective-permute-start.5 = (bf16[512,768]{1,0:T(8,128)(2,1)}, bf16[512,768]{1,0:T(8,128)(2,1)}, u32[]{:S(2)}, u32[]{:S(2)}) collective-permute-start(bf16[512,768]{1,0:T(8,128)(2,1)} %collective-permute-done.4.refs_0_), channel_id=1, source_target_pairs={{0,1},{1,2},{2,3},{3,0},{4,5},{5,6},{6,7},{7,4},{8,9},{9,10},{10,1... | collective-permute-start | bytes 2359304 | tf_op jit(solution)/shard_map/ppermute | solution.py:364
  71.3 3.7 %collective-permute-start.13 = (bf16[512,768]{1,0:T(8,128)(2,1)S(1)}, bf16[512,768]{1,0:T(8,128)(2,1)S(1)}, u32[]{:S(2)}, u32[]{:S(2)}) collective-permute-start(bf16[512,768]{1,0:T(8,128)(2,1)S(1)} %collective-permute-done.12.refs_2_), channel_id=1, source_target_pairs={{0,4},{4,0},{8,12},{12,8},{1,5},{5,1},{9,13},{13,9},{2,6},{6,2},{1... | collective-permute-start | bytes 2359304 | tf_op jit(solution)/shard_map/ppermute | solution.py:363
  71.3 20.4 %copy-start.4 = (bf16[512,768]{1,0:T(8,128)(2,1)S(1)}, bf16[512,768]{1,0:T(8,128)(2,1)}, u32[]{:S(2)}) copy-start(bf16[512,768]{1,0:T(8,128)(2,1)} %get-tuple-element.73) | copy-start | bytes 2359300
  71.3 17.4 %collective-permute-start.16 = (bf16[512,768]{1,0:T(8,128)(2,1)}, bf16[512,768]{1,0:T(8,128)(2,1)}, u32[]{:S(2)}, u32[]{:S(2)}) collective-permute-start(bf16[512,768]{1,0:T(8,128)(2,1)} %get-tuple-element.71), channel_id=1, source_target_pairs={{0,4},{4,0},{8,12},{12,8},{1,5},{5,1},{9,13},{13,9},{2,6},{6,2},{1... | collective-permute-start | bytes 2359304 | tf_op jit(solution)/shard_map/ppermute | solution.py:363
  71.8 19.9 %collective-permute-start.10 = (bf16[512,768]{1,0:T(8,128)(2,1)S(1)}, bf16[512,768]{1,0:T(8,128)(2,1)S(1)}, u32[]{:S(2)}, u32[]{:S(2)}) collective-permute-start(bf16[512,768]{1,0:T(8,128)(2,1)S(1)} %collective-permute-done.1.refs_2_), channel_id=1, source_target_pairs={{0,3},{1,0},{2,1},{3,2},{4,7},{5,4},{6,5},{7,6},{8,11},{9,8},{10,9... | collective-permute-start | bytes 2359304 | tf_op jit(solution)/shard_map/ppermute | solution.py:365
  75.0 20.4 %collective-permute-start.9 = (bf16[512,768]{1,0:T(8,128)(2,1)}, bf16[512,768]{1,0:T(8,128)(2,1)}, u32[]{:S(2)}, u32[]{:S(2)}) collective-permute-start(bf16[512,768]{1,0:T(8,128)(2,1)} %collective-permute-done.5.refs_0_), channel_id=1, source_target_pairs={{0,4},{4,0},{8,12},{12,8},{1,5},{5,1},{9,13},{13,9},{2,6},{6,2},{1... | collective-permute-start | bytes 2359304 | tf_op jit(solution)/shard_map/ppermute | solution.py:363
  91.7 3.7 %collective-permute-start.14 = (bf16[512,768]{1,0:T(8,128)(2,1)S(1)}, bf16[512,768]{1,0:T(8,128)(2,1)S(1)}, u32[]{:S(2)}, u32[]{:S(2)}) collective-permute-start(bf16[512,768]{1,0:T(8,128)(2,1)S(1)} %collective-permute-done.10.refs_2_), channel_id=1, source_target_pairs={{0,4},{4,0},{8,12},{12,8},{1,5},{5,1},{9,13},{13,9},{2,6},{6,2},{1... | collective-permute-start | bytes 2359304 | tf_op jit(solution)/shard_map/ppermute | solution.py:363
  93.9 28.9 %collective-permute-start.17 = (bf16[512,768]{1,0:T(8,128)(2,1)}, bf16[512,768]{1,0:T(8,128)(2,1)S(1)}, u32[]{:S(2)}, u32[]{:S(2)}) collective-permute-start(bf16[512,768]{1,0:T(8,128)(2,1)} %add_convert_fusion), channel_id=1, source_target_pairs={{0,8},{4,12},{8,0},{12,4},{1,9},{5,13},{9,1},{13,5},{2,10},{6,14},... | collective-permute-start | bytes 2359304 | tf_op jit(solution)/shard_map/ppermute | solution.py:363
  95.1 27.7 %collective-permute-start.15 = (bf16[512,768]{1,0:T(8,128)(2,1)}, bf16[512,768]{1,0:T(8,128)(2,1)S(1)}, u32[]{:S(2)}, u32[]{:S(2)}) collective-permute-start(bf16[512,768]{1,0:T(8,128)(2,1)} %get-tuple-element.68), channel_id=1, source_target_pairs={{0,4},{4,0},{8,12},{12,8},{1,5},{5,1},{9,13},{13,9},{2,6},{6,2},{1... | collective-permute-start | bytes 2359304 | tf_op jit(solution)/shard_map/ppermute | solution.py:363
  95.4 27.5 %copy-start.1 = (bf16[512,768]{1,0:T(8,128)(2,1)S(1)}, bf16[512,768]{1,0:T(8,128)(2,1)}, u32[]{:S(2)}) copy-start(bf16[512,768]{1,0:T(8,128)(2,1)} %get-tuple-element.66.refs_0_) | copy-start | bytes 2359300
  95.4 27.5 %copy-start.2 = (s32[256]{0:T(256)S(1)}, s32[256]{0:T(256)}, u32[]{:S(2)}) copy-start(s32[256]{0:T(256)} %param.6) | copy-start | bytes 3076
  (1 other events, 0.9 us)

commit v5 on v4

--- a/solution.py
+++ b/solution.py
@@ -386,7 +386,7 @@
         [tp_rank * units, jnp.int32(units * n_tp), dp_rank, jnp.int32(pair * width), jnp.int32((pair ^ 2) * width)]
         + [jnp.int32(offset * width) for offset in offsets]
     ).astype(jnp.int32)
-    size, away_size = unit_block(units, 512), unit_block(units, 1536)
+    size, home_size, away_size = unit_block(units, 512), unit_block(units, 768), unit_block(units, 1536)
     flat = lambda blocks, kind: [(piece, kind) for pieces in blocks for piece in pieces]
     counts_of = lambda blocks: tuple(len(pieces) for pieces in blocks)
     kept_outs = [((rows, units), bf16, "cols")] * 2 + [((rows, own), bf16, "whole")] * 2
@@ -425,7 +425,7 @@
     opposite = opposite_of(chunk)
     coming = onward(chunk)
     *parts, hidden, back_pre, x_cols, c_cols = run_kernel(
-        functools.partial(home_kernel, n_near, counts_of(late), len(held), len(begun)), "home_group", meta, size, units,
+        functools.partial(home_kernel, n_near, counts_of(late), len(held), len(begun)), "home_group", meta, home_size, units,
         flat(near, "any") + flat(late, "vmem") + held + [(array, "cols") for array in begun],
         [((2 * rows, width if paired else model), bf16, "whole")] * len(offsets) + kept_outs,
         landing + half + [pltpu.VMEM((rows, model), f32)] * 2,

time: 125 us -> 124 us (level)
  transfers between devices with their start and end apart: 18 -> 18, of which waited for: 5 -> 5; matrix products, arithmetic and copies ran while one was open for 2% -> 2% of each run, Pallas kernels for 77% -> 76%
where the time goes in v5:
time: 124 us
  Pallas kernels  97.3 us (78%)
  starting transfers between devices  14.5 us (12%)
  waiting for transfers between devices  6.4 us (5%)
  local copies, waits for them, and re-layouts  2.48 us (2%)
  other arithmetic  2.2 us (2%)
    pallas_call x5, Pallas kernels, run_kernel(): pl.pallas_call(kernel, name=name, out_shape=[shape_of(*out) for out in ou...  94.5 us
    ppermute x14, starting transfers between devices, shards(): cross = lambda array, pairs: lax.ppermute(array, 'tp', pairs)  7.55 us
    ppermute x3, starting transfers between devices, shards(): lax.ppermute(array, 'dp', [(rank, (rank + 1) % n_dp) for rank in range(n_...  4.17 us
    ppermute x1, waiting for transfers between devices, shards(): lax.ppermute(array, 'dp', [(rank, (rank - 1) % n_dp) for rank in range(n_...  3 us
    ppermute x1, starting transfers between devices, shards(): lax.ppermute(array, 'dp', [(rank, (rank - 1) % n_dp) for rank in range(n_...  2.8 us
  transfers between devices with their start and end apart: 18, of which 5 were waited for; matrix products, arithmetic and copies ran while one was open for 2% of the time, Pallas kernels for 76%

profile of v5, /device:TPU:0, one launch (start us, length us, event | category | flops | bytes accessed | tf_op | source)
XLA Modules:
  0.0 123.7 jit_solution(7213065374020960621)
XLA Ops:
  0.6 1.5 %sort_rows.1.refs_0_ = bf16[512,768]{1,0:T(8,128)(2,1)S(1)} custom-call(s32[1,256]{1,0:T(1,128)} %bitcast.9, bf16[256,768]{1,0:T(8,128)(2,1)} %patches.1, bf16[256,768]{1,0:T(8,128)(2,1)} %cotangent.1), custom_call_target="tpu_custom_call" | custom-call | tf_op jit(solution)/shard_map/sort_rows/pallas_call | solution.py:403
  2.2 0.5 collective-permute-start
  2.7 2.6 %collective-permute-start.1 = (bf16[512,768]{1,0:T(8,128)(2,1)S(1)}, bf16[512,768]{1,0:T(8,128)(2,1)S(1)}, u32[]{:S(2)}, u32[]{:S(2)}) collective-permute-start(bf16[512,768]{1,0:T(8,128)(2,1)S(1)} %sort_rows.1.refs_0_), channel_id=1, source_target_pairs={{0,8},{4,12},{8,0},{12,4},{1,9},{5,13},{9,1},{13,5},{2,10},{6,14},... | collective-permute-start | bytes 2359304 | tf_op jit(solution)/shard_map/ppermute | solution.py:363
  5.3 1.6 %collective-permute-start.3 = (bf16[512,768]{1,0:T(8,128)(2,1)S(1)}, bf16[512,768]{1,0:T(8,128)(2,1)S(1)}, u32[]{:S(2)}, u32[]{:S(2)}) collective-permute-start(bf16[512,768]{1,0:T(8,128)(2,1)S(1)} %sort_rows.1.refs_0_), channel_id=1, source_target_pairs={{0,1},{1,2},{2,3},{3,0},{4,5},{5,6},{6,7},{7,4},{8,9},{9,10},{10,1... | collective-permute-start | bytes 2359304 | tf_op jit(solution)/shard_map/ppermute | solution.py:364
  6.9 0.7 stack.35.meta
  7.6 0.9 copy-done.3
  8.5 17.6 %open_group.1 = (bf16[6144,3072]{1,0:T(8,128)(2,1)S(1)}, f32[256,3072]{1,0:T(8,128)}, f32[256,3072]{1,0:T(8,128)}) custom-call(s32[9]{0:T(128)} %stack.35.meta, bf16[512,768]{1,0:T(8,128)(2,1)} %copy-done, bf16[512,768]{1,0:T(8,128)(2,1)} %copy-done.3, bf16[3072,3072]{1,0:T(8,128)(2,1)} %refs_2_.1, bf16[3072,3072]{1,0:T(8,128)(2,1)} %refs_3_.1), custom_call_target="tpu_custom_call" | custom-call | flops 301989888 | bytes 2850816 | tf_op jit(solution)/shard_map/open_group/pallas_call | solution.py:338
  26.1 0.6 collective-permute-done.3.refs_0_
  26.8 0.5 collective-permute-start.7
  27.3 1.0 collective-permute-start.4
  28.4 22.2 %home_group.1 = (bf16[512,768]{1,0:T(8,128)(2,1)}, bf16[512,768]{1,0:T(8,128)(2,1)}, bf16[512,768]{1,0:T(8,128)(2,1)}, bf16[512,768]{1,0:T(8,128)(2,1)}, bf16[25...) custom-call(s32[9]{0:T(128)} %stack.35.meta, ...), custom_call_target="tpu_custom_call" | custom-call | flops 905969664 | bytes 933888 | tf_op jit(solution)/shard_map/home_group/pallas_call | solution.py:338
  51.1 1.4 %collective-permute-start.12 = (bf16[512,768]{1,0:T(8,128)(2,1)}, bf16[512,768]{1,0:T(8,128)(2,1)S(1)}, u32[]{:S(2)}, u32[]{:S(2)}) collective-permute-start(bf16[512,768]{1,0:T(8,128)(2,1)} %collective-permute-done.4.refs_0_), channel_id=1, source_target_pairs={{0,8},{4,12},{8,0},{12,4},{1,9},{5,13},{9,1},{13,5},{2,10},{6,14},... | collective-permute-start | bytes 2359304 | tf_op jit(solution)/shard_map/ppermute | solution.py:363
  52.5 1.6 %collective-permute-start.5 = (bf16[512,768]{1,0:T(8,128)(2,1)}, bf16[512,768]{1,0:T(8,128)(2,1)}, u32[]{:S(2)}, u32[]{:S(2)}) collective-permute-start(bf16[512,768]{1,0:T(8,128)(2,1)} %collective-permute-done.4.refs_0_), channel_id=1, source_target_pairs={{0,1},{1,2},{2,3},{3,0},{4,5},{5,6},{6,7},{7,4},{8,9},{9,10},{10,1... | collective-permute-start | bytes 2359304 | tf_op jit(solution)/shard_map/ppermute | solution.py:364
  54.1 0.9 copy-done.6
  55.0 13.7 %away_group.2 = (bf16[256,3072]{1,0:T(8,128)(2,1)}, bf16[256,3072]{1,0:T(8,128)(2,1)}, bf16[256,768]{1,0:T(8,128)(2,1)}, bf16[256,768]{1,0:T(8,128)(2,1)}) custom-call(s32[9]{0:T(128)} %stack.35.meta, bf16[512,768]{1,0:T(8,128)(2,1)} %copy-done.5, bf16[512,768]{1,0:T(8,128)(2,1)} %copy-done.6, bf16[512,768]{1,0:T(8,128)(2,1)S(1)} %collective-permute-done.7.refs_2_, ...), custom_call_target="tpu_custom_call" | custom-call | flops 603979776 | bytes 344064 | tf_op jit(solution)/shard_map/away_group/pallas_call | solution.py:338
  68.7 2.1 %collective-permute-done.12.refs_2_ = bf16[512,768]{1,0:T(8,128)(2,1)S(1)} collective-permute-done((bf16[512,768]{1,0:T(8,128)(2,1)}, bf16[512,768]{1,0:T(8,128)(2,1)S(1)}, u32[]{:S(2)}, u32[]{:S(2)}) %collective-permute-start.12) | collective-permute-done | bytes 786464 | tf_op jit(solution)/shard_map/ppermute | solution.py:363
  70.8 0.5 collective-permute-start.16
  71.3 2.8 %collective-permute-start.10 = (bf16[512,768]{1,0:T(8,128)(2,1)S(1)}, bf16[512,768]{1,0:T(8,128)(2,1)S(1)}, u32[]{:S(2)}, u32[]{:S(2)}) collective-permute-start(bf16[512,768]{1,0:T(8,128)(2,1)S(1)} %collective-permute-done.1.refs_2_), channel_id=1, source_target_pairs={{0,3},{1,0},{2,1},{3,2},{4,7},{5,4},{6,5},{7,6},{8,11},{9,8},{10,9... | collective-permute-start | bytes 2359304 | tf_op jit(solution)/shard_map/ppermute | solution.py:365
  74.6 13.7 %away_group.3 = (bf16[256,3072]{1,0:T(8,128)(2,1)}, bf16[256,3072]{1,0:T(8,128)(2,1)}, bf16[256,768]{1,0:T(8,128)(2,1)}, bf16[256,768]{1,0:T(8,128)(2,1)}) custom-call(s32[9]{0:T(128)} %stack.35.meta, bf16[512,768]{1,0:T(8,128)(2,1)} %collective-permute-done.4.refs_0_, bf16[512,768]{1,0:T(8,128)(2,1)} %collective-permute-done.11.refs_1_, ...), custom_call_target="tpu_custom_call" | custom-call | flops 603979776 | bytes 344064 | tf_op jit(solution)/shard_map/away_group/pallas_call | solution.py:338
  88.3 3.0 %collective-permute-done.10.refs_2_ = bf16[512,768]{1,0:T(8,128)(2,1)S(1)} collective-permute-done((bf16[512,768]{1,0:T(8,128)(2,1)S(1)}, bf16[512,768]{1,0:T(8,128)(2,1)S(1)}, u32[]{:S(2)}, u32[]{:S(2)}) %collective-permute-start.10) | collective-permute-done | bytes 786464 | tf_op jit(solution)/shard_map/ppermute | solution.py:365
  91.3 2.2 %add_convert_fusion = bf16[512,768]{1,0:T(8,128)(2,1)} fusion(bf16[512,768]{1,0:T(8,128)(2,1)S(1)} %copy-done.4, bf16[512,768]{1,0:T(8,128)(2,1)} %collective-permute-done.16), kind=kLoop, calls=%fused_computation | loop fusion | flops 1572864 | bytes 2359296 | tf_op jit(solution)/shard_map/convert_element_type | solution.py:476
  93.5 1.2 collective-permute-start.17
  95.0 27.4 %last_group.1 = (f32[768,3072]{1,0:T(8,128)}, f32[3072,768]{1,0:T(8,128)}) custom-call(s32[9]{0:T(128)} %stack.35.meta, bf16[512,768]{1,0:T(8,128)(2,1)} %collective-permute-done.5.refs_0_, bf16[512,768]{1,0:T(8,128)(2,1)} %collective-permute-done.9.refs_1_, bf16[512,768]{1,0:T(8,128)(2,1)S(1)} %collective-permute-done.10.refs_2_, ...), custom_call_target="tpu_custom_call" | custom-call | flops 1207959552 | bytes 2015232 | tf_op jit(solution)/shard_map/last_group/pallas_call | solution.py:338
  122.4 1.3 %restore_rows.1 = (bf16[256,768]{1,0:T(8,128)(2,1)}, bf16[256,768]{1,0:T(8,128)(2,1)}) custom-call(s32[1,256]{1,0:T(1,128)S(1)} %bitcast.10, bf16[512,768]{1,0:T(8,128)(2,1)S(1)} %copy-done.1, bf16[512,768]{1,0:T(8,128)(2,1)S(1)} %collective-permute-done.15.refs_1_, bf16[512,768]{1,0:T(8,128)(2,1)S(1)} %collective-permute-done.17.refs_2_), custom_call_target="tpu_custom_call" | custom-call | tf_op jit(solution)/shard_map/restore_rows/pallas_call | solution.py:480
  (35 shorter events, 1.4 us)
Async XLA Ops:
  2.2 5.4 %copy-start = (bf16[512,768]{1,0:T(8,128)(2,1)}, bf16[512,768]{1,0:T(8,128)(2,1)S(1)}, u32[]{:S(2)}) copy-start(bf16[512,768]{1,0:T(8,128)(2,1)S(1)} %sort_rows.1.refs_0_) | copy-start | bytes 2359300
  2.2 5.4 %collective-permute-start = (bf16[512,768]{1,0:T(8,128)(2,1)S(1)}, bf16[512,768]{1,0:T(8,128)(2,1)S(1)}, u32[]{:S(2)}, u32[]{:S(2)}) collective-permute-start(bf16[512,768]{1,0:T(8,128)(2,1)S(1)} %sort_rows.1.refs_0_), channel_id=1, source_target_pairs={{0,4},{4,0},{8,12},{12,8},{1,5},{5,1},{9,13},{13,9},{2,6},{6,2},{1... | collective-permute-start | bytes 2359304 | tf_op jit(solution)/shard_map/ppermute | solution.py:363
  2.7 23.3 %collective-permute-start.1 = (bf16[512,768]{1,0:T(8,128)(2,1)S(1)}, bf16[512,768]{1,0:T(8,128)(2,1)S(1)}, u32[]{:S(2)}, u32[]{:S(2)}) collective-permute-start(bf16[512,768]{1,0:T(8,128)(2,1)S(1)} %sort_rows.1.refs_0_), channel_id=1, source_target_pairs={{0,8},{4,12},{8,0},{12,4},{1,9},{5,13},{9,1},{13,5},{2,10},{6,14},... | collective-permute-start | bytes 2359304 | tf_op jit(solution)/shard_map/ppermute | solution.py:363
  5.3 21.5 %collective-permute-start.3 = (bf16[512,768]{1,0:T(8,128)(2,1)S(1)}, bf16[512,768]{1,0:T(8,128)(2,1)S(1)}, u32[]{:S(2)}, u32[]{:S(2)}) collective-permute-start(bf16[512,768]{1,0:T(8,128)(2,1)S(1)} %sort_rows.1.refs_0_), channel_id=1, source_target_pairs={{0,1},{1,2},{2,3},{3,0},{4,5},{5,6},{6,7},{7,4},{8,9},{9,10},{10,1... | collective-permute-start | bytes 2359304 | tf_op jit(solution)/shard_map/ppermute | solution.py:364
  7.6 0.9 copy-start.3
  26.0 2.4 %collective-permute-start.2 = (bf16[512,768]{1,0:T(8,128)(2,1)S(1)}, bf16[512,768]{1,0:T(8,128)(2,1)S(1)}, u32[]{:S(2)}, u32[]{:S(2)}) collective-permute-start(bf16[512,768]{1,0:T(8,128)(2,1)S(1)} %collective-permute-done.1.refs_2_), channel_id=1, source_target_pairs={{0,4},{4,0},{8,12},{12,8},{1,5},{5,1},{9,13},{13,9},{2,6},{6,2},{1... | collective-permute-start | bytes 2359304 | tf_op jit(solution)/shard_map/ppermute | solution.py:363
  26.8 23.8 %copy-start.5 = (bf16[512,768]{1,0:T(8,128)(2,1)}, bf16[512,768]{1,0:T(8,128)(2,1)S(1)}, u32[]{:S(2)}) copy-start(bf16[512,768]{1,0:T(8,128)(2,1)S(1)} %collective-permute-done.3.refs_0_) | copy-start | bytes 2359300
  26.8 23.8 %collective-permute-start.7 = (bf16[512,768]{1,0:T(8,128)(2,1)S(1)}, bf16[512,768]{1,0:T(8,128)(2,1)S(1)}, u32[]{:S(2)}, u32[]{:S(2)}) collective-permute-start(bf16[512,768]{1,0:T(8,128)(2,1)S(1)} %collective-permute-done.3.refs_0_), channel_id=1, source_target_pairs={{0,8},{4,12},{8,0},{12,4},{1,9},{5,13},{9,1},{13,5},{2,10},{6,14},... | collective-permute-start | bytes 2359304 | tf_op jit(solution)/shard_map/ppermute | solution.py:363
  27.3 23.8 %collective-permute-start.4 = (bf16[512,768]{1,0:T(8,128)(2,1)S(1)}, bf16[512,768]{1,0:T(8,128)(2,1)}, u32[]{:S(2)}, u32[]{:S(2)}) collective-permute-start(bf16[512,768]{1,0:T(8,128)(2,1)S(1)} %collective-permute-done.3.refs_0_), channel_id=1, source_target_pairs={{0,1},{1,2},{2,3},{3,0},{4,5},{5,6},{6,7},{7,4},{8,9},{9,10},{10,1... | collective-permute-start | bytes 2359304 | tf_op jit(solution)/shard_map/ppermute | solution.py:364
  28.3 25.8 %collective-permute-start.6 = (bf16[512,768]{1,0:T(8,128)(2,1)S(1)}, bf16[512,768]{1,0:T(8,128)(2,1)S(1)}, u32[]{:S(2)}, u32[]{:S(2)}) collective-permute-start(bf16[512,768]{1,0:T(8,128)(2,1)S(1)} %collective-permute-done.3.refs_0_), channel_id=1, source_target_pairs={{0,4},{4,0},{8,12},{12,8},{1,5},{5,1},{9,13},{13,9},{2,6},{6,2},{1... | collective-permute-start | bytes 2359304 | tf_op jit(solution)/shard_map/ppermute | solution.py:363
  50.6 3.5 %collective-permute-start.8 = (bf16[512,768]{1,0:T(8,128)(2,1)S(1)}, bf16[512,768]{1,0:T(8,128)(2,1)S(1)}, u32[]{:S(2)}, u32[]{:S(2)}) collective-permute-start(bf16[512,768]{1,0:T(8,128)(2,1)S(1)} %collective-permute-done.7.refs_2_), channel_id=1, source_target_pairs={{0,4},{4,0},{8,12},{12,8},{1,5},{5,1},{9,13},{13,9},{2,6},{6,2},{1... | collective-permute-start | bytes 2359304 | tf_op jit(solution)/shard_map/ppermute | solution.py:363
  51.1 19.8 %collective-permute-start.12 = (bf16[512,768]{1,0:T(8,128)(2,1)}, bf16[512,768]{1,0:T(8,128)(2,1)S(1)}, u32[]{:S(2)}, u32[]{:S(2)}) collective-permute-start(bf16[512,768]{1,0:T(8,128)(2,1)} %collective-permute-done.4.refs_0_), channel_id=1, source_target_pairs={{0,8},{4,12},{8,0},{12,4},{1,9},{5,13},{9,1},{13,5},{2,10},{6,14},... | collective-permute-start | bytes 2359304 | tf_op jit(solution)/shard_map/ppermute | solution.py:363
  52.5 22.1 %collective-permute-start.11 = (bf16[512,768]{1,0:T(8,128)(2,1)}, bf16[512,768]{1,0:T(8,128)(2,1)}, u32[]{:S(2)}, u32[]{:S(2)}) collective-permute-start(bf16[512,768]{1,0:T(8,128)(2,1)} %collective-permute-done.4.refs_0_), channel_id=1, source_target_pairs={{0,4},{4,0},{8,12},{12,8},{1,5},{5,1},{9,13},{13,9},{2,6},{6,2},{1... | collective-permute-start | bytes 2359304 | tf_op jit(solution)/shard_map/ppermute | solution.py:363
  52.5 22.1 %collective-permute-start.5 = (bf16[512,768]{1,0:T(8,128)(2,1)}, bf16[512,768]{1,0:T(8,128)(2,1)}, u32[]{:S(2)}, u32[]{:S(2)}) collective-permute-start(bf16[512,768]{1,0:T(8,128)(2,1)} %collective-permute-done.4.refs_0_), channel_id=1, source_target_pairs={{0,1},{1,2},{2,3},{3,0},{4,5},{5,6},{6,7},{7,4},{8,9},{9,10},{10,1... | collective-permute-start | bytes 2359304 | tf_op jit(solution)/shard_map/ppermute | solution.py:364
  70.8 3.8 %collective-permute-start.13 = (bf16[512,768]{1,0:T(8,128)(2,1)S(1)}, bf16[512,768]{1,0:T(8,128)(2,1)S(1)}, u32[]{:S(2)}, u32[]{:S(2)}) collective-permute-start(bf16[512,768]{1,0:T(8,128)(2,1)S(1)} %collective-permute-done.12.refs_2_), channel_id=1, source_target_pairs={{0,4},{4,0},{8,12},{12,8},{1,5},{5,1},{9,13},{13,9},{2,6},{6,2},{1... | collective-permute-start | bytes 2359304 | tf_op jit(solution)/shard_map/ppermute | solution.py:363
  70.8 20.5 %copy-start.4 = (bf16[512,768]{1,0:T(8,128)(2,1)S(1)}, bf16[512,768]{1,0:T(8,128)(2,1)}, u32[]{:S(2)}) copy-start(bf16[512,768]{1,0:T(8,128)(2,1)} %get-tuple-element.73) | copy-start | bytes 2359300
  70.8 17.5 %collective-permute-start.16 = (bf16[512,768]{1,0:T(8,128)(2,1)}, bf16[512,768]{1,0:T(8,128)(2,1)}, u32[]{:S(2)}, u32[]{:S(2)}) collective-permute-start(bf16[512,768]{1,0:T(8,128)(2,1)} %get-tuple-element.71), channel_id=1, source_target_pairs={{0,4},{4,0},{8,12},{12,8},{1,5},{5,1},{9,13},{13,9},{2,6},{6,2},{1... | collective-permute-start | bytes 2359304 | tf_op jit(solution)/shard_map/ppermute | solution.py:363
  71.3 20.0 %collective-permute-start.10 = (bf16[512,768]{1,0:T(8,128)(2,1)S(1)}, bf16[512,768]{1,0:T(8,128)(2,1)S(1)}, u32[]{:S(2)}, u32[]{:S(2)}) collective-permute-start(bf16[512,768]{1,0:T(8,128)(2,1)S(1)} %collective-permute-done.1.refs_2_), channel_id=1, source_target_pairs={{0,3},{1,0},{2,1},{3,2},{4,7},{5,4},{6,5},{7,6},{8,11},{9,8},{10,9... | collective-permute-start | bytes 2359304 | tf_op jit(solution)/shard_map/ppermute | solution.py:365
  74.6 20.3 %collective-permute-start.9 = (bf16[512,768]{1,0:T(8,128)(2,1)}, bf16[512,768]{1,0:T(8,128)(2,1)}, u32[]{:S(2)}, u32[]{:S(2)}) collective-permute-start(bf16[512,768]{1,0:T(8,128)(2,1)} %collective-permute-done.5.refs_0_), channel_id=1, source_target_pairs={{0,4},{4,0},{8,12},{12,8},{1,5},{5,1},{9,13},{13,9},{2,6},{6,2},{1... | collective-permute-start | bytes 2359304 | tf_op jit(solution)/shard_map/ppermute | solution.py:363
  91.3 3.6 %collective-permute-start.14 = (bf16[512,768]{1,0:T(8,128)(2,1)S(1)}, bf16[512,768]{1,0:T(8,128)(2,1)S(1)}, u32[]{:S(2)}, u32[]{:S(2)}) collective-permute-start(bf16[512,768]{1,0:T(8,128)(2,1)S(1)} %collective-permute-done.10.refs_2_), channel_id=1, source_target_pairs={{0,4},{4,0},{8,12},{12,8},{1,5},{5,1},{9,13},{13,9},{2,6},{6,2},{1... | collective-permute-start | bytes 2359304 | tf_op jit(solution)/shard_map/ppermute | solution.py:363
  93.5 28.9 %collective-permute-start.17 = (bf16[512,768]{1,0:T(8,128)(2,1)}, bf16[512,768]{1,0:T(8,128)(2,1)S(1)}, u32[]{:S(2)}, u32[]{:S(2)}) collective-permute-start(bf16[512,768]{1,0:T(8,128)(2,1)} %add_convert_fusion), channel_id=1, source_target_pairs={{0,8},{4,12},{8,0},{12,4},{1,9},{5,13},{9,1},{13,5},{2,10},{6,14},... | collective-permute-start | bytes 2359304 | tf_op jit(solution)/shard_map/ppermute | solution.py:363
  94.7 27.7 %collective-permute-start.15 = (bf16[512,768]{1,0:T(8,128)(2,1)}, bf16[512,768]{1,0:T(8,128)(2,1)S(1)}, u32[]{:S(2)}, u32[]{:S(2)}) collective-permute-start(bf16[512,768]{1,0:T(8,128)(2,1)} %get-tuple-element.68), channel_id=1, source_target_pairs={{0,4},{4,0},{8,12},{12,8},{1,5},{5,1},{9,13},{13,9},{2,6},{6,2},{1... | collective-permute-start | bytes 2359304 | tf_op jit(solution)/shard_map/ppermute | solution.py:363
  94.9 27.5 %copy-start.1 = (bf16[512,768]{1,0:T(8,128)(2,1)S(1)}, bf16[512,768]{1,0:T(8,128)(2,1)}, u32[]{:S(2)}) copy-start(bf16[512,768]{1,0:T(8,128)(2,1)} %get-tuple-element.66.refs_0_) | copy-start | bytes 2359300
  95.0 27.5 %copy-start.2 = (s32[256]{0:T(256)S(1)}, s32[256]{0:T(256)}, u32[]{:S(2)}) copy-start(s32[256]{0:T(256)} %param.6) | copy-start | bytes 3076
  (1 other events, 0.9 us)
